TPU v7x, 256 devices: a whole 4x4x8 slice. The times are simulated.
256 devices in a mesh: dp: 8 (over z), expert: 32 (over y, x, core).
Axes of the slice: x: 4, y: 4, z: 8, core: 2. Of those that a mesh axis runs over, the one named last changes fastest.
Arguments:
- tokens: bfloat16 [32768, 7168], P(('dp', 'expert')), may hold values from -6 to 6
- cotangent: bfloat16 [32768, 7168], P(('dp', 'expert')), may hold values from -6 to 6
- routes: int32 [32768, 8], P(('dp', 'expert')), may hold values from 0 to 255, as said below
- route_weights: bfloat16 [32768, 8], P(('dp', 'expert')), may hold values from 0.049804688 to 1
- weights: bfloat16 [7168, 3, 4096], P(None, None, 'expert'), may hold values from -0.1875 to 0.1875
Outputs:
- d_tokens: bfloat16 [32768, 7168], P(('dp', 'expert'))
- d_route_weights: float32 [32768, 8], P(('dp', 'expert'))
- d_weights: bfloat16 [7168, 3, 4096], P('dp', None, 'expert')
Inputs may be any that keep to these rules, and one draw needn't show every extreme that they name: `routes`: each row names 8 different experts, at most one of them below 4. On the rows of one device each expert below 4 is named by 1 to 8 rows; in each data group one such expert is named by exactly 8 rows on every device of the group.
All inputs are finite; a program needn't handle non-finite values.
Results may differ from a plain program's by a relative error of at most 0.023.
Values may be sent and summed in bfloat16 or wider, within the bound.
No kernel may reach another device: no remote copies, remote signals or barrier semaphores. Data moves between devices by JAX's collectives and lax.ppermute only.
A program may use at most 128 MiB of HBM per device.

v0:
```python
import jax
import jax.numpy as jnp
from jax import lax
from jax.sharding import PartitionSpec as P

GROUP = 8
MOST = 8


def contract_rows(left, right):
    return lax.dot_general(
        left, right, (((0,), (0,)), ((), ())), preferred_element_type=jnp.float32
    )


def slot_table(routes, route_weights, n_win):
    window = routes < n_win
    expert_row = jnp.sum(jnp.where(window, routes, 0), axis=1)
    has_row = jnp.any(window, axis=1)
    weight_row = jnp.sum(jnp.where(window, route_weights.astype(jnp.float32), 0.0), axis=1)
    member = (expert_row[:, None] == jnp.arange(n_win)[None, :]) & has_row[:, None]
    slot_rank = jnp.cumsum(member.astype(jnp.int32), axis=0) - 1
    slot_row = jnp.sum(jnp.where(member, jnp.arange(n_win)[None, :] * MOST + slot_rank, 0), axis=1)
    select = (jnp.arange(n_win * MOST)[:, None] == slot_row[None, :]) & has_row[None, :]
    return (window, weight_row, select)


def repeat_group(array_in, n_win):
    shape_tail = array_in.shape[1:]
    spread = jnp.broadcast_to(array_in[:, None], (n_win, GROUP) + shape_tail)
    return spread.reshape((n_win * GROUP,) + shape_tail)


def local(tokens, cotangent, routes, route_weights, weights):
    width = tokens.shape[1]
    hidden = weights.shape[2]
    n_expert = lax.axis_size("expert")
    n_win = n_expert // GROUP
    window, weight_row, select = slot_table(routes, route_weights, n_win)
    select_b = select.astype(jnp.bfloat16)
    x_slots = (
        jnp.dot(select_b, tokens, preferred_element_type=jnp.float32)
        .astype(jnp.bfloat16)
        .reshape(n_win, MOST, width)
    )
    dy_slots = (
        jnp.dot(select_b, cotangent, preferred_element_type=jnp.float32)
        .astype(jnp.bfloat16)
        .reshape(n_win, MOST, width)
    )
    w_slots = (
        jnp.dot(select.astype(jnp.float32), weight_row, precision=lax.Precision.HIGHEST)
        .astype(jnp.bfloat16)
        .reshape(n_win, MOST)
    )
    got_x, got_dy, got_w = (
        lax.all_to_all(
            repeat_group(x_slots, n_win), "expert", split_axis=0, concat_axis=0, tiled=True
        ),
        lax.all_to_all(
            repeat_group(dy_slots, n_win), "expert", split_axis=0, concat_axis=0, tiled=True
        ),
        lax.all_to_all(
            repeat_group(w_slots, n_win), "expert", split_axis=0, concat_axis=0, tiled=True
        ),
    )
    slot_count = n_expert * MOST
    x_flat = got_x.reshape(slot_count, width)
    dy_flat = got_dy.reshape(slot_count, width)
    w_flat = got_w.reshape(slot_count).astype(jnp.float32)
    w_in = weights[:, :2, :].reshape(width, 2 * hidden)
    w_out = weights[:, 2, :]
    gate_up = jnp.dot(x_flat, w_in, preferred_element_type=jnp.float32).reshape(
        slot_count, 2, hidden
    )
    gate_val = gate_up[:, 0]
    up_val = gate_up[:, 1]
    sigmoid_g = jax.nn.sigmoid(gate_val)
    activation = gate_val * sigmoid_g
    hidden_act = (activation * up_val).astype(jnp.bfloat16)
    back_proj = jnp.dot(dy_flat, w_out, preferred_element_type=jnp.float32)
    shard_weight = jnp.sum(hidden_act.astype(jnp.float32) * back_proj, axis=1).astype(jnp.bfloat16)
    scaled = w_flat[:, None] * back_proj
    d_gate = (scaled * up_val * sigmoid_g * (1.0 + gate_val * (1.0 - sigmoid_g))).astype(
        jnp.bfloat16
    )
    d_up = (scaled * activation).astype(jnp.bfloat16)
    d_both = jnp.stack([d_gate, d_up], axis=1).reshape(slot_count, 2 * hidden)
    weighted = (w_flat[:, None] * hidden_act.astype(jnp.float32)).astype(jnp.bfloat16)
    shard_grad = lax.dot_general(
        d_both, w_in, (((1,), (1,)), ((), ())), preferred_element_type=jnp.float32
    ).astype(jnp.bfloat16)
    in_part = contract_rows(x_flat, d_both).reshape(
        width // lax.axis_size("dp") * lax.axis_size("dp"), 2, hidden
    )
    out_part = contract_rows(dy_flat, weighted).reshape(
        width // lax.axis_size("dp") * lax.axis_size("dp"), 1, hidden
    )
    d_weights = lax.psum_scatter(
        jnp.concatenate([in_part, out_part], axis=1), "dp", scatter_dimension=0, tiled=True
    ).astype(jnp.bfloat16)
    shard_grad = shard_grad.reshape(n_expert, MOST, width)
    shard_weight = shard_weight.reshape(n_expert, MOST)
    back_x, back_w = (
        lax.all_to_all(shard_grad, "expert", split_axis=0, concat_axis=0, tiled=True),
        lax.all_to_all(shard_weight, "expert", split_axis=0, concat_axis=0, tiled=True),
    )
    summed_x = jnp.sum(back_x.astype(jnp.float32).reshape(n_win, GROUP, MOST, width), axis=1)
    summed_w = jnp.sum(back_w.astype(jnp.float32).reshape(n_win, GROUP, MOST), axis=1)
    select_f = select.astype(jnp.float32)
    d_tokens = lax.dot_general(
        select_f,
        summed_x.reshape(n_win * MOST, width),
        (((0,), (0,)), ((), ())),
        precision=lax.Precision.HIGHEST,
        preferred_element_type=jnp.float32,
    ).astype(jnp.bfloat16)
    d_row = jnp.dot(summed_w.reshape(n_win * MOST), select_f, precision=lax.Precision.HIGHEST)
    d_route_weights = jnp.where(window, d_row[:, None], 0.0)
    return (d_tokens, d_route_weights, d_weights)


def solution(mesh):
    placed = (
        P(("dp", "expert"), None),
        P(("dp", "expert"), None),
        P(("dp", "expert"), None),
        P(("dp", "expert"), None),
        P(None, None, "expert"),
    )
    return jax.shard_map(
        local,
        mesh=mesh,
        in_specs=placed,
        out_specs=(P(("dp", "expert"), None), P(("dp", "expert"), None), P("dp", None, "expert")),
        check_vma=False,
    )
```

profile of v0, /device:TPU:1, one launch (start us, length us, event | category | flops | bytes accessed | tf_op | source)
XLA Modules:
  0.0 278.3 jit_solution(6394068604174336029)
XLA Ops:
  7.2 0.9 select_reduce_fusion.1
  8.0 0.7 select_reduce_fusion.2
  9.0 0.2 select_reduce_fusion
  9.7 0.7 copy.18
  10.4 8.6 %all-to-all-start = ((bf16[32,1,8]{2,1,0:T(2,128)(2,1)}), bf16[32,1,8]{2,1,0:T(2,128)(2,1)S(1)}, u32[]{:S(2)}, u32[]{:S(2)}) async-start(bf16[32,1,8]{2,1,0:T(2,128)(2,1)} %copy.18), calls=%async_computation | async-start | bytes 32768 | tf_op jit(solution)/shard_map/all_to_all | solution.py:63
  19.0 0.4 fusion.3
  19.4 6.5 %all-to-all-done = bf16[32,1,8]{2,1,0:T(2,128)(2,1)S(1)} async-done(((bf16[32,1,8]{2,1,0:T(2,128)(2,1)}), bf16[32,1,8]{2,1,0:T(2,128)(2,1)S(1)}, u32[]{:S(2)}, u32[]{:S(2)}) %all-to-all-start) | async-done | bytes 544 | tf_op jit(solution)/shard_map/all_to_all | solution.py:63
  25.9 2.3 broadcast_in_dim.61
  28.1 5.1 %all-to-all-start.2 = ((bf16[32,8,7168]{2,1,0:T(8,128)(2,1)}), bf16[32,8,7168]{2,1,0:T(8,128)(2,1)}, u32[]{:S(2)}, u32[]{:S(2)}) async-start(bf16[32,8,7168]{2,1,0:T(8,128)(2,1)} %bitcast.120), calls=%async_computation.2 | async-start | bytes 7340032 | tf_op jit(solution)/shard_map/all_to_all | solution.py:57
  33.2 1.9 fusion.2
  35.1 43.4 %all-to-all-done.2 = bf16[32,8,7168]{2,1,0:T(8,128)(2,1)} async-done(((bf16[32,8,7168]{2,1,0:T(8,128)(2,1)}), bf16[32,8,7168]{2,1,0:T(8,128)(2,1)}, u32[]{:S(2)}, u32[]{:S(2)}) %all-to-all-start.2) | async-done | bytes 3670048 | tf_op jit(solution)/shard_map/all_to_all | solution.py:57
  78.5 2.3 broadcast_in_dim.59
  80.8 7.2 %all-to-all-start.1 = ((bf16[32,8,7168]{2,1,0:T(8,128)(2,1)}), bf16[32,8,7168]{2,1,0:T(8,128)(2,1)}, u32[]{:S(2)}, u32[]{:S(2)}) async-start(bf16[32,8,7168]{2,1,0:T(8,128)(2,1)} %bitcast.119), calls=%async_computation.1 | async-start | bytes 7340032 | tf_op jit(solution)/shard_map/all_to_all | solution.py:60
  88.1 4.2 %slice.13 = bf16[7168,2,128]{2,0,1:T(8,128)(2,1)} slice(bf16[7168,3,128]{2,0,1:T(8,128)(2,1)} %param.9), slice={[0:7168], [0:2], [0:128]} | slice | bytes 7340032 | tf_op jit(solution)/shard_map/slice | solution.py:71
  92.3 6.0 %copy.19 = bf16[7168,2,128]{0,2,1:T(8,128)(2,1)} copy(bf16[7168,2,128]{2,0,1:T(8,128)(2,1)} %slice.13) | data formatting | bytes 7340032 | tf_op jit(solution)/shard_map/slice | solution.py:71
  98.4 4.3 %fusion.4 = f32[256,2,128]{0,2,1:T(8,128)S(1)} fusion(bf16[7168,2,128]{0,2,1:T(8,128)(2,1)} %copy.19, bf16[32,8,7168]{2,1,0:T(8,128)(2,1)} %all-to-all-done.2), kind=kOutput, calls=%fused_computation.11 | convolution fusion | flops 939524096 | bytes 7602176 | tf_op jit(solution)/shard_map/dot_general | solution.py:73
  102.7 30.5 %all-to-all-done.1 = bf16[32,8,7168]{2,1,0:T(8,128)(2,1)} async-done(((bf16[32,8,7168]{2,1,0:T(8,128)(2,1)}), bf16[32,8,7168]{2,1,0:T(8,128)(2,1)}, u32[]{:S(2)}, u32[]{:S(2)}) %all-to-all-start.1) | async-done | bytes 3670048 | tf_op jit(solution)/shard_map/all_to_all | solution.py:60
  133.3 4.0 %fusion.31 = (bf16[256,1,128]{0,2,1:T(8,128)(2,1)S(1)}, bf16[256,1,128]{0,2,1:T(8,128)(2,1)S(1)}, bf16[256]{0:T(256)(128)(2,1)S(1)}) fusion(f32[256,2,128]{0,2,1:T(8,128)S(1)} %fusion.4, f32[256]{0:T(256)S(1)} %reshape.110, bf16[7168,3,128]{2,0,1:T(8,128)(2,1)} %param.9, bf16[32,8,7168]{2,1,0:T(8,128)(2,1)} %all-to-all-done.1), kind=kOutput, calls=%fused_computation.51 | convolution fusion | flops 470384384 | bytes 5899776 | tf_op jit(solution)/shard_map/dot_general | solution.py:81
  137.3 3.3 %convolution_bitcast_fusion.1 = f32[7168,1,128]{2,0,1:T(8,128)S(1)} fusion(bf16[32,8,7168]{2,1,0:T(8,128)(2,1)} %all-to-all-done.1, f32[256,2,128]{0,2,1:T(8,128)} %copy-done.1, f32[256]{0:T(256)S(1)} %reshape.110), kind=kOutput, calls=%fused_computation.4 | convolution fusion | flops 470056960 | bytes 7603200 | tf_op jit(solution)/shard_map/dot_general | solution.py:11
  140.6 3.2 %fusion.6 = f32[7168,2,128]{2,0,1:T(8,128)S(1)} fusion(bf16[32,8,7168]{2,1,0:T(8,128)(2,1)} %all-to-all-done.2, bf16[256,1,128]{0,2,1:T(8,128)(2,1)S(1)} %get-tuple-element.6, bf16[256,1,128]{0,2,1:T(8,128)(2,1)S(1)} %get-tuple-element.5), kind=kOutput, calls=%fused_computation.13 | convolution fusion | flops 939786240 | bytes 11141120 | tf_op jit(solution)/shard_map/dot_general | solution.py:11
  143.8 4.9 %pad_maximum_fusion = f32[7168,3,128]{2,0,1:T(8,128)} fusion(f32[7168,1,128]{2,0,1:T(8,128)S(1)} %convolution_bitcast_fusion.1, f32[7168,2,128]{2,0,1:T(8,128)S(1)} %fusion.6), kind=kLoop, calls=%fused_computation | loop fusion | flops 2752512 | bytes 22020096 | tf_op jit(solution)/shard_map/concatenate | solution.py:100
  148.7 0.7 convert_element_type.112
  149.4 6.3 %all-to-all-start.4 = ((bf16[32,1,8]{2,1,0:T(2,128)(2,1)}), bf16[32,1,8]{2,1,0:T(2,128)(2,1)S(1)}, u32[]{:S(2)}, u32[]{:S(2)}) async-start(bf16[32,1,8]{2,1,0:T(2,128)(2,1)} %convert_element_type.112), calls=%async_computation.4 | async-start | bytes 32768 | tf_op jit(solution)/shard_map/all_to_all | solution.py:106
  155.7 5.0 %fusion.1 = bf16[32,8,7168]{2,1,0:T(8,128)(2,1)} fusion(bf16[256,1,128]{0,2,1:T(8,128)(2,1)S(1)} %get-tuple-element.6, bf16[256,1,128]{0,2,1:T(8,128)(2,1)S(1)} %get-tuple-element.5, bf16[7168,3,128]{2,0,1:T(8,128)(2,1)} %param.9), kind=kOutput, calls=%fused_computation.3 | convolution fusion | flops 941424640 | bytes 7471104 | tf_op jit(solution)/shard_map/dot_general | solution.py:90
  160.7 2.0 all-to-all-done.4
  162.7 5.6 %all-to-all-start.3 = ((bf16[32,8,7168]{2,1,0:T(8,128)(2,1)}), bf16[32,8,7168]{2,1,0:T(8,128)(2,1)}, u32[]{:S(2)}, u32[]{:S(2)}) async-start(bf16[32,8,7168]{2,1,0:T(8,128)(2,1)} %fusion.1), calls=%async_computation.3 | async-start | bytes 7340032 | tf_op jit(solution)/shard_map/all_to_all | solution.py:105
  168.6 0.6 broadcast_select_fusion
  169.2 43.8 %all-to-all-done.3 = bf16[32,8,7168]{2,1,0:T(8,128)(2,1)} async-done(((bf16[32,8,7168]{2,1,0:T(8,128)(2,1)}), bf16[32,8,7168]{2,1,0:T(8,128)(2,1)}, u32[]{:S(2)}, u32[]{:S(2)}) %all-to-all-start.3) | async-done | bytes 3670048 | tf_op jit(solution)/shard_map/all_to_all | solution.py:105
  212.9 2.8 %convert_reduce_fusion = f32[4,8,7168]{2,1,0:T(8,128)S(1)} fusion(bf16[32,8,7168]{2,1,0:T(8,128)(2,1)} %all-to-all-done.3), kind=kLoop, calls=%fused_computation.10 | loop fusion | flops 3440640 | bytes 4587520 | tf_op jit(solution)/shard_map/reduce_sum | solution.py:108
  215.7 2.9 %convolution_convert_fusion = bf16[128,7168]{1,0:T(8,128)(2,1)} fusion(f32[4,8,7168]{2,1,0:T(8,128)S(1)} %convert_reduce_fusion, s32[128]{0:T(128)S(1)} %select_reduce_fusion, pred[128]{0:T(512)(128)(4,1)S(1)} %reduce_or.9), kind=kOutput, calls=%fused_computation.5 | convolution fusion | flops 353247232 | bytes 2753152 | tf_op jit(solution)/shard_map/dot_general | solution.py:111
  218.6 50.6 %reduce-scatter.2.cloned.1.call-done = f32[896,3,128]{2,0,1:T(8,128)} async-done(((f32[7168,3,128]{2,0,1:T(8,128)}), f32[896,3,128]{2,0,1:T(8,128)}) %reduce-scatter.2.cloned.1.call-update) | async-done | bytes 1376272 | tf_op jit(solution)/shard_map/reduce_scatter | solution.py:99
  269.2 2.3 convert_element_type.109
  (21 shorter events, 1.2 us)
Async XLA Ops:
  7.2 11.9 %copy-start = (bf16[128,7168]{1,0:T(8,128)(2,1)S(1)}, bf16[128,7168]{1,0:T(8,128)(2,1)}, u32[]{:S(2)}) copy-start(bf16[128,7168]{1,0:T(8,128)(2,1)} %param.5) | copy-start | bytes 5505028
  10.4 15.5 %all-to-all-start = ((bf16[32,1,8]{2,1,0:T(2,128)(2,1)}), bf16[32,1,8]{2,1,0:T(2,128)(2,1)S(1)}, u32[]{:S(2)}, u32[]{:S(2)}) async-start(bf16[32,1,8]{2,1,0:T(2,128)(2,1)} %copy.18), calls=%async_computation | async-start | bytes 32768 | tf_op jit(solution)/shard_map/all_to_all | solution.py:63
  28.1 50.3 %all-to-all-start.2 = ((bf16[32,8,7168]{2,1,0:T(8,128)(2,1)}), bf16[32,8,7168]{2,1,0:T(8,128)(2,1)}, u32[]{:S(2)}, u32[]{:S(2)}) async-start(bf16[32,8,7168]{2,1,0:T(8,128)(2,1)} %bitcast.120), calls=%async_computation.2 | async-start | bytes 7340032 | tf_op jit(solution)/shard_map/all_to_all | solution.py:57
  80.8 52.5 %all-to-all-start.1 = ((bf16[32,8,7168]{2,1,0:T(8,128)(2,1)}), bf16[32,8,7168]{2,1,0:T(8,128)(2,1)}, u32[]{:S(2)}, u32[]{:S(2)}) async-start(bf16[32,8,7168]{2,1,0:T(8,128)(2,1)} %bitcast.119), calls=%async_computation.1 | async-start | bytes 7340032 | tf_op jit(solution)/shard_map/all_to_all | solution.py:60
  88.0 181.1 %reduce-scatter.2.cloned.1.call-start = ((), (), s32[]{:S(2)}) async-start(), calls=%async_computation.6 | async-start | bytes 12386304 | tf_op jit(solution)/shard_map/reduce_scatter | solution.py:99
  102.7 30.6 %copy-start.1 = (f32[256,2,128]{0,2,1:T(8,128)}, f32[256,2,128]{0,2,1:T(8,128)S(1)}, u32[]{:S(2)}) copy-start(f32[256,2,128]{0,2,1:T(8,128)S(1)} %fusion.4) | copy-start | bytes 786436
  149.4 13.3 %all-to-all-start.4 = ((bf16[32,1,8]{2,1,0:T(2,128)(2,1)}), bf16[32,1,8]{2,1,0:T(2,128)(2,1)S(1)}, u32[]{:S(2)}, u32[]{:S(2)}) async-start(bf16[32,1,8]{2,1,0:T(2,128)(2,1)} %convert_element_type.112), calls=%async_computation.4 | async-start | bytes 32768 | tf_op jit(solution)/shard_map/all_to_all | solution.py:106
  162.7 50.2 %all-to-all-start.3 = ((bf16[32,8,7168]{2,1,0:T(8,128)(2,1)}), bf16[32,8,7168]{2,1,0:T(8,128)(2,1)}, u32[]{:S(2)}, u32[]{:S(2)}) async-start(bf16[32,8,7168]{2,1,0:T(8,128)(2,1)} %fusion.1), calls=%async_computation.3 | async-start | bytes 7340032 | tf_op jit(solution)/shard_map/all_to_all | solution.py:105
Sparse Core Ops, SparseCore 0:
  148.8 120.3 reduce-scatter.1
where the time goes:
time: 279 us; the launch traced here: 278 us
  waiting for transfers between devices  177 us (63%)
  starting transfers between devices  32.8 us (12%)
  matrix products  25.2 us (9%)
  local copies, waits for them, and re-layouts  16.7 us (6%)
  between operations  14.2 us (5%)
  other arithmetic  12.7 us (5%)
    reduce_scatter x1, waiting for transfers between devices, local(): lax.psum_scatter(jnp.concatenate([in_part, out_part], axis=1), 'dp', scat...  50.6 us
    all_to_all x1, waiting for transfers between devices, local(): lax.all_to_all(shard_grad, 'expert', split_axis=0, concat_axis=0, tiled=T...  43.8 us
    all_to_all x1, waiting for transfers between devices, local(): lax.all_to_all(repeat_group(x_slots, n_win), 'expert', split_axis=0, conc...  43.4 us
    all_to_all x1, waiting for transfers between devices, local(): lax.all_to_all(repeat_group(dy_slots, n_win), 'expert', split_axis=0, con...  30.5 us
    slice x2, local copies, waits for them, and re-layouts, local(): w_in = weights[:, :2, :].reshape(width, 2 * hidden)  10.2 us
    all_to_all x1, starting transfers between devices, local(): lax.all_to_all(repeat_group(w_slots, n_win), 'expert', split_axis=0, conc...  8.59 us
    all_to_all x1, starting transfers between devices, local(): lax.all_to_all(repeat_group(dy_slots, n_win), 'expert', split_axis=0, con...  7.25 us
    dot_general x2, matrix products, contract_rows(): lax.dot_general(left, right, (((0,), (0,)), ((), ())), preferred_element_...  6.51 us
  transfers between devices with their start and end apart: 6, of which 6 were waited for; matrix products, arithmetic and copies ran while one was open for 10% of the time, Pallas kernels for 0%

commit v1 on v0

v1 whole, which is shorter than its diff:
```python
import functools
import jax
import jax.numpy as jnp
from jax import lax
from jax.experimental import pallas as pl
from jax.experimental.pallas import tpu as pltpu
from jax.sharding import PartitionSpec as P

GROUP = 8
MOST = 8
N_WIN = 4
NX = 4
NC = 2
SLOTS = N_WIN * MOST
LANES = 128
CHUNK = 1024
F32 = jnp.float32
BF16 = jnp.bfloat16
VMEM = pltpu.MemorySpace.VMEM
SMEM = pltpu.MemorySpace.SMEM


def shifted(dy, dx, dc):
    pairs = []
    for y in range(N_WIN):
        for x in range(NX):
            for c in range(NC):
                to = (((y + dy) % N_WIN) * NX + (x + dx) % NX) * NC + (c + dc) % NC
                pairs.append(((y * NX + x) * NC + c, to))
    return pairs


def send(array, dy=0, dx=0, dc=0):
    return lax.ppermute(array, "expert", shifted(dy, dx, dc))


def call(body, outs, operands, scalars=0, limit=40):
    specs = [pl.BlockSpec(memory_space=SMEM)] * scalars
    specs += [pl.BlockSpec(memory_space=VMEM)] * (len(operands) - scalars)
    return pl.pallas_call(
        body,
        out_shape=[jax.ShapeDtypeStruct(s, d) for s, d in outs],
        in_specs=specs,
        out_specs=[pl.BlockSpec(memory_space=VMEM)] * len(outs),
        compiler_params=pltpu.CompilerParams(vmem_limit_bytes=limit * 1024 * 1024),
    )(*operands)


def slots_of(y_ref, routes_ref):
    routes = routes_ref[...]
    rows = routes.shape[1]
    window = routes < N_WIN
    expert = jnp.sum(jnp.where(window, routes, 0), axis=0, keepdims=True)
    has = jnp.sum(jnp.where(window, 1, 0), axis=0, keepdims=True) > 0
    near = (expert + N_WIN - y_ref[0]) & (N_WIN - 1)
    member = (lax.broadcasted_iota(jnp.int32, (MOST, rows), 0) == near) & has
    upto = lax.broadcasted_iota(jnp.int32, (rows, rows), 0) <= lax.broadcasted_iota(
        jnp.int32, (rows, rows), 1
    )
    ones = jnp.where(member, 1.0, 0.0)
    rank = jnp.dot(
        ones.astype(BF16), jnp.where(upto, 1.0, 0.0).astype(BF16), preferred_element_type=F32
    )
    base = lax.broadcasted_iota(jnp.int32, (MOST, rows), 0).astype(F32) * MOST
    slot = jnp.sum(ones * (base + rank), axis=0, keepdims=True) - 1.0
    slot = jnp.where(has, slot, -1.0).astype(jnp.int32)
    return window, lax.broadcasted_iota(jnp.int32, (SLOTS, rows), 0) == slot


def pick_tokens(y_ref, routes_ref, rw_ref, tok_ref, *outs):
    window, select = slots_of(y_ref, routes_ref)
    weight = jnp.sum(jnp.where(window, rw_ref[...].astype(F32), 0.0), axis=0, keepdims=True)
    chosen = jnp.sum(jnp.where(select, weight, 0.0), axis=1, keepdims=True)
    rows = jnp.dot(
        jnp.where(select, 1.0, 0.0).astype(BF16), tok_ref[...], preferred_element_type=F32
    )
    width = rows.shape[1]
    lanes = jnp.broadcast_to(chosen, (SLOTS, LANES))
    for k, out in enumerate(outs):
        out[:, :width] = rows[k * MOST : (k + 1) * MOST].astype(BF16)
        out[:, width:] = lanes[k * MOST : (k + 1) * MOST].astype(BF16)


def pick_rows(y_ref, routes_ref, tok_ref, *outs):
    _, select = slots_of(y_ref, routes_ref)
    rows = jnp.dot(
        jnp.where(select, 1.0, 0.0).astype(BF16), tok_ref[...], preferred_element_type=F32
    )
    for k, out in enumerate(outs):
        out[...] = rows[k * MOST : (k + 1) * MOST].astype(BF16)


def rows_of(blocks, cols):
    return jnp.concatenate([b[:, cols] for b in blocks], axis=0)


def gate_up(n_blocks, *refs):
    blocks, w_ref, out = refs[:n_blocks], refs[n_blocks], refs[n_blocks + 1]
    width = w_ref.shape[1]
    total = None
    for at in range(0, width, CHUNK):
        cols = slice(at, at + CHUNK)
        both = jnp.concatenate([w_ref[0, cols, :], w_ref[1, cols, :]], axis=1)
        part = jnp.dot(rows_of(blocks, cols), both, preferred_element_type=F32)
        total = part if total is None else total + part
    out[...] = total


def backward(n_blocks, *refs):
    xs, dys = refs[:n_blocks], refs[n_blocks : 2 * n_blocks]
    gu_ref, w_ref, g_ref, sw_ref, dw_ref = refs[2 * n_blocks :]
    width, hidden = w_ref.shape[1:]
    back = None
    for at in range(0, width, CHUNK):
        cols = slice(at, at + CHUNK)
        part = jnp.dot(rows_of(dys, cols), w_ref[2, cols, :], preferred_element_type=F32)
        back = part if back is None else back + part
    gate, up = gu_ref[:, :hidden], gu_ref[:, hidden:]
    w = rows_of(xs, slice(width, width + LANES)).astype(F32)
    sig = jax.nn.sigmoid(gate)
    act = gate * sig
    hid = (act * up).astype(BF16).astype(F32)
    sw = jnp.sum(hid * back, axis=1, keepdims=True)
    sw_ref[...] = jnp.broadcast_to(sw, (sw.shape[0], LANES)).astype(BF16)
    scaled = w * back
    d_gate = (scaled * up * sig * (1.0 + gate * (1.0 - sig))).astype(BF16)
    d_up = (scaled * act).astype(BF16)
    weighted = (w * hid).astype(BF16)
    d_both = jnp.concatenate([d_gate, d_up], axis=1)
    g_ref[...] = d_both
    down = (((0,), (0,)), ((), ()))
    for at in range(0, width, CHUNK):
        cols = slice(at, at + CHUNK)
        d_in = lax.dot_general(rows_of(xs, cols), d_both, down, preferred_element_type=F32)
        d_out = lax.dot_general(rows_of(dys, cols), weighted, down, preferred_element_type=F32)
        dw_ref[0, cols, :] = d_in[:, :hidden].astype(BF16)
        dw_ref[1, cols, :] = d_in[:, hidden:].astype(BF16)
        dw_ref[2, cols, :] = d_out.astype(BF16)


def shard_grads(g_ref, sw_ref, w_ref, *outs):
    width = w_ref.shape[1]
    across = (((1,), (1,)), ((), ()))
    d_both = g_ref[...]
    for at in range(0, width, CHUNK):
        cols = slice(at, at + CHUNK)
        both = jnp.concatenate([w_ref[0, cols, :], w_ref[1, cols, :]], axis=1)
        grad = lax.dot_general(d_both, both, across, preferred_element_type=F32).astype(BF16)
        row = 0
        for out in outs:
            out[:, cols] = grad[row : row + out.shape[0]]
            row += out.shape[0]
    row = 0
    for out in outs:
        out[:, width:] = sw_ref[row : row + out.shape[0], :]
        row += out.shape[0]


def add_pairs(mine_ref, got_ref, *outs):
    row = 0
    for out in outs:
        rows = slice(row, row + out.shape[0])
        out[...] = (mine_ref[rows, :].astype(F32) + got_ref[rows, :].astype(F32)).astype(BF16)
        row += out.shape[0]


def add_all(a_ref, b_ref, c_ref, d_ref, *outs):
    for k, out in enumerate(outs):
        rows = slice(k * MOST, (k + 1) * MOST)
        total = (a_ref[rows, :].astype(F32) + b_ref[rows, :].astype(F32)) + (
            c_ref[rows, :].astype(F32) + d_ref[rows, :].astype(F32)
        )
        out[...] = total.astype(BF16)


def put_back(y_ref, routes_ref, b0, b1, b2, b3, dtok_ref, drw_ref):
    window, select = slots_of(y_ref, routes_ref)
    width = dtok_ref.shape[1]
    grads = jnp.concatenate([b[...].astype(F32) for b in (b0, b1, b2, b3)], axis=0)
    one = jnp.where(select, 1.0, 0.0)
    dtok_ref[...] = lax.dot_general(
        one.astype(BF16),
        grads[:, :width].astype(BF16),
        (((0,), (0,)), ((), ())),
        preferred_element_type=F32,
    ).astype(BF16)
    row = jnp.sum(one * grads[:, width : width + 1], axis=0, keepdims=True)
    drw_ref[...] = jnp.where(window, row, 0.0)


def local(tokens, cotangent, routes, route_weights, weights):
    width = tokens.shape[1]
    wide = width + LANES
    hidden = weights.shape[2]
    y = (lax.axis_index("expert") // (NX * NC)).astype(jnp.int32).reshape(1)
    routes_t = routes.T
    w_t = jnp.transpose(weights, (1, 0, 2))
    total = SLOTS * NX * NC

    x_out = call(pick_tokens, [((MOST, wide), BF16)] * N_WIN, [y, routes_t, route_weights.T, tokens], 1)
    x_mine = jnp.concatenate([x_out[0]] + [send(x_out[k], dy=k) for k in range(1, N_WIN)], axis=0)
    dy_out = call(pick_rows, [((MOST, width), BF16)] * N_WIN, [y, routes_t, cotangent], 1)
    dy_mine = jnp.concatenate([dy_out[0]] + [send(dy_out[k], dy=k) for k in range(1, N_WIN)], axis=0)

    def spread(mine):
        half = SLOTS // 2
        left, right = send(mine, dx=1), send(mine, dx=-1)
        far_a, far_b = send(left[:half], dx=1), send(right[half:], dx=-1)
        own = [mine, left, right, far_a, far_b]
        return own + [send(b, dc=1) for b in own]

    xs = spread(x_mine)
    gu = call(
        functools.partial(gate_up, len(xs)), [((total, 2 * hidden), F32)], [*xs, w_t]
    )[0]
    dys = spread(dy_mine)
    g, sw, dw = call(
        functools.partial(backward, len(xs)),
        [((total, 2 * hidden), BF16), ((total, LANES), BF16), ((3, width, hidden), BF16)],
        [*xs, *dys, gu, w_t],
    )
    d_weights = jnp.transpose(
        lax.psum_scatter(dw, "dp", scatter_dimension=1, tiled=True), (1, 0, 2)
    )
    mine, other = call(
        shard_grads, [((total // 2, wide), BF16)] * 2, [g, sw, w_t]
    )
    got = send(other, dc=1)
    parts = call(add_pairs, [((SLOTS, wide), BF16)] * NX, [mine, got])
    keep, to_left, to_right, to_far = parts
    back = call(
        add_all,
        [((MOST, wide), BF16)] * N_WIN,
        [keep, send(to_left, dx=-1), send(to_right, dx=1), send(to_far, dx=2)],
    )
    home = [back[0]] + [send(back[k], dy=-k) for k in range(1, N_WIN)]
    d_tokens, d_rw = call(
        put_back,
        [(tokens.shape, BF16), (routes_t.shape, F32)],
        [y, routes_t, *home],
        1,
    )
    return d_tokens, d_rw.T, d_weights


def solution(mesh):
    placed = (
        P(("dp", "expert"), None),
        P(("dp", "expert"), None),
        P(("dp", "expert"), None),
        P(("dp", "expert"), None),
        P(None, None, "expert"),
    )
    return jax.shard_map(
        local,
        mesh=mesh,
        in_specs=placed,
        out_specs=(P(("dp", "expert"), None), P(("dp", "expert"), None), P("dp", None, "expert")),
        check_vma=False,
    )
```

time: 279 us -> 155 us (0.56)
  waiting for transfers between devices: 177 us -> 67.7 us
  matrix products: 25.2 us -> 0 us
  starting transfers between devices: 32.8 us -> 51.7 us
  other arithmetic: 12.7 us -> 0 us
  Pallas kernels: 0 us -> 11.9 us
  local copies, waits for them, and re-layouts: 16.7 us -> 8.81 us
    all_to_all x5 -> x0, waiting for transfers between devices: 126 us -> none  [the longest x1 43.8 us: local(): lax.all_to_all(shard_grad, 'expert', split_axis=0, concat_axis=0, tiled=T...]
    ppermute x0 -> x31, starting transfers between devices: none -> 51.7 us  [send(): return lax.ppermute(array, 'expert', shifted(dy, dx, dc))]
    ppermute x0 -> x31, waiting for transfers between devices: none -> 41.8 us  [send(): return lax.ppermute(array, 'expert', shifted(dy, dx, dc))]
    all_to_all x5 -> x0, starting transfers between devices: 32.8 us -> none  [the longest x1 8.59 us: local(): lax.all_to_all(repeat_group(w_slots, n_win), 'expert', split_axis=0, conc...]
    dot_general x10 -> x0, matrix products: 25.2 us -> none  [the longest x2 6.51 us: contract_rows(): lax.dot_general(left, right, (((0,), (0,)), ((), ())), preferred_element_...]
    reduce_scatter x1, waiting for transfers between devices: 50.6 us -> 25.8 us  [local(): lax.psum_scatter(dw, 'dp', scatter_dimension=1, tiled=True)]
    pallas_call x0 -> x8, Pallas kernels: none -> 11.9 us  [call(): pl.pallas_call(body, out_shape=[jax.ShapeDtypeStruct(s, d) for s, d in ou...]
    slice x2 -> x4, local copies, waits for them, and re-layouts: 10.2 us -> 0.07 us  [spread(): far_a, far_b = (send(left[:half], dx=1), send(right[half:], dx=-1))]
  transfers between devices with their start and end apart: 6 -> 32, of which waited for: 6 -> 16; matrix products, arithmetic and copies ran while one was open for 10% -> 0% of each run, Pallas kernels for 0% -> 4%
where the time goes in v1:
time: 155 us; the launch traced here: 154 us
  waiting for transfers between devices  67.7 us (44%)
  starting transfers between devices  51.7 us (33%)
  between operations  14.2 us (9%)
  Pallas kernels  11.9 us (8%)
  local copies, waits for them, and re-layouts  8.81 us (6%)
    ppermute x31, starting transfers between devices, send(): return lax.ppermute(array, 'expert', shifted(dy, dx, dc))  51.7 us
    ppermute x31, waiting for transfers between devices, send(): return lax.ppermute(array, 'expert', shifted(dy, dx, dc))  41.8 us
    reduce_scatter x1, waiting for transfers between devices, local(): lax.psum_scatter(dw, 'dp', scatter_dimension=1, tiled=True)  25.8 us
    pallas_call x8, Pallas kernels, call(): pl.pallas_call(body, out_shape=[jax.ShapeDtypeStruct(s, d) for s, d in ou...  11.9 us
    unnamed x24, local copies, waits for them, and re-layouts  8.72 us
  transfers between devices with their start and end apart: 32, of which 16 were waited for; matrix products, arithmetic and copies ran while one was open for 0% of the time, Pallas kernels for 4%

profile of v1, /device:TPU:1, one launch (start us, length us, event | category | flops | bytes accessed | tf_op | source)
XLA Modules:
  0.0 154.3 jit_solution(14046443176957463542)
XLA Ops:
  7.2 1.6 %copy-done.4 = bf16[128,7168]{1,0:T(8,128)(2,1)S(1)} copy-done((bf16[128,7168]{1,0:T(8,128)(2,1)S(1)}, bf16[128,7168]{1,0:T(8,128)(2,1)}, u32[]{:S(2)}) %copy-start.4) | copy-done | bytes 1835032
  10.1 2.2 %collective-permute-start.12 = (bf16[8,7168]{1,0:T(8,128)(2,1)S(1)}, bf16[8,7168]{1,0:T(8,128)(2,1)S(1)}, u32[]{:S(2)}, u32[]{:S(2)}) collective-permute-start(bf16[8,7168]{1,0:T(8,128)(2,1)S(1)} %get-tuple-element.31), channel_id=1, source_target_pairs={{0,8},{1,9},{2,10},{3,11},{4,12},{5,13},{6,14},{7,15},{8,16},{9,17... | collective-permute-start | bytes 344072 | tf_op jit(solution)/shard_map/ppermute | solution.py:34
  12.3 2.6 %collective-permute-start.13 = (bf16[8,7168]{1,0:T(8,128)(2,1)S(1)}, bf16[8,7168]{1,0:T(8,128)(2,1)S(1)}, u32[]{:S(2)}, u32[]{:S(2)}) collective-permute-start(bf16[8,7168]{1,0:T(8,128)(2,1)S(1)} %get-tuple-element.32), channel_id=1, source_target_pairs={{0,16},{1,17},{2,18},{3,19},{4,20},{5,21},{6,22},{7,23},{8,24},{9,... | collective-permute-start | bytes 344072 | tf_op jit(solution)/shard_map/ppermute | solution.py:34
  19.1 1.8 %collective-permute-start.2 = (bf16[8,7296]{1,0:T(8,128)(2,1)S(1)}, bf16[8,7296]{1,0:T(8,128)(2,1)S(1)}, u32[]{:S(2)}, u32[]{:S(2)}) collective-permute-start(bf16[8,7296]{1,0:T(8,128)(2,1)S(1)} %get-tuple-element.29), channel_id=1, source_target_pairs={{0,24},{1,25},{2,26},{3,27},{4,28},{5,29},{6,30},{7,31},{8,0},{9,1... | collective-permute-start | bytes 350216 | tf_op jit(solution)/shard_map/ppermute | solution.py:34
  21.0 2.5 %collective-permute-done = bf16[8,7296]{1,0:T(8,128)(2,1)S(1)} collective-permute-done((bf16[8,7296]{1,0:T(8,128)(2,1)S(1)}, bf16[8,7296]{1,0:T(8,128)(2,1)S(1)}, u32[]{:S(2)}, u32[]{:S(2)}) %collective-permute-start) | collective-permute-done | bytes 116768 | tf_op jit(solution)/shard_map/ppermute | solution.py:34
  25.1 2.6 %collective-permute-start.4 = (bf16[32,7296]{1,0:T(8,128)(2,1)S(1)}, bf16[32,7296]{1,0:T(8,128)(2,1)S(1)}, u32[]{:S(2)}, u32[]{:S(2)}) collective-permute-start(bf16[32,7296]{1,0:T(8,128)(2,1)S(1)} %constant_dynamic-update-slice_fusion.refs_0_), channel_id=1, source_target_pairs={{0,6},{1,7},{2,0},{3,1},{4,2},{5,3},{6,4},{7,5},{8,14},{9,15},{10,... | collective-permute-start | bytes 1400840 | tf_op jit(solution)/shard_map/ppermute | solution.py:34
  27.7 2.8 %collective-permute-start.16 = (bf16[32,7168]{1,0:T(8,128)(2,1)S(1)}, bf16[32,7168]{1,0:T(8,128)(2,1)S(1)}, u32[]{:S(2)}, u32[]{:S(2)}) collective-permute-start(bf16[32,7168]{1,0:T(8,128)(2,1)S(1)} %constant_dynamic-update-slice_fusion.4.refs_10_), channel_id=1, source_target_pairs={{0,6},{1,7},{2,0},{3,1},{4,2},{5,3},{6,4},{7,5},{8,14},{9,15},{10,... | collective-permute-start | bytes 1376264 | tf_op jit(solution)/shard_map/ppermute | solution.py:34
  30.4 3.6 %collective-permute-start.7 = (bf16[32,7296]{1,0:T(8,128)(2,1)S(1)}, bf16[32,7296]{1,0:T(8,128)(2,1)S(1)}, u32[]{:S(2)}, u32[]{:S(2)}) collective-permute-start(bf16[32,7296]{1,0:T(8,128)(2,1)S(1)} %constant_dynamic-update-slice_fusion.refs_0_), channel_id=1, source_target_pairs={{0,1},{1,0},{2,3},{3,2},{4,5},{5,4},{6,7},{7,6},{8,9},{9,8},{10,11... | collective-permute-start | bytes 1400840 | tf_op jit(solution)/shard_map/ppermute | solution.py:34
  34.9 6.9 %collective-permute-start.9 = (bf16[32,7296]{1,0:T(8,128)(2,1)S(1)}, bf16[32,7296]{1,0:T(8,128)(2,1)S(1)}, u32[]{:S(2)}, u32[]{:S(2)}) collective-permute-start(bf16[32,7296]{1,0:T(8,128)(2,1)S(1)} %collective-permute-done.4.refs_2_), channel_id=1, source_target_pairs={{0,1},{1,0},{2,3},{3,2},{4,5},{5,4},{6,7},{7,6},{8,9},{9,8},{10,11... | collective-permute-start | bytes 1400840 | tf_op jit(solution)/shard_map/ppermute | solution.py:34
  41.8 3.7 %collective-permute-start.8 = (bf16[32,7296]{1,0:T(8,128)(2,1)S(1)}, bf16[32,7296]{1,0:T(8,128)(2,1)S(1)}, u32[]{:S(2)}, u32[]{:S(2)}) collective-permute-start(bf16[32,7296]{1,0:T(8,128)(2,1)S(1)} %collective-permute-done.3.refs_1_), channel_id=1, source_target_pairs={{0,1},{1,0},{2,3},{3,2},{4,5},{5,4},{6,7},{7,6},{8,9},{9,8},{10,11... | collective-permute-start | bytes 1400840 | tf_op jit(solution)/shard_map/ppermute | solution.py:34
  45.5 2.7 %collective-permute-start.18 = (bf16[16,7168]{1,0:T(8,128)(2,1)S(1)}, bf16[16,7168]{1,0:T(8,128)(2,1)S(1)}, u32[]{:S(2)}, u32[]{:S(2)}) collective-permute-start(bf16[16,7168]{1,0:T(8,128)(2,1)S(1)} %slice.19), channel_id=1, source_target_pairs={{0,6},{1,7},{2,0},{3,1},{4,2},{5,3},{6,4},{7,5},{8,14},{9,15},{10,... | collective-permute-start | bytes 688136 | tf_op jit(solution)/shard_map/ppermute | solution.py:34
  48.4 1.5 collective-permute-start.5
  49.9 1.3 collective-permute-done.18.refs_14_
  51.2 4.4 %collective-permute-done.6.refs_4_ = bf16[16,7296]{1,0:T(8,128)(2,1)S(1)} collective-permute-done((bf16[16,7296]{1,0:T(8,128)(2,1)S(1)}, bf16[16,7296]{1,0:T(8,128)(2,1)S(1)}, u32[]{:S(2)}, u32[]{:S(2)}) %collective-permute-start.6) | collective-permute-done | bytes 233504 | tf_op jit(solution)/shard_map/ppermute | solution.py:34
  55.6 3.4 %collective-permute-start.11 = (bf16[16,7296]{1,0:T(8,128)(2,1)S(1)}, bf16[16,7296]{1,0:T(8,128)(2,1)S(1)}, u32[]{:S(2)}, u32[]{:S(2)}) collective-permute-start(bf16[16,7296]{1,0:T(8,128)(2,1)S(1)} %collective-permute-done.6.refs_4_), channel_id=1, source_target_pairs={{0,1},{1,0},{2,3},{3,2},{4,5},{5,4},{6,7},{7,6},{8,9},{9,8},{10,11... | collective-permute-start | bytes 700424 | tf_op jit(solution)/shard_map/ppermute | solution.py:34
  59.1 1.9 %collective-permute-start.10 = (bf16[16,7296]{1,0:T(8,128)(2,1)S(1)}, bf16[16,7296]{1,0:T(8,128)(2,1)S(1)}, u32[]{:S(2)}, u32[]{:S(2)}) collective-permute-start(bf16[16,7296]{1,0:T(8,128)(2,1)S(1)} %collective-permute-done.5.refs_3_), channel_id=1, source_target_pairs={{0,1},{1,0},{2,3},{3,2},{4,5},{5,4},{6,7},{7,6},{8,9},{9,8},{10,11... | collective-permute-start | bytes 700424 | tf_op jit(solution)/shard_map/ppermute | solution.py:34
  60.9 3.3 %collective-permute-start.19 = (bf16[32,7168]{1,0:T(8,128)(2,1)S(1)}, bf16[32,7168]{1,0:T(8,128)(2,1)S(1)}, u32[]{:S(2)}, u32[]{:S(2)}) collective-permute-start(bf16[32,7168]{1,0:T(8,128)(2,1)S(1)} %constant_dynamic-update-slice_fusion.4.refs_10_), channel_id=1, source_target_pairs={{0,1},{1,0},{2,3},{3,2},{4,5},{5,4},{6,7},{7,6},{8,9},{9,8},{10,11... | collective-permute-start | bytes 1376264 | tf_op jit(solution)/shard_map/ppermute | solution.py:34
  67.7 5.9 %shard_map.79 = (bf16[256,256]{1,0:T(8,128)(2,1)S(1)}, bf16[256,128]{1,0:T(8,128)(2,1)S(1)}, bf16[3,7168,128]{2,1,0:T(8,128)(2,1)S(1)}) custom-call(bf16[32,7296]{1,0:T(8,128)(2,1)S(1)} %constant_dynamic-update-slice_fusion.refs_0_, bf16[32,7296]{1,0:T(8,128)(2,1)S(1)} %collective-permute-done.3.refs_1_, ...), custom_call_target="tpu_custom_call" | custom-call | tf_op jit(solution)/shard_map/pallas_call | solution.py:40
  73.6 2.4 %copy-done.2 = bf16[3,7168,128]{2,1,0:T(8,128)(2,1)} copy-done((bf16[3,7168,128]{2,1,0:T(8,128)(2,1)}, bf16[3,7168,128]{2,1,0:T(8,128)(2,1)S(1)}, u32[]{:S(2)}) %copy-start.2) | copy-done | bytes 5505048
  76.0 2.6 %copy-done.1 = bf16[7168,3,128]{2,0,1:T(8,128)(2,1)S(1)} copy-done((bf16[7168,3,128]{2,0,1:T(8,128)(2,1)S(1)}, bf16[7168,3,128]{2,0,1:T(8,128)(2,1)}, u32[]{:S(2)}) %copy-start.1) | copy-done | bytes 5505048
  80.2 3.5 %collective-permute-done.24.got_ref = bf16[128,7296]{1,0:T(8,128)(2,1)S(1)} collective-permute-done((bf16[128,7296]{1,0:T(8,128)(2,1)S(1)}, bf16[128,7296]{1,0:T(8,128)(2,1)S(1)}, u32[]{:S(2)}, u32[]{:S(2)}) %collective-permute-start.24) | collective-permute-done | bytes 1867808 | tf_op jit(solution)/shard_map/ppermute | solution.py:34
  84.1 1.8 %collective-permute-start.25 = (bf16[32,7296]{1,0:T(8,128)(2,1)S(1)}, bf16[32,7296]{1,0:T(8,128)(2,1)S(1)}, u32[]{:S(2)}, u32[]{:S(2)}) collective-permute-start(bf16[32,7296]{1,0:T(8,128)(2,1)S(1)} %get-tuple-element.39), channel_id=1, source_target_pairs={{0,6},{1,7},{2,0},{3,1},{4,2},{5,3},{6,4},{7,5},{8,14},{9,15},{10,... | collective-permute-start | bytes 1400840 | tf_op jit(solution)/shard_map/ppermute | solution.py:34
  85.9 1.5 collective-permute-start.27
  87.4 8.8 %collective-permute-done.25.b_ref = bf16[32,7296]{1,0:T(8,128)(2,1)S(1)} collective-permute-done((bf16[32,7296]{1,0:T(8,128)(2,1)S(1)}, bf16[32,7296]{1,0:T(8,128)(2,1)S(1)}, u32[]{:S(2)}, u32[]{:S(2)}) %collective-permute-start.25) | collective-permute-done | bytes 466976 | tf_op jit(solution)/shard_map/ppermute | solution.py:34
  96.2 3.5 %collective-permute-done.26.c_ref = bf16[32,7296]{1,0:T(8,128)(2,1)S(1)} collective-permute-done((bf16[32,7296]{1,0:T(8,128)(2,1)S(1)}, bf16[32,7296]{1,0:T(8,128)(2,1)S(1)}, u32[]{:S(2)}, u32[]{:S(2)}) %collective-permute-start.26) | collective-permute-done | bytes 466976 | tf_op jit(solution)/shard_map/ppermute | solution.py:34
  99.6 8.3 %collective-permute-done.27.d_ref = bf16[32,7296]{1,0:T(8,128)(2,1)S(1)} collective-permute-done((bf16[32,7296]{1,0:T(8,128)(2,1)S(1)}, bf16[32,7296]{1,0:T(8,128)(2,1)S(1)}, u32[]{:S(2)}, u32[]{:S(2)}) %collective-permute-start.27) | collective-permute-done | bytes 466976 | tf_op jit(solution)/shard_map/ppermute | solution.py:34
  108.1 4.9 %collective-permute-start.28 = (bf16[8,7296]{1,0:T(8,128)(2,1)S(1)}, bf16[8,7296]{1,0:T(8,128)(2,1)S(1)}, u32[]{:S(2)}, u32[]{:S(2)}) collective-permute-start(bf16[8,7296]{1,0:T(8,128)(2,1)S(1)} %get-tuple-element.43), channel_id=1, source_target_pairs={{0,24},{1,25},{2,26},{3,27},{4,28},{5,29},{6,30},{7,31},{8,0},{9,1... | collective-permute-start | bytes 350216 | tf_op jit(solution)/shard_map/ppermute | solution.py:34
  113.7 2.3 %collective-permute-done.28.b1 = bf16[8,7296]{1,0:T(8,128)(2,1)S(1)} collective-permute-done((bf16[8,7296]{1,0:T(8,128)(2,1)S(1)}, bf16[8,7296]{1,0:T(8,128)(2,1)S(1)}, u32[]{:S(2)}, u32[]{:S(2)}) %collective-permute-start.28) | collective-permute-done | bytes 116768 | tf_op jit(solution)/shard_map/ppermute | solution.py:34
  116.0 2.3 %collective-permute-done.29.b2 = bf16[8,7296]{1,0:T(8,128)(2,1)S(1)} collective-permute-done((bf16[8,7296]{1,0:T(8,128)(2,1)S(1)}, bf16[8,7296]{1,0:T(8,128)(2,1)S(1)}, u32[]{:S(2)}, u32[]{:S(2)}) %collective-permute-start.29) | collective-permute-done | bytes 116768 | tf_op jit(solution)/shard_map/ppermute | solution.py:34
  118.3 1.3 collective-permute-done.30.b3
  119.6 2.1 %shard_map.83 = (bf16[128,7168]{1,0:T(8,128)(2,1)}, f32[8,128]{1,0:T(8,128)}) custom-call(s32[1]{0:T(128)} %bitcast.y_ref, s32[8,128]{1,0:T(8,128)S(1)} %bitcast.11, bf16[8,7296]{1,0:T(8,128)(2,1)S(1)} %get-tuple-element.42.b0, bf16[8,7296]{1,0:T(8,128)(2,1)S(1)} %collective-permute-done.28.b1, bf16[8,7296]{1,0:T(8,128)(2,1)S(1)} %collective-permute-done.29.b2, ...), custom_call_target="tpu_custom_call" | custom-call | tf_op jit(solution)/shard_map/pallas_call | solution.py:40
  121.6 25.8 %reduce-scatter.2.cloned.1.call-done = bf16[3,896,128]{2,1,0:T(8,128)(2,1)} async-done(((bf16[3,7168,128]{2,1,0:T(8,128)(2,1)}), bf16[3,896,128]{2,1,0:T(8,128)(2,1)}) %reduce-scatter.2.cloned.1.call-update) | async-done | bytes 688144 | tf_op jit(solution)/shard_map/reduce_scatter | solution.py:223
  (71 shorter events, 14.6 us)
Async XLA Ops:
  7.2 140.3 %reduce-scatter.2.cloned.1.call-start = ((), (), s32[]{:S(2)}) async-start(), calls=%async_computation.1 | async-start | bytes 6193152 | tf_op jit(solution)/shard_map/reduce_scatter | solution.py:223
  10.1 9.1 %collective-permute-start.12 = (bf16[8,7168]{1,0:T(8,128)(2,1)S(1)}, bf16[8,7168]{1,0:T(8,128)(2,1)S(1)}, u32[]{:S(2)}, u32[]{:S(2)}) collective-permute-start(bf16[8,7168]{1,0:T(8,128)(2,1)S(1)} %get-tuple-element.31), channel_id=1, source_target_pairs={{0,8},{1,9},{2,10},{3,11},{4,12},{5,13},{6,14},{7,15},{8,16},{9,17... | collective-permute-start | bytes 344072 | tf_op jit(solution)/shard_map/ppermute | solution.py:34
  12.3 8.7 %collective-permute-start.13 = (bf16[8,7168]{1,0:T(8,128)(2,1)S(1)}, bf16[8,7168]{1,0:T(8,128)(2,1)S(1)}, u32[]{:S(2)}, u32[]{:S(2)}) collective-permute-start(bf16[8,7168]{1,0:T(8,128)(2,1)S(1)} %get-tuple-element.32), channel_id=1, source_target_pairs={{0,16},{1,17},{2,18},{3,19},{4,20},{5,21},{6,22},{7,23},{8,24},{9,... | collective-permute-start | bytes 344072 | tf_op jit(solution)/shard_map/ppermute | solution.py:34
  14.9 12.8 %collective-permute-start.14 = (bf16[8,7168]{1,0:T(8,128)(2,1)S(1)}, bf16[8,7168]{1,0:T(8,128)(2,1)S(1)}, u32[]{:S(2)}, u32[]{:S(2)}) collective-permute-start(bf16[8,7168]{1,0:T(8,128)(2,1)S(1)} %get-tuple-element.33), channel_id=1, source_target_pairs={{0,24},{1,25},{2,26},{3,27},{4,28},{5,29},{6,30},{7,31},{8,0},{9,1... | collective-permute-start | bytes 344072 | tf_op jit(solution)/shard_map/ppermute | solution.py:34
  17.8 5.6 %collective-permute-start = (bf16[8,7296]{1,0:T(8,128)(2,1)S(1)}, bf16[8,7296]{1,0:T(8,128)(2,1)S(1)}, u32[]{:S(2)}, u32[]{:S(2)}) collective-permute-start(bf16[8,7296]{1,0:T(8,128)(2,1)S(1)} %get-tuple-element.27), channel_id=1, source_target_pairs={{0,8},{1,9},{2,10},{3,11},{4,12},{5,13},{6,14},{7,15},{8,16},{9,17... | collective-permute-start | bytes 350216 | tf_op jit(solution)/shard_map/ppermute | solution.py:34
  18.3 6.3 %collective-permute-start.1 = (bf16[8,7296]{1,0:T(8,128)(2,1)S(1)}, bf16[8,7296]{1,0:T(8,128)(2,1)S(1)}, u32[]{:S(2)}, u32[]{:S(2)}) collective-permute-start(bf16[8,7296]{1,0:T(8,128)(2,1)S(1)} %get-tuple-element.28), channel_id=1, source_target_pairs={{0,16},{1,17},{2,18},{3,19},{4,20},{5,21},{6,22},{7,23},{8,24},{9,... | collective-permute-start | bytes 350216 | tf_op jit(solution)/shard_map/ppermute | solution.py:34
  19.1 5.9 %collective-permute-start.2 = (bf16[8,7296]{1,0:T(8,128)(2,1)S(1)}, bf16[8,7296]{1,0:T(8,128)(2,1)S(1)}, u32[]{:S(2)}, u32[]{:S(2)}) collective-permute-start(bf16[8,7296]{1,0:T(8,128)(2,1)S(1)} %get-tuple-element.29), channel_id=1, source_target_pairs={{0,24},{1,25},{2,26},{3,27},{4,28},{5,29},{6,30},{7,31},{8,0},{9,1... | collective-permute-start | bytes 350216 | tf_op jit(solution)/shard_map/ppermute | solution.py:34
  25.1 9.8 %collective-permute-start.4 = (bf16[32,7296]{1,0:T(8,128)(2,1)S(1)}, bf16[32,7296]{1,0:T(8,128)(2,1)S(1)}, u32[]{:S(2)}, u32[]{:S(2)}) collective-permute-start(bf16[32,7296]{1,0:T(8,128)(2,1)S(1)} %constant_dynamic-update-slice_fusion.refs_0_), channel_id=1, source_target_pairs={{0,6},{1,7},{2,0},{3,1},{4,2},{5,3},{6,4},{7,5},{8,14},{9,15},{10,... | collective-permute-start | bytes 1400840 | tf_op jit(solution)/shard_map/ppermute | solution.py:34
  27.7 14.2 %collective-permute-start.3 = (bf16[32,7296]{1,0:T(8,128)(2,1)S(1)}, bf16[32,7296]{1,0:T(8,128)(2,1)S(1)}, u32[]{:S(2)}, u32[]{:S(2)}) collective-permute-start(bf16[32,7296]{1,0:T(8,128)(2,1)S(1)} %constant_dynamic-update-slice_fusion.refs_0_), channel_id=1, source_target_pairs={{0,2},{1,3},{2,4},{3,5},{4,6},{5,7},{6,0},{7,1},{8,10},{9,11},{10,... | collective-permute-start | bytes 1400840 | tf_op jit(solution)/shard_map/ppermute | solution.py:34
  27.7 17.8 %collective-permute-start.16 = (bf16[32,7168]{1,0:T(8,128)(2,1)S(1)}, bf16[32,7168]{1,0:T(8,128)(2,1)S(1)}, u32[]{:S(2)}, u32[]{:S(2)}) collective-permute-start(bf16[32,7168]{1,0:T(8,128)(2,1)S(1)} %constant_dynamic-update-slice_fusion.4.refs_10_), channel_id=1, source_target_pairs={{0,6},{1,7},{2,0},{3,1},{4,2},{5,3},{6,4},{7,5},{8,14},{9,15},{10,... | collective-permute-start | bytes 1376264 | tf_op jit(solution)/shard_map/ppermute | solution.py:34
  30.4 18.0 %collective-permute-start.7 = (bf16[32,7296]{1,0:T(8,128)(2,1)S(1)}, bf16[32,7296]{1,0:T(8,128)(2,1)S(1)}, u32[]{:S(2)}, u32[]{:S(2)}) collective-permute-start(bf16[32,7296]{1,0:T(8,128)(2,1)S(1)} %constant_dynamic-update-slice_fusion.refs_0_), channel_id=1, source_target_pairs={{0,1},{1,0},{2,3},{3,2},{4,5},{5,4},{6,7},{7,6},{8,9},{9,8},{10,11... | collective-permute-start | bytes 1400840 | tf_op jit(solution)/shard_map/ppermute | solution.py:34
  34.0 14.3 %collective-permute-start.15 = (bf16[32,7168]{1,0:T(8,128)(2,1)S(1)}, bf16[32,7168]{1,0:T(8,128)(2,1)S(1)}, u32[]{:S(2)}, u32[]{:S(2)}) collective-permute-start(bf16[32,7168]{1,0:T(8,128)(2,1)S(1)} %constant_dynamic-update-slice_fusion.4.refs_10_), channel_id=1, source_target_pairs={{0,2},{1,3},{2,4},{3,5},{4,6},{5,7},{6,0},{7,1},{8,10},{9,11},{10,... | collective-permute-start | bytes 1376264 | tf_op jit(solution)/shard_map/ppermute | solution.py:34
  34.9 29.4 %collective-permute-start.9 = (bf16[32,7296]{1,0:T(8,128)(2,1)S(1)}, bf16[32,7296]{1,0:T(8,128)(2,1)S(1)}, u32[]{:S(2)}, u32[]{:S(2)}) collective-permute-start(bf16[32,7296]{1,0:T(8,128)(2,1)S(1)} %collective-permute-done.4.refs_2_), channel_id=1, source_target_pairs={{0,1},{1,0},{2,3},{3,2},{4,5},{5,4},{6,7},{7,6},{8,9},{9,8},{10,11... | collective-permute-start | bytes 1400840 | tf_op jit(solution)/shard_map/ppermute | solution.py:34
  41.8 22.5 %collective-permute-start.8 = (bf16[32,7296]{1,0:T(8,128)(2,1)S(1)}, bf16[32,7296]{1,0:T(8,128)(2,1)S(1)}, u32[]{:S(2)}, u32[]{:S(2)}) collective-permute-start(bf16[32,7296]{1,0:T(8,128)(2,1)S(1)} %collective-permute-done.3.refs_1_), channel_id=1, source_target_pairs={{0,1},{1,0},{2,3},{3,2},{4,5},{5,4},{6,7},{7,6},{8,9},{9,8},{10,11... | collective-permute-start | bytes 1400840 | tf_op jit(solution)/shard_map/ppermute | solution.py:34
  45.5 5.7 %collective-permute-start.18 = (bf16[16,7168]{1,0:T(8,128)(2,1)S(1)}, bf16[16,7168]{1,0:T(8,128)(2,1)S(1)}, u32[]{:S(2)}, u32[]{:S(2)}) collective-permute-start(bf16[16,7168]{1,0:T(8,128)(2,1)S(1)} %slice.19), channel_id=1, source_target_pairs={{0,6},{1,7},{2,0},{3,1},{4,2},{5,3},{6,4},{7,5},{8,14},{9,15},{10,... | collective-permute-start | bytes 688136 | tf_op jit(solution)/shard_map/ppermute | solution.py:34
  48.3 7.3 %collective-permute-start.6 = (bf16[16,7296]{1,0:T(8,128)(2,1)S(1)}, bf16[16,7296]{1,0:T(8,128)(2,1)S(1)}, u32[]{:S(2)}, u32[]{:S(2)}) collective-permute-start(bf16[16,7296]{1,0:T(8,128)(2,1)S(1)} %slice.17), channel_id=1, source_target_pairs={{0,6},{1,7},{2,0},{3,1},{4,2},{5,3},{6,4},{7,5},{8,14},{9,15},{10,... | collective-permute-start | bytes 700424 | tf_op jit(solution)/shard_map/ppermute | solution.py:34
  48.4 10.7 %collective-permute-start.5 = (bf16[16,7296]{1,0:T(8,128)(2,1)S(1)}, bf16[16,7296]{1,0:T(8,128)(2,1)S(1)}, u32[]{:S(2)}, u32[]{:S(2)}) collective-permute-start(bf16[16,7296]{1,0:T(8,128)(2,1)S(1)} %slice.16), channel_id=1, source_target_pairs={{0,2},{1,3},{2,4},{3,5},{4,6},{5,7},{6,0},{7,1},{8,10},{9,11},{10,... | collective-permute-start | bytes 700424 | tf_op jit(solution)/shard_map/ppermute | solution.py:34
  51.2 9.7 %collective-permute-start.17 = (bf16[16,7168]{1,0:T(8,128)(2,1)S(1)}, bf16[16,7168]{1,0:T(8,128)(2,1)S(1)}, u32[]{:S(2)}, u32[]{:S(2)}) collective-permute-start(bf16[16,7168]{1,0:T(8,128)(2,1)S(1)} %slice.18), channel_id=1, source_target_pairs={{0,2},{1,3},{2,4},{3,5},{4,6},{5,7},{6,0},{7,1},{8,10},{9,11},{10,... | collective-permute-start | bytes 688136 | tf_op jit(solution)/shard_map/ppermute | solution.py:34
  55.6 9.1 %collective-permute-start.11 = (bf16[16,7296]{1,0:T(8,128)(2,1)S(1)}, bf16[16,7296]{1,0:T(8,128)(2,1)S(1)}, u32[]{:S(2)}, u32[]{:S(2)}) collective-permute-start(bf16[16,7296]{1,0:T(8,128)(2,1)S(1)} %collective-permute-done.6.refs_4_), channel_id=1, source_target_pairs={{0,1},{1,0},{2,3},{3,2},{4,5},{5,4},{6,7},{7,6},{8,9},{9,8},{10,11... | collective-permute-start | bytes 700424 | tf_op jit(solution)/shard_map/ppermute | solution.py:34
  59.1 5.8 %collective-permute-start.10 = (bf16[16,7296]{1,0:T(8,128)(2,1)S(1)}, bf16[16,7296]{1,0:T(8,128)(2,1)S(1)}, u32[]{:S(2)}, u32[]{:S(2)}) collective-permute-start(bf16[16,7296]{1,0:T(8,128)(2,1)S(1)} %collective-permute-done.5.refs_3_), channel_id=1, source_target_pairs={{0,1},{1,0},{2,3},{3,2},{4,5},{5,4},{6,7},{7,6},{8,9},{9,8},{10,11... | collective-permute-start | bytes 700424 | tf_op jit(solution)/shard_map/ppermute | solution.py:34
  60.9 5.5 %collective-permute-start.19 = (bf16[32,7168]{1,0:T(8,128)(2,1)S(1)}, bf16[32,7168]{1,0:T(8,128)(2,1)S(1)}, u32[]{:S(2)}, u32[]{:S(2)}) collective-permute-start(bf16[32,7168]{1,0:T(8,128)(2,1)S(1)} %constant_dynamic-update-slice_fusion.4.refs_10_), channel_id=1, source_target_pairs={{0,1},{1,0},{2,3},{3,2},{4,5},{5,4},{6,7},{7,6},{8,9},{9,8},{10,11... | collective-permute-start | bytes 1376264 | tf_op jit(solution)/shard_map/ppermute | solution.py:34
  64.3 3.1 %collective-permute-start.21 = (bf16[32,7168]{1,0:T(8,128)(2,1)S(1)}, bf16[32,7168]{1,0:T(8,128)(2,1)S(1)}, u32[]{:S(2)}, u32[]{:S(2)}) collective-permute-start(bf16[32,7168]{1,0:T(8,128)(2,1)S(1)} %collective-permute-done.16.refs_12_), channel_id=1, source_target_pairs={{0,1},{1,0},{2,3},{3,2},{4,5},{5,4},{6,7},{7,6},{8,9},{9,8},{10,11... | collective-permute-start | bytes 1376264 | tf_op jit(solution)/shard_map/ppermute | solution.py:34
  64.3 3.4 %collective-permute-start.20 = (bf16[32,7168]{1,0:T(8,128)(2,1)S(1)}, bf16[32,7168]{1,0:T(8,128)(2,1)S(1)}, u32[]{:S(2)}, u32[]{:S(2)}) collective-permute-start(bf16[32,7168]{1,0:T(8,128)(2,1)S(1)} %collective-permute-done.15.refs_11_), channel_id=1, source_target_pairs={{0,1},{1,0},{2,3},{3,2},{4,5},{5,4},{6,7},{7,6},{8,9},{9,8},{10,11... | collective-permute-start | bytes 1376264 | tf_op jit(solution)/shard_map/ppermute | solution.py:34
  64.8 2.6 %collective-permute-start.23 = (bf16[16,7168]{1,0:T(8,128)(2,1)S(1)}, bf16[16,7168]{1,0:T(8,128)(2,1)S(1)}, u32[]{:S(2)}, u32[]{:S(2)}) collective-permute-start(bf16[16,7168]{1,0:T(8,128)(2,1)S(1)} %collective-permute-done.18.refs_14_), channel_id=1, source_target_pairs={{0,1},{1,0},{2,3},{3,2},{4,5},{5,4},{6,7},{7,6},{8,9},{9,8},{10,11... | collective-permute-start | bytes 688136 | tf_op jit(solution)/shard_map/ppermute | solution.py:34
  64.9 2.8 %collective-permute-start.22 = (bf16[16,7168]{1,0:T(8,128)(2,1)S(1)}, bf16[16,7168]{1,0:T(8,128)(2,1)S(1)}, u32[]{:S(2)}, u32[]{:S(2)}) collective-permute-start(bf16[16,7168]{1,0:T(8,128)(2,1)S(1)} %collective-permute-done.17.refs_13_), channel_id=1, source_target_pairs={{0,1},{1,0},{2,3},{3,2},{4,5},{5,4},{6,7},{7,6},{8,9},{9,8},{10,11... | collective-permute-start | bytes 688136 | tf_op jit(solution)/shard_map/ppermute | solution.py:34
  79.7 3.9 %collective-permute-start.24 = (bf16[128,7296]{1,0:T(8,128)(2,1)S(1)}, bf16[128,7296]{1,0:T(8,128)(2,1)S(1)}, u32[]{:S(2)}, u32[]{:S(2)}) collective-permute-start(bf16[128,7296]{1,0:T(8,128)(2,1)S(1)} %get-tuple-element.37), channel_id=1, source_target_pairs={{0,1},{1,0},{2,3},{3,2},{4,5},{5,4},{6,7},{7,6},{8,9},{9,8},{10,11... | collective-permute-start | bytes 5603336 | tf_op jit(solution)/shard_map/ppermute | solution.py:34
  84.1 12.1 %collective-permute-start.25 = (bf16[32,7296]{1,0:T(8,128)(2,1)S(1)}, bf16[32,7296]{1,0:T(8,128)(2,1)S(1)}, u32[]{:S(2)}, u32[]{:S(2)}) collective-permute-start(bf16[32,7296]{1,0:T(8,128)(2,1)S(1)} %get-tuple-element.39), channel_id=1, source_target_pairs={{0,6},{1,7},{2,0},{3,1},{4,2},{5,3},{6,4},{7,5},{8,14},{9,15},{10,... | collective-permute-start | bytes 1400840 | tf_op jit(solution)/shard_map/ppermute | solution.py:34
  85.9 13.7 %collective-permute-start.26 = (bf16[32,7296]{1,0:T(8,128)(2,1)S(1)}, bf16[32,7296]{1,0:T(8,128)(2,1)S(1)}, u32[]{:S(2)}, u32[]{:S(2)}) collective-permute-start(bf16[32,7296]{1,0:T(8,128)(2,1)S(1)} %get-tuple-element.40), channel_id=1, source_target_pairs={{0,2},{1,3},{2,4},{3,5},{4,6},{5,7},{6,0},{7,1},{8,10},{9,11},{10,... | collective-permute-start | bytes 1400840 | tf_op jit(solution)/shard_map/ppermute | solution.py:34
  85.9 22.0 %collective-permute-start.27 = (bf16[32,7296]{1,0:T(8,128)(2,1)S(1)}, bf16[32,7296]{1,0:T(8,128)(2,1)S(1)}, u32[]{:S(2)}, u32[]{:S(2)}) collective-permute-start(bf16[32,7296]{1,0:T(8,128)(2,1)S(1)} %get-tuple-element.41), channel_id=1, source_target_pairs={{0,4},{1,5},{2,6},{3,7},{4,0},{5,1},{6,2},{7,3},{8,12},{9,13},{10,... | collective-permute-start | bytes 1400840 | tf_op jit(solution)/shard_map/ppermute | solution.py:34
  108.1 7.9 %collective-permute-start.28 = (bf16[8,7296]{1,0:T(8,128)(2,1)S(1)}, bf16[8,7296]{1,0:T(8,128)(2,1)S(1)}, u32[]{:S(2)}, u32[]{:S(2)}) collective-permute-start(bf16[8,7296]{1,0:T(8,128)(2,1)S(1)} %get-tuple-element.43), channel_id=1, source_target_pairs={{0,24},{1,25},{2,26},{3,27},{4,28},{5,29},{6,30},{7,31},{8,0},{9,1... | collective-permute-start | bytes 350216 | tf_op jit(solution)/shard_map/ppermute | solution.py:34
  113.0 5.3 %collective-permute-start.29 = (bf16[8,7296]{1,0:T(8,128)(2,1)S(1)}, bf16[8,7296]{1,0:T(8,128)(2,1)S(1)}, u32[]{:S(2)}, u32[]{:S(2)}) collective-permute-start(bf16[8,7296]{1,0:T(8,128)(2,1)S(1)} %get-tuple-element.44), channel_id=1, source_target_pairs={{0,16},{1,17},{2,18},{3,19},{4,20},{5,21},{6,22},{7,23},{8,24},{9,... | collective-permute-start | bytes 350216 | tf_op jit(solution)/shard_map/ppermute | solution.py:34
  113.0 6.5 %collective-permute-start.30 = (bf16[8,7296]{1,0:T(8,128)(2,1)S(1)}, bf16[8,7296]{1,0:T(8,128)(2,1)S(1)}, u32[]{:S(2)}, u32[]{:S(2)}) collective-permute-start(bf16[8,7296]{1,0:T(8,128)(2,1)S(1)} %get-tuple-element.45), channel_id=1, source_target_pairs={{0,8},{1,9},{2,10},{3,11},{4,12},{5,13},{6,14},{7,15},{8,16},{9,17... | collective-permute-start | bytes 350216 | tf_op jit(solution)/shard_map/ppermute | solution.py:34
  (9 other events, 100.9 us)
Sparse Core Ops, SparseCore 0:
  76.1 71.2 reduce-scatter.1

commit v2 on v1

v2 whole, which is shorter than its diff:
```python
import functools
import math

import jax
import jax.numpy as jnp
from jax import lax
from jax.experimental import pallas as pl
from jax.experimental.pallas import tpu as pltpu
from jax.sharding import PartitionSpec as P

GROUP = 8
MOST = 8
N_WIN = 4
NX = 4
NC = 2
SLOTS = N_WIN * MOST
LANES = 128
CHUNK = 1024
F32 = jnp.float32
BF16 = jnp.bfloat16
VMEM = pltpu.MemorySpace.VMEM
SMEM = pltpu.MemorySpace.SMEM


def shifted(dy, dx, dc):
    pairs = []
    for y in range(N_WIN):
        for x in range(NX):
            for c in range(NC):
                to = (((y + dy) % N_WIN) * NX + (x + dx) % NX) * NC + (c + dc) % NC
                pairs.append(((y * NX + x) * NC + c, to))
    return pairs


def send(array, dy=0, dx=0, dc=0):
    return lax.ppermute(array, "expert", shifted(dy, dx, dc))


def after(array, *others):
    return lax.optimization_barrier((array, *others))[0]


def call(body, outs, operands, scalars=0, flops=0, limit=12):
    moved = sum(o.size * o.dtype.itemsize for o in operands)
    moved += sum(math.prod(s) * jnp.dtype(d).itemsize for s, d in outs)
    specs = [pl.BlockSpec(memory_space=SMEM)] * scalars
    specs += [pl.BlockSpec(memory_space=VMEM)] * (len(operands) - scalars)
    return pl.pallas_call(
        body,
        out_shape=[jax.ShapeDtypeStruct(s, d) for s, d in outs],
        in_specs=specs,
        out_specs=[pl.BlockSpec(memory_space=VMEM)] * len(outs),
        cost_estimate=pl.CostEstimate(flops=flops, bytes_accessed=moved, transcendentals=0),
        compiler_params=pltpu.CompilerParams(vmem_limit_bytes=limit * 1024 * 1024),
    )(*operands)


def slots_of(y_ref, routes_ref):
    routes = routes_ref[...]
    rows = routes.shape[1]
    window = routes < N_WIN
    expert = jnp.sum(jnp.where(window, routes, 0), axis=0, keepdims=True)
    has = jnp.sum(jnp.where(window, 1, 0), axis=0, keepdims=True) > 0
    near = (expert + N_WIN - y_ref[0]) & (N_WIN - 1)
    member = (lax.broadcasted_iota(jnp.int32, (MOST, rows), 0) == near) & has
    upto = lax.broadcasted_iota(jnp.int32, (rows, rows), 0) <= lax.broadcasted_iota(
        jnp.int32, (rows, rows), 1
    )
    ones = jnp.where(member, 1.0, 0.0)
    rank = jnp.dot(
        ones.astype(BF16), jnp.where(upto, 1.0, 0.0).astype(BF16), preferred_element_type=F32
    )
    base = lax.broadcasted_iota(jnp.int32, (MOST, rows), 0).astype(F32) * MOST
    slot = jnp.sum(ones * (base + rank), axis=0, keepdims=True) - 1.0
    slot = jnp.where(has, slot, -1.0).astype(jnp.int32)
    return window, lax.broadcasted_iota(jnp.int32, (SLOTS, rows), 0) == slot


def pick_rows(y_ref, routes_ref, rw_ref, tok_ref, cot_ref, *outs):
    window, select = slots_of(y_ref, routes_ref)
    weight = jnp.sum(jnp.where(window, rw_ref[...].astype(F32), 0.0), axis=0, keepdims=True)
    chosen = jnp.sum(jnp.where(select, weight, 0.0), axis=1, keepdims=True)
    one = jnp.where(select, 1.0, 0.0).astype(BF16)
    rows_x = jnp.dot(one, tok_ref[...], preferred_element_type=F32)
    rows_dy = jnp.dot(one, cot_ref[...], preferred_element_type=F32)
    width = rows_x.shape[1]
    lanes = jnp.broadcast_to(chosen, (SLOTS, LANES))
    for k, out in enumerate(outs):
        at = slice(k * MOST, (k + 1) * MOST)
        out[:, :width] = rows_x[at].astype(BF16)
        out[:, width : width + LANES] = lanes[at].astype(BF16)
        out[:, width + LANES :] = rows_dy[at].astype(BF16)


def cut_columns(top_ref, bottom_ref, out):
    piece = out.shape[1]
    half = top_ref.shape[0]
    n_dp = out.shape[0] // (2 * SLOTS)
    for z in range(n_dp):
        for k, first in enumerate((z * piece, n_dp * piece + LANES + z * piece)):
            cols = slice(first, first + piece)
            at = (2 * z + k) * SLOTS
            out[at : at + half, :] = top_ref[:, cols]
            out[at + half : at + SLOTS, :] = bottom_ref[:, cols]


def join(*refs):
    for k, out in enumerate(refs[N_WIN:]):
        two = [b[...].astype(F32) for b in refs[2 * k : 2 * k + 2]]
        out[...] = jnp.concatenate(two, axis=0).astype(BF16)


def rows_of(blocks, cols):
    return jnp.concatenate([b[:, cols] for b in blocks], axis=0)


def side_by_side(w_refs, kinds, cols):
    return jnp.concatenate([w[k, cols, :] for w in w_refs for k in kinds], axis=1)


def experts(n_blocks, *refs):
    blocks, w_refs = refs[:n_blocks], refs[n_blocks : n_blocks + NC]
    g_ref, sw_ref = refs[n_blocks + NC :]
    width, hidden = w_refs[0].shape[1:]
    both, back = None, None
    for at in range(0, width, CHUNK):
        cols = slice(at, at + CHUNK)
        part = jnp.dot(
            rows_of(blocks, cols), side_by_side(w_refs, (0, 1), cols), preferred_element_type=F32
        )
        both = part if both is None else both + part
        rows_dy = rows_of(blocks, slice(width + LANES + at, width + LANES + at + CHUNK))
        part = jnp.dot(rows_dy, side_by_side(w_refs, (2,), cols), preferred_element_type=F32)
        back = part if back is None else back + part
    w = rows_of(blocks, slice(width, width + LANES)).astype(F32)
    sw = None
    grads = []
    for c in range(NC):
        gate = both[:, 2 * c * hidden : (2 * c + 1) * hidden]
        up = both[:, (2 * c + 1) * hidden : (2 * c + 2) * hidden]
        proj = back[:, c * hidden : (c + 1) * hidden]
        sig = jax.nn.sigmoid(gate)
        act = gate * sig
        hid = (act * up).astype(BF16).astype(F32)
        part = jnp.sum(hid * proj, axis=1, keepdims=True)
        sw = part if sw is None else sw + part
        scaled = w * proj
        grads.append((scaled * up * sig * (1.0 + gate * (1.0 - sig))).astype(BF16))
        grads.append((scaled * act).astype(BF16))
        g_ref[:, (2 * NC + c) * hidden : (2 * NC + c + 1) * hidden] = (w * hid).astype(BF16)
    g_ref[:, : 2 * NC * hidden] = jnp.concatenate(grads, axis=1)
    sw_ref[...] = jnp.broadcast_to(sw, (sw.shape[0], LANES)).astype(BF16)


def shard_grads(*refs):
    w_refs, (g_ref, sw_ref), outs = refs[:NC], refs[NC : NC + 2], refs[NC + 2 :]
    width, hidden = w_refs[0].shape[1:]
    d_both = g_ref[:, : 2 * NC * hidden]
    across = (((1,), (1,)), ((), ()))
    for at in range(0, width, CHUNK):
        cols = slice(at, at + CHUNK)
        grad = lax.dot_general(
            d_both, side_by_side(w_refs, (0, 1), cols), across, preferred_element_type=F32
        ).astype(BF16)
        for k, out in enumerate(outs):
            out[:, cols] = grad[k * SLOTS : (k + 1) * SLOTS]
    for k, out in enumerate(outs):
        out[:, width:] = sw_ref[k * SLOTS : (k + 1) * SLOTS, :]


def weight_grads(n_cuts, *refs):
    cuts, (g_ref, mine, other) = refs[:n_cuts], refs[n_cuts:]
    n_dp = g_ref.shape[0]
    hidden = mine.shape[2]
    blocks = [(cuts[0],), (cuts[1],), (cuts[2],), tuple(cuts[3:])]
    down = (((0,), (0,)), ((), ()))
    d_in, d_out = None, None
    for k, block in enumerate(blocks):
        pieces = []
        for ref in block:
            pieces += [ref[at : at + SLOTS, :] for at in range(0, ref.shape[0], SLOTS)]
        rows_x = jnp.concatenate(pieces[0::2], axis=0)
        rows_dy = jnp.concatenate(pieces[1::2], axis=0)
        at = slice(k * SLOTS, (k + 1) * SLOTS)
        grads = jnp.concatenate([g_ref[z, at, :] for z in range(n_dp)], axis=0)
        part_in = lax.dot_general(
            rows_x, grads[:, : 2 * NC * hidden], down, preferred_element_type=F32
        )
        part_out = lax.dot_general(
            rows_dy, grads[:, 2 * NC * hidden :], down, preferred_element_type=F32
        )
        d_in = part_in if d_in is None else d_in + part_in
        d_out = part_out if d_out is None else d_out + part_out
    mine[0] = d_in[:, :hidden]
    mine[1] = d_in[:, hidden : 2 * hidden]
    mine[2] = d_out[:, :hidden]
    other[0] = d_in[:, 2 * hidden : 3 * hidden].astype(BF16)
    other[1] = d_in[:, 3 * hidden :].astype(BF16)
    other[2] = d_out[:, hidden:].astype(BF16)


def add_cores(mine_ref, got_ref, out):
    out[...] = (mine_ref[...] + got_ref[...].astype(F32)).astype(BF16)


def add_all(a_ref, b_ref, c_ref, d_ref, *outs):
    for k, out in enumerate(outs):
        rows = slice(k * MOST, (k + 1) * MOST)
        total = (a_ref[rows, :].astype(F32) + b_ref[rows, :].astype(F32)) + (
            c_ref[rows, :].astype(F32) + d_ref[rows, :].astype(F32)
        )
        out[...] = total.astype(BF16)


def two_halves(left_ref, right_ref, _, *outs):
    half = outs[0].shape[0]
    outs[0][...] = left_ref[:half, :]
    outs[1][...] = right_ref[half:, :]


def put_back(y_ref, routes_ref, b0, b1, b2, b3, dtok_ref, drw_ref):
    window, select = slots_of(y_ref, routes_ref)
    width = dtok_ref.shape[1]
    grads = jnp.concatenate([b[...].astype(F32) for b in (b0, b1, b2, b3)], axis=0)
    one = jnp.where(select, 1.0, 0.0)
    dtok_ref[...] = lax.dot_general(
        one.astype(BF16),
        grads[:, :width].astype(BF16),
        (((0,), (0,)), ((), ())),
        preferred_element_type=F32,
    ).astype(BF16)
    row = jnp.sum(one * grads[:, width : width + 1], axis=0, keepdims=True)
    drw_ref[...] = jnp.where(window, row, 0.0)


def local(tokens, cotangent, routes, route_weights, weights):
    width = tokens.shape[1]
    wide = width + LANES
    hidden = weights.shape[2]
    y = (lax.axis_index("expert") // (NX * NC)).astype(jnp.int32).reshape(1)
    routes_t = routes.T
    w_t = jnp.transpose(weights, (1, 0, 2))
    total = SLOTS * NX

    n_dp = lax.axis_size("dp")
    piece = width // n_dp

    half = SLOTS // 2
    full = wide + width
    out = call(
        pick_rows,
        [((MOST, full), BF16)] * N_WIN,
        [y, routes_t, route_weights.T, tokens, cotangent],
        1,
    )
    got = [out[0]] + [send(out[k], dy=k) for k in range(1, N_WIN)]
    top, bottom = call(join, [((half, full), BF16)] * 2, got)
    left_top, right_bottom = send(top, dx=1), send(bottom, dx=-1)
    left_bottom, right_top = send(bottom, dx=1), send(top, dx=-1)
    far_top, far_bottom = send(left_top, dx=1), send(right_bottom, dx=-1)
    blocks = [top, bottom, left_top, left_bottom, right_top, right_bottom, far_top, far_bottom]
    cut = call(cut_columns, [((2 * n_dp * SLOTS, piece), BF16)], [top, bottom])[0]
    cut = lax.all_to_all(cut, "dp", split_axis=0, concat_axis=0, tiled=True)

    work = 2 * total * width * NC * hidden
    work = 2 * total * width * NC * hidden
    w_all = [w_t, send(w_t, dc=1)]
    g, sw = call(
        functools.partial(experts, len(blocks)),
        [((total, 3 * NC * hidden), BF16), ((total, LANES), BF16)],
        [*blocks, *w_all],
        flops=3 * work,
    )
    keep, to_left, to_right, to_far = call(
        shard_grads, [((SLOTS, wide), BF16)] * NX, [*w_all, g, sw], flops=2 * work
    )
    cut_left, cut_right = send(cut, dx=1), send(cut, dx=-1)
    to_left, to_right, to_far, cut_left, cut_right = lax.optimization_barrier(
        (to_left, to_right, to_far, cut_left, cut_right)
    )
    g_all = lax.all_gather(g, "dp", axis=0)
    back = call(
        add_all,
        [((MOST, wide), BF16)] * N_WIN,
        [keep, send(to_left, dx=-1), send(to_right, dx=1), send(to_far, dx=2)],
    )
    home = [back[0]] + [send(back[k], dy=-k) for k in range(1, N_WIN)]
    top, bottom = call(
        two_halves,
        [((n_dp * SLOTS, piece), BF16)] * 2,
        [cut_left, cut_right, back[0]],
    )
    cuts = [cut, cut_left, cut_right, send(top, dx=1), send(bottom, dx=-1)]
    g_all = after(g_all, *home[1:])
    d_tokens, d_rw = call(
        put_back,
        [(tokens.shape, BF16), (routes_t.shape, F32)],
        [y, routes_t, *home],
        1,
    )
    d_mine, d_other = call(
        functools.partial(weight_grads, len(cuts)),
        [((3, piece, hidden), F32), ((3, piece, hidden), BF16)],
        [*cuts, g_all],
        flops=3 * work,
    )
    d_weights = call(add_cores, [((3, piece, hidden), BF16)], [d_mine, send(d_other, dc=1)])[0]
    return d_tokens, d_rw.T, jnp.transpose(d_weights, (1, 0, 2))


def solution(mesh):
    placed = (
        P(("dp", "expert"), None),
        P(("dp", "expert"), None),
        P(("dp", "expert"), None),
        P(("dp", "expert"), None),
        P(None, None, "expert"),
    )
    return jax.shard_map(
        local,
        mesh=mesh,
        in_specs=placed,
        out_specs=(P(("dp", "expert"), None), P(("dp", "expert"), None), P("dp", None, "expert")),
        check_vma=False,
    )
```

time: 155 us -> 148 us (0.955)
  waiting for transfers between devices: 67.7 us -> 57.6 us
  starting transfers between devices: 51.7 us -> 44.7 us
  Pallas kernels: 11.9 us -> 18.8 us
  local copies, waits for them, and re-layouts: 8.81 us -> 12.2 us
    reduce_scatter x1 -> x0, waiting for transfers between devices: 25.8 us -> none  [local(): lax.psum_scatter(dw, 'dp', scatter_dimension=1, tiled=True)]
    ppermute x31 -> x21, waiting for transfers between devices: 41.8 us -> 57.6 us  [send(): return lax.ppermute(array, 'expert', shifted(dy, dx, dc))]
    ppermute x31 -> x21, starting transfers between devices: 51.7 us -> 37.3 us  [send(): return lax.ppermute(array, 'expert', shifted(dy, dx, dc))]
    all_to_all x0 -> x1, starting transfers between devices: none -> 7.39 us  [local(): cut = lax.all_to_all(cut, 'dp', split_axis=0, concat_axis=0, tiled=True)]
    pallas_call x8 -> x10, Pallas kernels: 11.9 us -> 18.8 us  [call(): pl.pallas_call(body, out_shape=[jax.ShapeDtypeStruct(s, d) for s, d in ou...]
    unnamed x24, local copies, waits for them, and re-layouts: 8.72 us -> 12.2 us
  transfers between devices with their start and end apart: 32 -> 23, of which waited for: 16 -> 12; matrix products, arithmetic and copies ran while one was open for 0% -> 0% of each run, Pallas kernels for 4% -> 10%
where the time goes in v2:
time: 148 us; the launch traced here: 147 us
  waiting for transfers between devices  57.6 us (39%)
  starting transfers between devices  44.7 us (30%)
  Pallas kernels  18.8 us (13%)
  between operations  14.1 us (10%)
  local copies, waits for them, and re-layouts  12.2 us (8%)
    ppermute x21, waiting for transfers between devices, send(): return lax.ppermute(array, 'expert', shifted(dy, dx, dc))  57.6 us
    ppermute x21, starting transfers between devices, send(): return lax.ppermute(array, 'expert', shifted(dy, dx, dc))  37.3 us
    pallas_call x10, Pallas kernels, call(): pl.pallas_call(body, out_shape=[jax.ShapeDtypeStruct(s, d) for s, d in ou...  18.8 us
    unnamed x24, local copies, waits for them, and re-layouts  12.2 us
    all_to_all x1, starting transfers between devices, local(): cut = lax.all_to_all(cut, 'dp', split_axis=0, concat_axis=0, tiled=True)  7.39 us
  transfers between devices with their start and end apart: 23, of which 12 were waited for; matrix products, arithmetic and copies ran while one was open for 0% of the time, Pallas kernels for 10%

profile of v2, /device:TPU:1, one launch (start us, length us, event | category | flops | bytes accessed | tf_op | source)
XLA Modules:
  0.0 147.5 jit_solution(13961125927821680916)
XLA Ops:
  7.2 3.3 %collective-permute-start = (bf16[3,7168,128]{2,1,0:T(8,128)(2,1)}, bf16[3,7168,128]{2,1,0:T(8,128)(2,1)}, u32[]{:S(2)}, u32[]{:S(2)}) collective-permute-start(bf16[3,7168,128]{2,1,0:T(8,128)(2,1)} %bitcast.9), channel_id=1, source_target_pairs={{0,1},{1,0},{2,3},{3,2},{4,5},{5,4},{6,7},{7,6},{8,9},{9,8},{10,11... | collective-permute-start | bytes 16515080 | tf_op jit(solution)/shard_map/ppermute | solution.py:36
  10.5 1.5 %copy-done.2 = bf16[128,7168]{1,0:T(8,128)(2,1)S(1)} copy-done((bf16[128,7168]{1,0:T(8,128)(2,1)S(1)}, bf16[128,7168]{1,0:T(8,128)(2,1)}, u32[]{:S(2)}) %copy-start.2) | copy-done | bytes 1835032
  12.0 1.5 %copy-done.3 = bf16[128,7168]{1,0:T(8,128)(2,1)S(1)} copy-done((bf16[128,7168]{1,0:T(8,128)(2,1)S(1)}, bf16[128,7168]{1,0:T(8,128)(2,1)}, u32[]{:S(2)}) %copy-start.3) | copy-done | bytes 1835032
  15.7 2.2 %collective-permute-start.2 = (bf16[8,14464]{1,0:T(8,128)(2,1)S(1)}, bf16[8,14464]{1,0:T(8,128)(2,1)S(1)}, u32[]{:S(2)}, u32[]{:S(2)}) collective-permute-start(bf16[8,14464]{1,0:T(8,128)(2,1)S(1)} %get-tuple-element.33), channel_id=1, source_target_pairs={{0,16},{1,17},{2,18},{3,19},{4,20},{5,21},{6,22},{7,23},{8,24},{9,... | collective-permute-start | bytes 694280 | tf_op jit(solution)/shard_map/ppermute | solution.py:36
  18.9 5.6 %collective-permute-done.1.refs_1_ = bf16[8,14464]{1,0:T(8,128)(2,1)S(1)} collective-permute-done((bf16[8,14464]{1,0:T(8,128)(2,1)S(1)}, bf16[8,14464]{1,0:T(8,128)(2,1)S(1)}, u32[]{:S(2)}, u32[]{:S(2)}) %collective-permute-start.1) | collective-permute-done | bytes 231456 | tf_op jit(solution)/shard_map/ppermute | solution.py:36
  24.6 4.1 %collective-permute-done.2.refs_2_ = bf16[8,14464]{1,0:T(8,128)(2,1)S(1)} collective-permute-done((bf16[8,14464]{1,0:T(8,128)(2,1)S(1)}, bf16[8,14464]{1,0:T(8,128)(2,1)S(1)}, u32[]{:S(2)}, u32[]{:S(2)}) %collective-permute-start.2) | collective-permute-done | bytes 231456 | tf_op jit(solution)/shard_map/ppermute | solution.py:36
  30.0 2.3 %collective-permute-start.7 = (bf16[16,14464]{1,0:T(8,128)(2,1)S(1)}, bf16[16,14464]{1,0:T(8,128)(2,1)S(1)}, u32[]{:S(2)}, u32[]{:S(2)}) collective-permute-start(bf16[16,14464]{1,0:T(8,128)(2,1)S(1)} %get-tuple-element.36.refs_1_.bottom_ref), channel_id=1, source_target_pairs={{0,6},{1,7},{2,0},{3,1},{4,2},{5,3},{6,4},{7,5},{8,14},{9,15},{10,... | collective-permute-start | bytes 1388552 | tf_op jit(solution)/shard_map/ppermute | solution.py:36
  33.2 7.4 %all-to-all-start = ((bf16[8,64,896]{2,1,0:T(8,128)(2,1)}), bf16[8,64,896]{2,1,0:T(8,128)(2,1)S(1)}, u32[]{:S(2)}, u32[]{:S(2)}) async-start(bf16[8,64,896]{2,1,0:T(8,128)(2,1)} %bitcast.4), calls=%async_computation | async-start | bytes 1835008 | tf_op jit(solution)/shard_map/all_to_all | solution.py:263
  40.8 2.7 %collective-permute-start.6 = (bf16[16,14464]{1,0:T(8,128)(2,1)S(1)}, bf16[16,14464]{1,0:T(8,128)(2,1)S(1)}, u32[]{:S(2)}, u32[]{:S(2)}) collective-permute-start(bf16[16,14464]{1,0:T(8,128)(2,1)S(1)} %get-tuple-element.35.refs_0_.top_ref), channel_id=1, source_target_pairs={{0,6},{1,7},{2,0},{3,1},{4,2},{5,3},{6,4},{7,5},{8,14},{9,15},{10,... | collective-permute-start | bytes 1388552 | tf_op jit(solution)/shard_map/ppermute | solution.py:36
  43.4 2.7 %collective-permute-start.9 = (bf16[16,14464]{1,0:T(8,128)(2,1)S(1)}, bf16[16,14464]{1,0:T(8,128)(2,1)S(1)}, u32[]{:S(2)}, u32[]{:S(2)}) collective-permute-start(bf16[16,14464]{1,0:T(8,128)(2,1)S(1)} %collective-permute-done.7.refs_5_), channel_id=1, source_target_pairs={{0,6},{1,7},{2,0},{3,1},{4,2},{5,3},{6,4},{7,5},{8,14},{9,15},{10,... | collective-permute-start | bytes 1388552 | tf_op jit(solution)/shard_map/ppermute | solution.py:36
  46.1 6.3 %collective-permute-done.5.refs_3_ = bf16[16,14464]{1,0:T(8,128)(2,1)S(1)} collective-permute-done((bf16[16,14464]{1,0:T(8,128)(2,1)S(1)}, bf16[16,14464]{1,0:T(8,128)(2,1)S(1)}, u32[]{:S(2)}, u32[]{:S(2)}) %collective-permute-start.5) | collective-permute-done | bytes 462880 | tf_op jit(solution)/shard_map/ppermute | solution.py:36
  52.4 9.9 %collective-permute-done.8.refs_6_ = bf16[16,14464]{1,0:T(8,128)(2,1)S(1)} collective-permute-done((bf16[16,14464]{1,0:T(8,128)(2,1)S(1)}, bf16[16,14464]{1,0:T(8,128)(2,1)S(1)}, u32[]{:S(2)}, u32[]{:S(2)}) %collective-permute-start.8) | collective-permute-done | bytes 462880 | tf_op jit(solution)/shard_map/ppermute | solution.py:36
  62.3 2.6 %copy-done = bf16[7168,3,128]{2,0,1:T(8,128)(2,1)S(1)} copy-done((bf16[7168,3,128]{2,0,1:T(8,128)(2,1)S(1)}, bf16[7168,3,128]{2,0,1:T(8,128)(2,1)}, u32[]{:S(2)}) %copy-start) | copy-done | bytes 5505048
  64.9 5.0 %shard_map.78 = (bf16[128,768]{1,0:T(8,128)(2,1)}, bf16[128,128]{1,0:T(8,128)(2,1)S(1)}) custom-call(bf16[16,14464]{1,0:T(8,128)(2,1)S(1)} %get-tuple-element.35.refs_0_.top_ref, bf16[16,14464]{1,0:T(8,128)(2,1)S(1)} %get-tuple-element.36.refs_1_.bottom_ref, bf16[16,14464]{1,0:T(8,128)(2,1)S(1)} %collective-permute-done.4.refs_2_, ...), custom_call_target="tpu_custom_call" | custom-call | flops 1409286144 | bytes 14942208 | tf_op jit(solution)/shard_map/pallas_call | solution.py:48
  70.0 2.7 %collective-permute-start.11 = (bf16[512,896]{1,0:T(8,128)(2,1)S(1)}, bf16[512,896]{1,0:T(8,128)(2,1)S(1)}, u32[]{:S(2)}, u32[]{:S(2)}) collective-permute-start(bf16[512,896]{1,0:T(8,128)(2,1)S(1)} %bitcast.13), channel_id=1, source_target_pairs={{0,6},{1,7},{2,0},{3,1},{4,2},{5,3},{6,4},{7,5},{8,14},{9,15},{10,... | collective-permute-start | bytes 2752520 | tf_op jit(solution)/shard_map/ppermute | solution.py:36
  72.7 2.6 %copy-done.1 = bf16[7168,3,128]{2,0,1:T(8,128)(2,1)S(1)} copy-done((bf16[7168,3,128]{2,0,1:T(8,128)(2,1)S(1)}, bf16[7168,3,128]{2,0,1:T(8,128)(2,1)}, u32[]{:S(2)}) %copy-start.1) | copy-done | bytes 5505048
  75.3 5.0 %shard_map.79 = (bf16[32,7296]{1,0:T(8,128)(2,1)S(1)}, bf16[32,7296]{1,0:T(8,128)(2,1)S(1)}, bf16[32,7296]{1,0:T(8,128)(2,1)S(1)}, bf16[32,7296]{1,0:T(8,128)(2,1)S(1)}) custom-call(bf16[3,7168,128]{2,1,0:T(8,128)(2,1)S(1)} %bitcast.11, bf16[3,7168,128]{2,1,0:T(8,128)(2,1)} %collective-permute-done.refs_9_.refs_1_, ...), custom_call_target="tpu_custom_call" | custom-call | flops 939524096 | bytes 13107200 | tf_op jit(solution)/shard_map/pallas_call | solution.py:48
  80.3 10.2 %collective-permute-done.10.left_ref.refs_1_ = bf16[512,896]{1,0:T(8,128)(2,1)S(1)} collective-permute-done((bf16[512,896]{1,0:T(8,128)(2,1)S(1)}, bf16[512,896]{1,0:T(8,128)(2,1)S(1)}, u32[]{:S(2)}, u32[]{:S(2)}) %collective-permute-start.10) | collective-permute-done | bytes 917536 | tf_op jit(solution)/shard_map/ppermute | solution.py:36
  90.5 2.4 %collective-permute-start.12 = (bf16[32,7296]{1,0:T(8,128)(2,1)S(1)}, bf16[32,7296]{1,0:T(8,128)(2,1)S(1)}, u32[]{:S(2)}, u32[]{:S(2)}) collective-permute-start(bf16[32,7296]{1,0:T(8,128)(2,1)S(1)} %get-tuple-element.43), channel_id=1, source_target_pairs={{0,6},{1,7},{2,0},{3,1},{4,2},{5,3},{6,4},{7,5},{8,14},{9,15},{10,... | collective-permute-start | bytes 1400840 | tf_op jit(solution)/shard_map/ppermute | solution.py:36
  92.9 1.2 collective-permute-start.14
  94.1 5.5 %collective-permute-done.12.b_ref = bf16[32,7296]{1,0:T(8,128)(2,1)S(1)} collective-permute-done((bf16[32,7296]{1,0:T(8,128)(2,1)S(1)}, bf16[32,7296]{1,0:T(8,128)(2,1)S(1)}, u32[]{:S(2)}, u32[]{:S(2)}) %collective-permute-start.12) | collective-permute-done | bytes 466976 | tf_op jit(solution)/shard_map/ppermute | solution.py:36
  99.5 6.0 %collective-permute-done.13.c_ref = bf16[32,7296]{1,0:T(8,128)(2,1)S(1)} collective-permute-done((bf16[32,7296]{1,0:T(8,128)(2,1)S(1)}, bf16[32,7296]{1,0:T(8,128)(2,1)S(1)}, u32[]{:S(2)}, u32[]{:S(2)}) %collective-permute-start.13) | collective-permute-done | bytes 466976 | tf_op jit(solution)/shard_map/ppermute | solution.py:36
  105.5 4.4 %collective-permute-done.14.d_ref = bf16[32,7296]{1,0:T(8,128)(2,1)S(1)} collective-permute-done((bf16[32,7296]{1,0:T(8,128)(2,1)S(1)}, bf16[32,7296]{1,0:T(8,128)(2,1)S(1)}, u32[]{:S(2)}, u32[]{:S(2)}) %collective-permute-start.14) | collective-permute-done | bytes 466976 | tf_op jit(solution)/shard_map/ppermute | solution.py:36
  111.1 1.3 collective-permute-start.18
  112.4 1.4 collective-permute-start.19
  113.8 3.8 %collective-permute-start.15 = (bf16[8,7296]{1,0:T(8,128)(2,1)S(1)}, bf16[8,7296]{1,0:T(8,128)(2,1)S(1)}, u32[]{:S(2)}, u32[]{:S(2)}) collective-permute-start(bf16[8,7296]{1,0:T(8,128)(2,1)S(1)} %get-tuple-element.47), channel_id=1, source_target_pairs={{0,24},{1,25},{2,26},{3,27},{4,28},{5,29},{6,30},{7,31},{8,0},{9,1... | collective-permute-start | bytes 350216 | tf_op jit(solution)/shard_map/ppermute | solution.py:36
  118.2 2.4 %collective-permute-done.15.b1 = bf16[8,7296]{1,0:T(8,128)(2,1)S(1)} collective-permute-done((bf16[8,7296]{1,0:T(8,128)(2,1)S(1)}, bf16[8,7296]{1,0:T(8,128)(2,1)S(1)}, u32[]{:S(2)}, u32[]{:S(2)}) %collective-permute-start.15) | collective-permute-done | bytes 116768 | tf_op jit(solution)/shard_map/ppermute | solution.py:36
  120.6 2.3 %collective-permute-done.16.b2 = bf16[8,7296]{1,0:T(8,128)(2,1)S(1)} collective-permute-done((bf16[8,7296]{1,0:T(8,128)(2,1)S(1)}, bf16[8,7296]{1,0:T(8,128)(2,1)S(1)}, u32[]{:S(2)}, u32[]{:S(2)}) %collective-permute-start.16) | collective-permute-done | bytes 116768 | tf_op jit(solution)/shard_map/ppermute | solution.py:36
  124.4 1.4 copy-done.4
  125.8 2.7 %shard_map.84 = (f32[3,896,128]{2,1,0:T(8,128)S(1)}, bf16[3,896,128]{2,1,0:T(8,128)(2,1)S(1)}) custom-call(bf16[512,896]{1,0:T(8,128)(2,1)S(1)} %bitcast.14, bf16[512,896]{1,0:T(8,128)(2,1)S(1)} %collective-permute-done.10.left_ref.refs_1_, bf16[512,896]{1,0:T(8,128)(2,1)S(1)} %collective-permute-done.11.right_ref.refs_2_, ...), custom_call_target="tpu_custom_call" | custom-call | flops 1409286144 | bytes 7307264 | tf_op jit(solution)/shard_map/pallas_call | solution.py:48
  128.6 9.0 %collective-permute-start.20 = (bf16[3,896,128]{2,1,0:T(8,128)(2,1)S(1)}, bf16[3,896,128]{2,1,0:T(8,128)(2,1)S(1)}, u32[]{:S(2)}, u32[]{:S(2)}) collective-permute-start(bf16[3,896,128]{2,1,0:T(8,128)(2,1)S(1)} %get-tuple-element.58), channel_id=1, source_target_pairs={{0,1},{1,0},{2,3},{3,2},{4,5},{5,4},{6,7},{7,6},{8,9},{9,8},{10,11... | collective-permute-start | bytes 2064392 | tf_op jit(solution)/shard_map/ppermute | solution.py:36
  137.6 2.1 %shard_map.82 = (bf16[128,7168]{1,0:T(8,128)(2,1)}, f32[8,128]{1,0:T(8,128)}) custom-call(s32[1]{0:T(128)} %bitcast.y_ref, s32[8,128]{1,0:T(8,128)S(1)} %bitcast.17, bf16[8,7296]{1,0:T(8,128)(2,1)S(1)} %get-tuple-element.46.b0._, bf16[8,7296]{1,0:T(8,128)(2,1)S(1)} %collective-permute-done.15.b1, bf16[8,7296]{1,0:T(8,128)(2,1)S(1)} %copy-done.6, ...), custom_call_target="tpu_custom_call" | custom-call | bytes 2310148 | tf_op jit(solution)/shard_map/pallas_call | solution.py:48
  (49 shorter events, 10.1 us)
Async XLA Ops:
  7.2 55.2 %collective-permute-start = (bf16[3,7168,128]{2,1,0:T(8,128)(2,1)}, bf16[3,7168,128]{2,1,0:T(8,128)(2,1)}, u32[]{:S(2)}, u32[]{:S(2)}) collective-permute-start(bf16[3,7168,128]{2,1,0:T(8,128)(2,1)} %bitcast.9), channel_id=1, source_target_pairs={{0,1},{1,0},{2,3},{3,2},{4,5},{5,4},{6,7},{7,6},{8,9},{9,8},{10,11... | collective-permute-start | bytes 16515080 | tf_op jit(solution)/shard_map/ppermute | solution.py:36
  10.5 1.5 %copy-start.2 = (bf16[128,7168]{1,0:T(8,128)(2,1)S(1)}, bf16[128,7168]{1,0:T(8,128)(2,1)}, u32[]{:S(2)}) copy-start(bf16[128,7168]{1,0:T(8,128)(2,1)} %tok_ref.1) | copy-start | bytes 5505028
  12.0 1.5 %copy-start.3 = (bf16[128,7168]{1,0:T(8,128)(2,1)S(1)}, bf16[128,7168]{1,0:T(8,128)(2,1)}, u32[]{:S(2)}) copy-start(bf16[128,7168]{1,0:T(8,128)(2,1)} %cot_ref.1) | copy-start | bytes 5505028
  13.5 0.7 copy-start.9
  15.6 9.0 %collective-permute-start.1 = (bf16[8,14464]{1,0:T(8,128)(2,1)S(1)}, bf16[8,14464]{1,0:T(8,128)(2,1)S(1)}, u32[]{:S(2)}, u32[]{:S(2)}) collective-permute-start(bf16[8,14464]{1,0:T(8,128)(2,1)S(1)} %get-tuple-element.32), channel_id=1, source_target_pairs={{0,8},{1,9},{2,10},{3,11},{4,12},{5,13},{6,14},{7,15},{8,16},{9,17... | collective-permute-start | bytes 694280 | tf_op jit(solution)/shard_map/ppermute | solution.py:36
  15.7 13.0 %collective-permute-start.2 = (bf16[8,14464]{1,0:T(8,128)(2,1)S(1)}, bf16[8,14464]{1,0:T(8,128)(2,1)S(1)}, u32[]{:S(2)}, u32[]{:S(2)}) collective-permute-start(bf16[8,14464]{1,0:T(8,128)(2,1)S(1)} %get-tuple-element.33), channel_id=1, source_target_pairs={{0,16},{1,17},{2,18},{3,19},{4,20},{5,21},{6,22},{7,23},{8,24},{9,... | collective-permute-start | bytes 694280 | tf_op jit(solution)/shard_map/ppermute | solution.py:36
  17.9 11.5 %collective-permute-start.3 = (bf16[8,14464]{1,0:T(8,128)(2,1)S(1)}, bf16[8,14464]{1,0:T(8,128)(2,1)S(1)}, u32[]{:S(2)}, u32[]{:S(2)}) collective-permute-start(bf16[8,14464]{1,0:T(8,128)(2,1)S(1)} %get-tuple-element.34), channel_id=1, source_target_pairs={{0,24},{1,25},{2,26},{3,27},{4,28},{5,29},{6,30},{7,31},{8,0},{9,1... | collective-permute-start | bytes 694280 | tf_op jit(solution)/shard_map/ppermute | solution.py:36
  29.5 13.9 %collective-permute-start.4 = (bf16[16,14464]{1,0:T(8,128)(2,1)S(1)}, bf16[16,14464]{1,0:T(8,128)(2,1)S(1)}, u32[]{:S(2)}, u32[]{:S(2)}) collective-permute-start(bf16[16,14464]{1,0:T(8,128)(2,1)S(1)} %get-tuple-element.35.refs_0_.top_ref), channel_id=1, source_target_pairs={{0,2},{1,3},{2,4},{3,5},{4,6},{5,7},{6,0},{7,1},{8,10},{9,11},{10,... | collective-permute-start | bytes 1388552 | tf_op jit(solution)/shard_map/ppermute | solution.py:36
  30.0 13.5 %collective-permute-start.7 = (bf16[16,14464]{1,0:T(8,128)(2,1)S(1)}, bf16[16,14464]{1,0:T(8,128)(2,1)S(1)}, u32[]{:S(2)}, u32[]{:S(2)}) collective-permute-start(bf16[16,14464]{1,0:T(8,128)(2,1)S(1)} %get-tuple-element.36.refs_1_.bottom_ref), channel_id=1, source_target_pairs={{0,6},{1,7},{2,0},{3,1},{4,2},{5,3},{6,4},{7,5},{8,14},{9,15},{10,... | collective-permute-start | bytes 1388552 | tf_op jit(solution)/shard_map/ppermute | solution.py:36
  33.2 36.7 %all-to-all-start = ((bf16[8,64,896]{2,1,0:T(8,128)(2,1)}), bf16[8,64,896]{2,1,0:T(8,128)(2,1)S(1)}, u32[]{:S(2)}, u32[]{:S(2)}) async-start(bf16[8,64,896]{2,1,0:T(8,128)(2,1)} %bitcast.4), calls=%async_computation | async-start | bytes 1835008 | tf_op jit(solution)/shard_map/all_to_all | solution.py:263
  40.6 83.8 %all-gather.3.cloned.1.call-start = ((), (), s32[]{:S(2)}) async-start(), calls=%async_computation.1 | async-start | bytes 1769472 | tf_op jit(solution)/shard_map/all_gather | solution.py:281
  40.7 11.7 %collective-permute-start.5 = (bf16[16,14464]{1,0:T(8,128)(2,1)S(1)}, bf16[16,14464]{1,0:T(8,128)(2,1)S(1)}, u32[]{:S(2)}, u32[]{:S(2)}) collective-permute-start(bf16[16,14464]{1,0:T(8,128)(2,1)S(1)} %get-tuple-element.36.refs_1_.bottom_ref), channel_id=1, source_target_pairs={{0,2},{1,3},{2,4},{3,5},{4,6},{5,7},{6,0},{7,1},{8,10},{9,11},{10,... | collective-permute-start | bytes 1388552 | tf_op jit(solution)/shard_map/ppermute | solution.py:36
  40.8 11.6 %collective-permute-start.6 = (bf16[16,14464]{1,0:T(8,128)(2,1)S(1)}, bf16[16,14464]{1,0:T(8,128)(2,1)S(1)}, u32[]{:S(2)}, u32[]{:S(2)}) collective-permute-start(bf16[16,14464]{1,0:T(8,128)(2,1)S(1)} %get-tuple-element.35.refs_0_.top_ref), channel_id=1, source_target_pairs={{0,6},{1,7},{2,0},{3,1},{4,2},{5,3},{6,4},{7,5},{8,14},{9,15},{10,... | collective-permute-start | bytes 1388552 | tf_op jit(solution)/shard_map/ppermute | solution.py:36
  43.4 18.9 %collective-permute-start.8 = (bf16[16,14464]{1,0:T(8,128)(2,1)S(1)}, bf16[16,14464]{1,0:T(8,128)(2,1)S(1)}, u32[]{:S(2)}, u32[]{:S(2)}) collective-permute-start(bf16[16,14464]{1,0:T(8,128)(2,1)S(1)} %collective-permute-done.4.refs_2_), channel_id=1, source_target_pairs={{0,2},{1,3},{2,4},{3,5},{4,6},{5,7},{6,0},{7,1},{8,10},{9,11},{10,... | collective-permute-start | bytes 1388552 | tf_op jit(solution)/shard_map/ppermute | solution.py:36
  43.4 18.9 %collective-permute-start.9 = (bf16[16,14464]{1,0:T(8,128)(2,1)S(1)}, bf16[16,14464]{1,0:T(8,128)(2,1)S(1)}, u32[]{:S(2)}, u32[]{:S(2)}) collective-permute-start(bf16[16,14464]{1,0:T(8,128)(2,1)S(1)} %collective-permute-done.7.refs_5_), channel_id=1, source_target_pairs={{0,6},{1,7},{2,0},{3,1},{4,2},{5,3},{6,4},{7,5},{8,14},{9,15},{10,... | collective-permute-start | bytes 1388552 | tf_op jit(solution)/shard_map/ppermute | solution.py:36
  62.3 2.6 %copy-start = (bf16[7168,3,128]{2,0,1:T(8,128)(2,1)S(1)}, bf16[7168,3,128]{2,0,1:T(8,128)(2,1)}, u32[]{:S(2)}) copy-start(bf16[7168,3,128]{2,0,1:T(8,128)(2,1)} %param.9) | copy-start | bytes 16515076
  69.9 20.6 %collective-permute-start.10 = (bf16[512,896]{1,0:T(8,128)(2,1)S(1)}, bf16[512,896]{1,0:T(8,128)(2,1)S(1)}, u32[]{:S(2)}, u32[]{:S(2)}) collective-permute-start(bf16[512,896]{1,0:T(8,128)(2,1)S(1)} %bitcast.12), channel_id=1, source_target_pairs={{0,2},{1,3},{2,4},{3,5},{4,6},{5,7},{6,0},{7,1},{8,10},{9,11},{10,... | collective-permute-start | bytes 2752520 | tf_op jit(solution)/shard_map/ppermute | solution.py:36
  70.0 20.5 %collective-permute-start.11 = (bf16[512,896]{1,0:T(8,128)(2,1)S(1)}, bf16[512,896]{1,0:T(8,128)(2,1)S(1)}, u32[]{:S(2)}, u32[]{:S(2)}) collective-permute-start(bf16[512,896]{1,0:T(8,128)(2,1)S(1)} %bitcast.13), channel_id=1, source_target_pairs={{0,6},{1,7},{2,0},{3,1},{4,2},{5,3},{6,4},{7,5},{8,14},{9,15},{10,... | collective-permute-start | bytes 2752520 | tf_op jit(solution)/shard_map/ppermute | solution.py:36
  72.7 2.6 %copy-start.1 = (bf16[7168,3,128]{2,0,1:T(8,128)(2,1)S(1)}, bf16[7168,3,128]{2,0,1:T(8,128)(2,1)}, u32[]{:S(2)}) copy-start(bf16[7168,3,128]{2,0,1:T(8,128)(2,1)} %param.9) | copy-start | bytes 16515076
  90.5 9.0 %collective-permute-start.12 = (bf16[32,7296]{1,0:T(8,128)(2,1)S(1)}, bf16[32,7296]{1,0:T(8,128)(2,1)S(1)}, u32[]{:S(2)}, u32[]{:S(2)}) collective-permute-start(bf16[32,7296]{1,0:T(8,128)(2,1)S(1)} %get-tuple-element.43), channel_id=1, source_target_pairs={{0,6},{1,7},{2,0},{3,1},{4,2},{5,3},{6,4},{7,5},{8,14},{9,15},{10,... | collective-permute-start | bytes 1400840 | tf_op jit(solution)/shard_map/ppermute | solution.py:36
  92.9 12.6 %collective-permute-start.13 = (bf16[32,7296]{1,0:T(8,128)(2,1)S(1)}, bf16[32,7296]{1,0:T(8,128)(2,1)S(1)}, u32[]{:S(2)}, u32[]{:S(2)}) collective-permute-start(bf16[32,7296]{1,0:T(8,128)(2,1)S(1)} %get-tuple-element.44), channel_id=1, source_target_pairs={{0,2},{1,3},{2,4},{3,5},{4,6},{5,7},{6,0},{7,1},{8,10},{9,11},{10,... | collective-permute-start | bytes 1400840 | tf_op jit(solution)/shard_map/ppermute | solution.py:36
  92.9 17.0 %collective-permute-start.14 = (bf16[32,7296]{1,0:T(8,128)(2,1)S(1)}, bf16[32,7296]{1,0:T(8,128)(2,1)S(1)}, u32[]{:S(2)}, u32[]{:S(2)}) collective-permute-start(bf16[32,7296]{1,0:T(8,128)(2,1)S(1)} %get-tuple-element.45), channel_id=1, source_target_pairs={{0,4},{1,5},{2,6},{3,7},{4,0},{5,1},{6,2},{7,3},{8,12},{9,13},{10,... | collective-permute-start | bytes 1400840 | tf_op jit(solution)/shard_map/ppermute | solution.py:36
  111.1 13.3 %collective-permute-start.18 = (bf16[256,896]{1,0:T(8,128)(2,1)}, bf16[256,896]{1,0:T(8,128)(2,1)S(1)}, u32[]{:S(2)}, u32[]{:S(2)}) collective-permute-start(bf16[256,896]{1,0:T(8,128)(2,1)} %get-tuple-element.54), channel_id=1, source_target_pairs={{0,2},{1,3},{2,4},{3,5},{4,6},{5,7},{6,0},{7,1},{8,10},{9,11},{10,... | collective-permute-start | bytes 1376264 | tf_op jit(solution)/shard_map/ppermute | solution.py:36
  112.4 12.0 %collective-permute-start.19 = (bf16[256,896]{1,0:T(8,128)(2,1)}, bf16[256,896]{1,0:T(8,128)(2,1)}, u32[]{:S(2)}, u32[]{:S(2)}) collective-permute-start(bf16[256,896]{1,0:T(8,128)(2,1)} %get-tuple-element.55), channel_id=1, source_target_pairs={{0,6},{1,7},{2,0},{3,1},{4,2},{5,3},{6,4},{7,5},{8,14},{9,15},{10,... | collective-permute-start | bytes 1376264 | tf_op jit(solution)/shard_map/ppermute | solution.py:36
  113.8 6.8 %collective-permute-start.15 = (bf16[8,7296]{1,0:T(8,128)(2,1)S(1)}, bf16[8,7296]{1,0:T(8,128)(2,1)S(1)}, u32[]{:S(2)}, u32[]{:S(2)}) collective-permute-start(bf16[8,7296]{1,0:T(8,128)(2,1)S(1)} %get-tuple-element.47), channel_id=1, source_target_pairs={{0,24},{1,25},{2,26},{3,27},{4,28},{5,29},{6,30},{7,31},{8,0},{9,1... | collective-permute-start | bytes 350216 | tf_op jit(solution)/shard_map/ppermute | solution.py:36
  117.6 5.3 %collective-permute-start.16 = (bf16[8,7296]{1,0:T(8,128)(2,1)S(1)}, bf16[8,7296]{1,0:T(8,128)(2,1)S(1)}, u32[]{:S(2)}, u32[]{:S(2)}) collective-permute-start(bf16[8,7296]{1,0:T(8,128)(2,1)S(1)} %get-tuple-element.48), channel_id=1, source_target_pairs={{0,16},{1,17},{2,18},{3,19},{4,20},{5,21},{6,22},{7,23},{8,24},{9,... | collective-permute-start | bytes 350216 | tf_op jit(solution)/shard_map/ppermute | solution.py:36
  117.6 6.1 %collective-permute-start.17 = (bf16[8,7296]{1,0:T(8,128)(2,1)S(1)}, bf16[8,7296]{1,0:T(8,128)(2,1)S(1)}, u32[]{:S(2)}, u32[]{:S(2)}) collective-permute-start(bf16[8,7296]{1,0:T(8,128)(2,1)S(1)} %get-tuple-element.49), channel_id=1, source_target_pairs={{0,8},{1,9},{2,10},{3,11},{4,12},{5,13},{6,14},{7,15},{8,16},{9,17... | collective-permute-start | bytes 350216 | tf_op jit(solution)/shard_map/ppermute | solution.py:36
  124.4 1.4 copy-start.4
  125.8 11.8 %copy-start.6 = (bf16[8,7296]{1,0:T(8,128)(2,1)S(1)}, bf16[8,7296]{1,0:T(8,128)(2,1)}, u32[]{:S(2)}) copy-start(bf16[8,7296]{1,0:T(8,128)(2,1)} %copy-done.5) | copy-start | bytes 350212
  125.8 11.8 %copy-start.8 = (bf16[8,7296]{1,0:T(8,128)(2,1)S(1)}, bf16[8,7296]{1,0:T(8,128)(2,1)}, u32[]{:S(2)}) copy-start(bf16[8,7296]{1,0:T(8,128)(2,1)} %copy-done.7) | copy-start | bytes 350212
  125.8 11.8 %copy-start.10 = (s32[128,8]{0,1:T(8,128)S(1)}, s32[128,8]{0,1:T(8,128)}, u32[]{:S(2)}) copy-start(s32[128,8]{0,1:T(8,128)} %param.7) | copy-start | bytes 12292
  128.6 11.1 %collective-permute-start.20 = (bf16[3,896,128]{2,1,0:T(8,128)(2,1)S(1)}, bf16[3,896,128]{2,1,0:T(8,128)(2,1)S(1)}, u32[]{:S(2)}, u32[]{:S(2)}) collective-permute-start(bf16[3,896,128]{2,1,0:T(8,128)(2,1)S(1)} %get-tuple-element.58), channel_id=1, source_target_pairs={{0,1},{1,0},{2,3},{3,2},{4,5},{5,4},{6,7},{7,6},{8,9},{9,8},{10,11... | collective-permute-start | bytes 2064392 | tf_op jit(solution)/shard_map/ppermute | solution.py:36
  (3 other events, 2.0 us)
Sparse Core Ops, SparseCore 0:
  70.1 38.3 all-gather.2

commit v3 on v2

--- a/solution.py
+++ b/solution.py
@@ -162,10 +162,14 @@
         grad = lax.dot_general(
             d_both, side_by_side(w_refs, (0, 1), cols), across, preferred_element_type=F32
         ).astype(BF16)
-        for k, out in enumerate(outs):
-            out[:, cols] = grad[k * SLOTS : (k + 1) * SLOTS]
-    for k, out in enumerate(outs):
-        out[:, width:] = sw_ref[k * SLOTS : (k + 1) * SLOTS, :]
+        row = 0
+        for out in outs:
+            out[:, cols] = grad[row : row + out.shape[0]]
+            row += out.shape[0]
+    row = 0
+    for out in outs:
+        out[:, width:] = sw_ref[row : row + out.shape[0], :]
+        row += out.shape[0]
 
 
 def weight_grads(n_cuts, *refs):
@@ -203,13 +207,21 @@
     out[...] = (mine_ref[...] + got_ref[...].astype(F32)).astype(BF16)
 
 
-def add_all(a_ref, b_ref, c_ref, d_ref, *outs):
+def add_far(left_ref, right_ref, top_ref, bottom_ref, left_out, right_out):
+    half = top_ref.shape[0]
+    left_out[:half, :] = (left_ref[:half, :].astype(F32) + top_ref[...].astype(F32)).astype(BF16)
+    left_out[half:, :] = left_ref[half:, :]
+    right_out[:half, :] = right_ref[:half, :]
+    right_out[half:, :] = (
+        right_ref[half:, :].astype(F32) + bottom_ref[...].astype(F32)
+    ).astype(BF16)
+
+
+def add_all(a_ref, b_ref, c_ref, *outs):
     for k, out in enumerate(outs):
         rows = slice(k * MOST, (k + 1) * MOST)
-        total = (a_ref[rows, :].astype(F32) + b_ref[rows, :].astype(F32)) + (
-            c_ref[rows, :].astype(F32) + d_ref[rows, :].astype(F32)
-        )
-        out[...] = total.astype(BF16)
+        total = a_ref[rows, :].astype(F32) + b_ref[rows, :].astype(F32)
+        out[...] = (total + c_ref[rows, :].astype(F32)).astype(BF16)
 
 
 def two_halves(left_ref, right_ref, _, *outs):
@@ -271,18 +283,26 @@
         [*blocks, *w_all],
         flops=3 * work,
     )
-    keep, to_left, to_right, to_far = call(
-        shard_grads, [((SLOTS, wide), BF16)] * NX, [*w_all, g, sw], flops=2 * work
+    keep, to_left, to_right, far_up, far_down = call(
+        shard_grads,
+        [((SLOTS, wide), BF16)] * 3 + [((half, wide), BF16)] * 2,
+        [*w_all, g, sw],
+        flops=2 * work,
+    )
+    to_left, to_right = call(
+        add_far,
+        [((SLOTS, wide), BF16)] * 2,
+        [to_left, to_right, send(far_up, dx=-1), send(far_down, dx=1)],
     )
     cut_left, cut_right = send(cut, dx=1), send(cut, dx=-1)
-    to_left, to_right, to_far, cut_left, cut_right = lax.optimization_barrier(
-        (to_left, to_right, to_far, cut_left, cut_right)
+    to_left, to_right, cut_left, cut_right = lax.optimization_barrier(
+        (to_left, to_right, cut_left, cut_right)
     )
     g_all = lax.all_gather(g, "dp", axis=0)
     back = call(
         add_all,
         [((MOST, wide), BF16)] * N_WIN,
-        [keep, send(to_left, dx=-1), send(to_right, dx=1), send(to_far, dx=2)],
+        [keep, send(to_left, dx=-1), send(to_right, dx=1)],
     )
     home = [back[0]] + [send(back[k], dy=-k) for k in range(1, N_WIN)]
     top, bottom = call(

time: 148 us -> 143 us (0.966)
  starting transfers between devices: 44.7 us -> 41.7 us
  waiting for transfers between devices: 57.6 us -> 55.2 us
    ppermute x21 -> x22, starting transfers between devices: 37.3 us -> 34.2 us  [send(): return lax.ppermute(array, 'expert', shifted(dy, dx, dc))]
    ppermute x21 -> x22, waiting for transfers between devices: 57.6 us -> 55.2 us  [send(): return lax.ppermute(array, 'expert', shifted(dy, dx, dc))]
    pallas_call x10 -> x11, Pallas kernels: 18.8 us -> 18.9 us  [call(): pl.pallas_call(body, out_shape=[jax.ShapeDtypeStruct(s, d) for s, d in ou...]
  transfers between devices with their start and end apart: 23 -> 24, of which waited for: 12 -> 12; matrix products, arithmetic and copies ran while one was open for 0% -> 0% of each run, Pallas kernels for 10% -> 11%
where the time goes in v3:
time: 143 us; the launch traced here: 142 us
  waiting for transfers between devices  55.2 us (39%)
  starting transfers between devices  41.7 us (29%)
  Pallas kernels  18.9 us (13%)
  between operations  14.2 us (10%)
  local copies, waits for them, and re-layouts  12.2 us (9%)
    ppermute x22, waiting for transfers between devices, send(): return lax.ppermute(array, 'expert', shifted(dy, dx, dc))  55.2 us
    ppermute x22, starting transfers between devices, send(): return lax.ppermute(array, 'expert', shifted(dy, dx, dc))  34.2 us
    pallas_call x11, Pallas kernels, call(): pl.pallas_call(body, out_shape=[jax.ShapeDtypeStruct(s, d) for s, d in ou...  18.9 us
    unnamed x24, local copies, waits for them, and re-layouts  12.2 us
    all_to_all x1, starting transfers between devices, local(): cut = lax.all_to_all(cut, 'dp', split_axis=0, concat_axis=0, tiled=True)  7.39 us
  transfers between devices with their start and end apart: 24, of which 12 were waited for; matrix products, arithmetic and copies ran while one was open for 0% of the time, Pallas kernels for 11%

profile of v3, /device:TPU:1, one launch (start us, length us, event | category | flops | bytes accessed | tf_op | source)
XLA Modules:
  0.0 142.2 jit_solution(6848417969961950512)
XLA Ops:
  7.2 3.3 %collective-permute-start = (bf16[3,7168,128]{2,1,0:T(8,128)(2,1)}, bf16[3,7168,128]{2,1,0:T(8,128)(2,1)}, u32[]{:S(2)}, u32[]{:S(2)}) collective-permute-start(bf16[3,7168,128]{2,1,0:T(8,128)(2,1)} %bitcast.9), channel_id=1, source_target_pairs={{0,1},{1,0},{2,3},{3,2},{4,5},{5,4},{6,7},{7,6},{8,9},{9,8},{10,11... | collective-permute-start | bytes 16515080 | tf_op jit(solution)/shard_map/ppermute | solution.py:36
  10.5 1.5 %copy-done.2 = bf16[128,7168]{1,0:T(8,128)(2,1)S(1)} copy-done((bf16[128,7168]{1,0:T(8,128)(2,1)S(1)}, bf16[128,7168]{1,0:T(8,128)(2,1)}, u32[]{:S(2)}) %copy-start.2) | copy-done | bytes 1835032
  12.0 1.5 %copy-done.3 = bf16[128,7168]{1,0:T(8,128)(2,1)S(1)} copy-done((bf16[128,7168]{1,0:T(8,128)(2,1)S(1)}, bf16[128,7168]{1,0:T(8,128)(2,1)}, u32[]{:S(2)}) %copy-start.3) | copy-done | bytes 1835032
  15.7 2.2 %collective-permute-start.2 = (bf16[8,14464]{1,0:T(8,128)(2,1)S(1)}, bf16[8,14464]{1,0:T(8,128)(2,1)S(1)}, u32[]{:S(2)}, u32[]{:S(2)}) collective-permute-start(bf16[8,14464]{1,0:T(8,128)(2,1)S(1)} %get-tuple-element.35), channel_id=1, source_target_pairs={{0,16},{1,17},{2,18},{3,19},{4,20},{5,21},{6,22},{7,23},{8,24},{9,... | collective-permute-start | bytes 694280 | tf_op jit(solution)/shard_map/ppermute | solution.py:36
  17.9 1.1 collective-permute-start.3
  18.9 5.6 %collective-permute-done.1.refs_1_ = bf16[8,14464]{1,0:T(8,128)(2,1)S(1)} collective-permute-done((bf16[8,14464]{1,0:T(8,128)(2,1)S(1)}, bf16[8,14464]{1,0:T(8,128)(2,1)S(1)}, u32[]{:S(2)}, u32[]{:S(2)}) %collective-permute-start.1) | collective-permute-done | bytes 231456 | tf_op jit(solution)/shard_map/ppermute | solution.py:36
  24.6 4.1 %collective-permute-done.2.refs_2_ = bf16[8,14464]{1,0:T(8,128)(2,1)S(1)} collective-permute-done((bf16[8,14464]{1,0:T(8,128)(2,1)S(1)}, bf16[8,14464]{1,0:T(8,128)(2,1)S(1)}, u32[]{:S(2)}, u32[]{:S(2)}) %collective-permute-start.2) | collective-permute-done | bytes 231456 | tf_op jit(solution)/shard_map/ppermute | solution.py:36
  30.0 2.3 %collective-permute-start.7 = (bf16[16,14464]{1,0:T(8,128)(2,1)S(1)}, bf16[16,14464]{1,0:T(8,128)(2,1)S(1)}, u32[]{:S(2)}, u32[]{:S(2)}) collective-permute-start(bf16[16,14464]{1,0:T(8,128)(2,1)S(1)} %get-tuple-element.38.refs_1_.bottom_ref), channel_id=1, source_target_pairs={{0,6},{1,7},{2,0},{3,1},{4,2},{5,3},{6,4},{7,5},{8,14},{9,15},{10,... | collective-permute-start | bytes 1388552 | tf_op jit(solution)/shard_map/ppermute | solution.py:36
  33.2 7.4 %all-to-all-start = ((bf16[8,64,896]{2,1,0:T(8,128)(2,1)}), bf16[8,64,896]{2,1,0:T(8,128)(2,1)S(1)}, u32[]{:S(2)}, u32[]{:S(2)}) async-start(bf16[8,64,896]{2,1,0:T(8,128)(2,1)} %bitcast.4), calls=%async_computation | async-start | bytes 1835008 | tf_op jit(solution)/shard_map/all_to_all | solution.py:275
  40.8 2.7 %collective-permute-start.6 = (bf16[16,14464]{1,0:T(8,128)(2,1)S(1)}, bf16[16,14464]{1,0:T(8,128)(2,1)S(1)}, u32[]{:S(2)}, u32[]{:S(2)}) collective-permute-start(bf16[16,14464]{1,0:T(8,128)(2,1)S(1)} %get-tuple-element.37.refs_0_.top_ref), channel_id=1, source_target_pairs={{0,6},{1,7},{2,0},{3,1},{4,2},{5,3},{6,4},{7,5},{8,14},{9,15},{10,... | collective-permute-start | bytes 1388552 | tf_op jit(solution)/shard_map/ppermute | solution.py:36
  43.4 2.7 %collective-permute-start.9 = (bf16[16,14464]{1,0:T(8,128)(2,1)S(1)}, bf16[16,14464]{1,0:T(8,128)(2,1)S(1)}, u32[]{:S(2)}, u32[]{:S(2)}) collective-permute-start(bf16[16,14464]{1,0:T(8,128)(2,1)S(1)} %collective-permute-done.7.refs_5_), channel_id=1, source_target_pairs={{0,6},{1,7},{2,0},{3,1},{4,2},{5,3},{6,4},{7,5},{8,14},{9,15},{10,... | collective-permute-start | bytes 1388552 | tf_op jit(solution)/shard_map/ppermute | solution.py:36
  46.1 6.3 %collective-permute-done.5.refs_3_ = bf16[16,14464]{1,0:T(8,128)(2,1)S(1)} collective-permute-done((bf16[16,14464]{1,0:T(8,128)(2,1)S(1)}, bf16[16,14464]{1,0:T(8,128)(2,1)S(1)}, u32[]{:S(2)}, u32[]{:S(2)}) %collective-permute-start.5) | collective-permute-done | bytes 462880 | tf_op jit(solution)/shard_map/ppermute | solution.py:36
  52.4 9.9 %collective-permute-done.8.refs_6_ = bf16[16,14464]{1,0:T(8,128)(2,1)S(1)} collective-permute-done((bf16[16,14464]{1,0:T(8,128)(2,1)S(1)}, bf16[16,14464]{1,0:T(8,128)(2,1)S(1)}, u32[]{:S(2)}, u32[]{:S(2)}) %collective-permute-start.8) | collective-permute-done | bytes 462880 | tf_op jit(solution)/shard_map/ppermute | solution.py:36
  62.3 2.6 %copy-done = bf16[7168,3,128]{2,0,1:T(8,128)(2,1)S(1)} copy-done((bf16[7168,3,128]{2,0,1:T(8,128)(2,1)S(1)}, bf16[7168,3,128]{2,0,1:T(8,128)(2,1)}, u32[]{:S(2)}) %copy-start) | copy-done | bytes 5505048
  64.9 5.0 %shard_map.78 = (bf16[128,768]{1,0:T(8,128)(2,1)}, bf16[128,128]{1,0:T(8,128)(2,1)S(1)}) custom-call(bf16[16,14464]{1,0:T(8,128)(2,1)S(1)} %get-tuple-element.37.refs_0_.top_ref, bf16[16,14464]{1,0:T(8,128)(2,1)S(1)} %get-tuple-element.38.refs_1_.bottom_ref, bf16[16,14464]{1,0:T(8,128)(2,1)S(1)} %collective-permute-done.4.refs_2_, ...), custom_call_target="tpu_custom_call" | custom-call | flops 1409286144 | bytes 14942208 | tf_op jit(solution)/shard_map/pallas_call | solution.py:48
  70.0 2.7 %collective-permute-start.13 = (bf16[512,896]{1,0:T(8,128)(2,1)S(1)}, bf16[512,896]{1,0:T(8,128)(2,1)S(1)}, u32[]{:S(2)}, u32[]{:S(2)}) collective-permute-start(bf16[512,896]{1,0:T(8,128)(2,1)S(1)} %bitcast.13), channel_id=1, source_target_pairs={{0,6},{1,7},{2,0},{3,1},{4,2},{5,3},{6,4},{7,5},{8,14},{9,15},{10,... | collective-permute-start | bytes 2752520 | tf_op jit(solution)/shard_map/ppermute | solution.py:36
  72.7 2.6 %copy-done.1 = bf16[7168,3,128]{2,0,1:T(8,128)(2,1)S(1)} copy-done((bf16[7168,3,128]{2,0,1:T(8,128)(2,1)S(1)}, bf16[7168,3,128]{2,0,1:T(8,128)(2,1)}, u32[]{:S(2)}) %copy-start.1) | copy-done | bytes 5505048
  75.3 5.0 %shard_map.79 = (bf16[32,7296]{1,0:T(8,128)(2,1)S(1)}, bf16[32,7296]{1,0:T(8,128)(2,1)S(1)}, bf16[32,7296]{1,0:T(8,128)(2,1)S(1)}, bf16[16,7296]{1,0:T(8,128)(2,1)S(1)}, bf16[16,7296]{1,0:T(8,128)(2,1)S(1)}) custom-call(bf16[3,7168,128]{2,1,0:T(8,128)(2,1)S(1)} %bitcast.11, bf16[3,7168,128]{2,1,0:T(8,128)(2,1)} %collective-permute-done.refs_9_.refs_1_, ...), custom_call_target="tpu_custom_call" | custom-call | flops 939524096 | bytes 13107200 | tf_op jit(solution)/shard_map/pallas_call | solution.py:48
  80.3 1.3 collective-permute-start.10
  81.9 12.7 %collective-permute-done.10.top_ref = bf16[16,7296]{1,0:T(8,128)(2,1)S(1)} collective-permute-done((bf16[16,7296]{1,0:T(8,128)(2,1)S(1)}, bf16[16,7296]{1,0:T(8,128)(2,1)S(1)}, u32[]{:S(2)}, u32[]{:S(2)}) %collective-permute-start.10) | collective-permute-done | bytes 233504 | tf_op jit(solution)/shard_map/ppermute | solution.py:36
  94.6 1.0 collective-permute-done.11.bottom_ref
  95.8 2.5 %collective-permute-start.14 = (bf16[32,7296]{1,0:T(8,128)(2,1)S(1)}, bf16[32,7296]{1,0:T(8,128)(2,1)S(1)}, u32[]{:S(2)}, u32[]{:S(2)}) collective-permute-start(bf16[32,7296]{1,0:T(8,128)(2,1)S(1)} %get-tuple-element.48), channel_id=1, source_target_pairs={{0,6},{1,7},{2,0},{3,1},{4,2},{5,3},{6,4},{7,5},{8,14},{9,15},{10,... | collective-permute-start | bytes 1400840 | tf_op jit(solution)/shard_map/ppermute | solution.py:36
  98.3 6.5 %collective-permute-done.14.b_ref = bf16[32,7296]{1,0:T(8,128)(2,1)S(1)} collective-permute-done((bf16[32,7296]{1,0:T(8,128)(2,1)S(1)}, bf16[32,7296]{1,0:T(8,128)(2,1)S(1)}, u32[]{:S(2)}, u32[]{:S(2)}) %collective-permute-start.14) | collective-permute-done | bytes 466976 | tf_op jit(solution)/shard_map/ppermute | solution.py:36
  104.8 3.1 %collective-permute-done.15.c_ref = bf16[32,7296]{1,0:T(8,128)(2,1)S(1)} collective-permute-done((bf16[32,7296]{1,0:T(8,128)(2,1)S(1)}, bf16[32,7296]{1,0:T(8,128)(2,1)S(1)}, u32[]{:S(2)}, u32[]{:S(2)}) %collective-permute-start.15) | collective-permute-done | bytes 466976 | tf_op jit(solution)/shard_map/ppermute | solution.py:36
  109.0 2.7 %collective-permute-start.20 = (bf16[256,896]{1,0:T(8,128)(2,1)}, bf16[256,896]{1,0:T(8,128)(2,1)}, u32[]{:S(2)}, u32[]{:S(2)}) collective-permute-start(bf16[256,896]{1,0:T(8,128)(2,1)} %get-tuple-element.59), channel_id=1, source_target_pairs={{0,6},{1,7},{2,0},{3,1},{4,2},{5,3},{6,4},{7,5},{8,14},{9,15},{10,... | collective-permute-start | bytes 1376264 | tf_op jit(solution)/shard_map/ppermute | solution.py:36
  111.7 3.2 %collective-permute-start.16 = (bf16[8,7296]{1,0:T(8,128)(2,1)S(1)}, bf16[8,7296]{1,0:T(8,128)(2,1)S(1)}, u32[]{:S(2)}, u32[]{:S(2)}) collective-permute-start(bf16[8,7296]{1,0:T(8,128)(2,1)S(1)} %get-tuple-element.51), channel_id=1, source_target_pairs={{0,24},{1,25},{2,26},{3,27},{4,28},{5,29},{6,30},{7,31},{8,0},{9,1... | collective-permute-start | bytes 350216 | tf_op jit(solution)/shard_map/ppermute | solution.py:36
  115.4 2.4 %collective-permute-done.16.b1 = bf16[8,7296]{1,0:T(8,128)(2,1)S(1)} collective-permute-done((bf16[8,7296]{1,0:T(8,128)(2,1)S(1)}, bf16[8,7296]{1,0:T(8,128)(2,1)S(1)}, u32[]{:S(2)}, u32[]{:S(2)}) %collective-permute-start.16) | collective-permute-done | bytes 116768 | tf_op jit(solution)/shard_map/ppermute | solution.py:36
  117.8 2.3 %collective-permute-done.17.b2 = bf16[8,7296]{1,0:T(8,128)(2,1)S(1)} collective-permute-done((bf16[8,7296]{1,0:T(8,128)(2,1)S(1)}, bf16[8,7296]{1,0:T(8,128)(2,1)S(1)}, u32[]{:S(2)}, u32[]{:S(2)}) %collective-permute-start.17) | collective-permute-done | bytes 116768 | tf_op jit(solution)/shard_map/ppermute | solution.py:36
  121.9 1.4 copy-done.4
  123.3 2.7 %shard_map.85 = (f32[3,896,128]{2,1,0:T(8,128)S(1)}, bf16[3,896,128]{2,1,0:T(8,128)(2,1)S(1)}) custom-call(bf16[512,896]{1,0:T(8,128)(2,1)S(1)} %bitcast.14, bf16[512,896]{1,0:T(8,128)(2,1)S(1)} %collective-permute-done.12.left_ref.refs_1_, bf16[512,896]{1,0:T(8,128)(2,1)S(1)} %collective-permute-done.13.right_ref.refs_2_, ...), custom_call_target="tpu_custom_call" | custom-call | flops 1409286144 | bytes 7307264 | tf_op jit(solution)/shard_map/pallas_call | solution.py:48
  126.0 6.2 %collective-permute-start.21 = (bf16[3,896,128]{2,1,0:T(8,128)(2,1)S(1)}, bf16[3,896,128]{2,1,0:T(8,128)(2,1)S(1)}, u32[]{:S(2)}, u32[]{:S(2)}) collective-permute-start(bf16[3,896,128]{2,1,0:T(8,128)(2,1)S(1)} %get-tuple-element.62), channel_id=1, source_target_pairs={{0,1},{1,0},{2,3},{3,2},{4,5},{5,4},{6,7},{7,6},{8,9},{9,8},{10,11... | collective-permute-start | bytes 2064392 | tf_op jit(solution)/shard_map/ppermute | solution.py:36
  132.3 2.1 %shard_map.83 = (bf16[128,7168]{1,0:T(8,128)(2,1)}, f32[8,128]{1,0:T(8,128)}) custom-call(s32[1]{0:T(128)} %bitcast.y_ref, s32[8,128]{1,0:T(8,128)S(1)} %bitcast.17, bf16[8,7296]{1,0:T(8,128)(2,1)S(1)} %get-tuple-element.50.b0._, bf16[8,7296]{1,0:T(8,128)(2,1)S(1)} %collective-permute-done.16.b1, bf16[8,7296]{1,0:T(8,128)(2,1)S(1)} %copy-done.6, ...), custom_call_target="tpu_custom_call" | custom-call | bytes 2310148 | tf_op jit(solution)/shard_map/pallas_call | solution.py:48
  (52 shorter events, 9.7 us)
Async XLA Ops:
  7.2 55.2 %collective-permute-start = (bf16[3,7168,128]{2,1,0:T(8,128)(2,1)}, bf16[3,7168,128]{2,1,0:T(8,128)(2,1)}, u32[]{:S(2)}, u32[]{:S(2)}) collective-permute-start(bf16[3,7168,128]{2,1,0:T(8,128)(2,1)} %bitcast.9), channel_id=1, source_target_pairs={{0,1},{1,0},{2,3},{3,2},{4,5},{5,4},{6,7},{7,6},{8,9},{9,8},{10,11... | collective-permute-start | bytes 16515080 | tf_op jit(solution)/shard_map/ppermute | solution.py:36
  10.5 1.5 %copy-start.2 = (bf16[128,7168]{1,0:T(8,128)(2,1)S(1)}, bf16[128,7168]{1,0:T(8,128)(2,1)}, u32[]{:S(2)}) copy-start(bf16[128,7168]{1,0:T(8,128)(2,1)} %tok_ref.1) | copy-start | bytes 5505028
  12.0 1.5 %copy-start.3 = (bf16[128,7168]{1,0:T(8,128)(2,1)S(1)}, bf16[128,7168]{1,0:T(8,128)(2,1)}, u32[]{:S(2)}) copy-start(bf16[128,7168]{1,0:T(8,128)(2,1)} %cot_ref.1) | copy-start | bytes 5505028
  15.6 9.0 %collective-permute-start.1 = (bf16[8,14464]{1,0:T(8,128)(2,1)S(1)}, bf16[8,14464]{1,0:T(8,128)(2,1)S(1)}, u32[]{:S(2)}, u32[]{:S(2)}) collective-permute-start(bf16[8,14464]{1,0:T(8,128)(2,1)S(1)} %get-tuple-element.34), channel_id=1, source_target_pairs={{0,8},{1,9},{2,10},{3,11},{4,12},{5,13},{6,14},{7,15},{8,16},{9,17... | collective-permute-start | bytes 694280 | tf_op jit(solution)/shard_map/ppermute | solution.py:36
  15.7 13.0 %collective-permute-start.2 = (bf16[8,14464]{1,0:T(8,128)(2,1)S(1)}, bf16[8,14464]{1,0:T(8,128)(2,1)S(1)}, u32[]{:S(2)}, u32[]{:S(2)}) collective-permute-start(bf16[8,14464]{1,0:T(8,128)(2,1)S(1)} %get-tuple-element.35), channel_id=1, source_target_pairs={{0,16},{1,17},{2,18},{3,19},{4,20},{5,21},{6,22},{7,23},{8,24},{9,... | collective-permute-start | bytes 694280 | tf_op jit(solution)/shard_map/ppermute | solution.py:36
  17.9 11.5 %collective-permute-start.3 = (bf16[8,14464]{1,0:T(8,128)(2,1)S(1)}, bf16[8,14464]{1,0:T(8,128)(2,1)S(1)}, u32[]{:S(2)}, u32[]{:S(2)}) collective-permute-start(bf16[8,14464]{1,0:T(8,128)(2,1)S(1)} %get-tuple-element.36), channel_id=1, source_target_pairs={{0,24},{1,25},{2,26},{3,27},{4,28},{5,29},{6,30},{7,31},{8,0},{9,1... | collective-permute-start | bytes 694280 | tf_op jit(solution)/shard_map/ppermute | solution.py:36
  29.5 13.9 %collective-permute-start.4 = (bf16[16,14464]{1,0:T(8,128)(2,1)S(1)}, bf16[16,14464]{1,0:T(8,128)(2,1)S(1)}, u32[]{:S(2)}, u32[]{:S(2)}) collective-permute-start(bf16[16,14464]{1,0:T(8,128)(2,1)S(1)} %get-tuple-element.37.refs_0_.top_ref), channel_id=1, source_target_pairs={{0,2},{1,3},{2,4},{3,5},{4,6},{5,7},{6,0},{7,1},{8,10},{9,11},{10,... | collective-permute-start | bytes 1388552 | tf_op jit(solution)/shard_map/ppermute | solution.py:36
  30.0 13.5 %collective-permute-start.7 = (bf16[16,14464]{1,0:T(8,128)(2,1)S(1)}, bf16[16,14464]{1,0:T(8,128)(2,1)S(1)}, u32[]{:S(2)}, u32[]{:S(2)}) collective-permute-start(bf16[16,14464]{1,0:T(8,128)(2,1)S(1)} %get-tuple-element.38.refs_1_.bottom_ref), channel_id=1, source_target_pairs={{0,6},{1,7},{2,0},{3,1},{4,2},{5,3},{6,4},{7,5},{8,14},{9,15},{10,... | collective-permute-start | bytes 1388552 | tf_op jit(solution)/shard_map/ppermute | solution.py:36
  33.2 36.7 %all-to-all-start = ((bf16[8,64,896]{2,1,0:T(8,128)(2,1)}), bf16[8,64,896]{2,1,0:T(8,128)(2,1)S(1)}, u32[]{:S(2)}, u32[]{:S(2)}) async-start(bf16[8,64,896]{2,1,0:T(8,128)(2,1)} %bitcast.4), calls=%async_computation | async-start | bytes 1835008 | tf_op jit(solution)/shard_map/all_to_all | solution.py:275
  40.6 81.3 %all-gather.3.cloned.1.call-start = ((), (), s32[]{:S(2)}) async-start(), calls=%async_computation.1 | async-start | bytes 1769472 | tf_op jit(solution)/shard_map/all_gather | solution.py:301
  40.7 11.7 %collective-permute-start.5 = (bf16[16,14464]{1,0:T(8,128)(2,1)S(1)}, bf16[16,14464]{1,0:T(8,128)(2,1)S(1)}, u32[]{:S(2)}, u32[]{:S(2)}) collective-permute-start(bf16[16,14464]{1,0:T(8,128)(2,1)S(1)} %get-tuple-element.38.refs_1_.bottom_ref), channel_id=1, source_target_pairs={{0,2},{1,3},{2,4},{3,5},{4,6},{5,7},{6,0},{7,1},{8,10},{9,11},{10,... | collective-permute-start | bytes 1388552 | tf_op jit(solution)/shard_map/ppermute | solution.py:36
  40.8 11.6 %collective-permute-start.6 = (bf16[16,14464]{1,0:T(8,128)(2,1)S(1)}, bf16[16,14464]{1,0:T(8,128)(2,1)S(1)}, u32[]{:S(2)}, u32[]{:S(2)}) collective-permute-start(bf16[16,14464]{1,0:T(8,128)(2,1)S(1)} %get-tuple-element.37.refs_0_.top_ref), channel_id=1, source_target_pairs={{0,6},{1,7},{2,0},{3,1},{4,2},{5,3},{6,4},{7,5},{8,14},{9,15},{10,... | collective-permute-start | bytes 1388552 | tf_op jit(solution)/shard_map/ppermute | solution.py:36
  43.4 18.9 %collective-permute-start.8 = (bf16[16,14464]{1,0:T(8,128)(2,1)S(1)}, bf16[16,14464]{1,0:T(8,128)(2,1)S(1)}, u32[]{:S(2)}, u32[]{:S(2)}) collective-permute-start(bf16[16,14464]{1,0:T(8,128)(2,1)S(1)} %collective-permute-done.4.refs_2_), channel_id=1, source_target_pairs={{0,2},{1,3},{2,4},{3,5},{4,6},{5,7},{6,0},{7,1},{8,10},{9,11},{10,... | collective-permute-start | bytes 1388552 | tf_op jit(solution)/shard_map/ppermute | solution.py:36
  43.4 18.9 %collective-permute-start.9 = (bf16[16,14464]{1,0:T(8,128)(2,1)S(1)}, bf16[16,14464]{1,0:T(8,128)(2,1)S(1)}, u32[]{:S(2)}, u32[]{:S(2)}) collective-permute-start(bf16[16,14464]{1,0:T(8,128)(2,1)S(1)} %collective-permute-done.7.refs_5_), channel_id=1, source_target_pairs={{0,6},{1,7},{2,0},{3,1},{4,2},{5,3},{6,4},{7,5},{8,14},{9,15},{10,... | collective-permute-start | bytes 1388552 | tf_op jit(solution)/shard_map/ppermute | solution.py:36
  62.3 2.6 %copy-start = (bf16[7168,3,128]{2,0,1:T(8,128)(2,1)S(1)}, bf16[7168,3,128]{2,0,1:T(8,128)(2,1)}, u32[]{:S(2)}) copy-start(bf16[7168,3,128]{2,0,1:T(8,128)(2,1)} %param.9) | copy-start | bytes 16515076
  69.9 25.8 %collective-permute-start.12 = (bf16[512,896]{1,0:T(8,128)(2,1)S(1)}, bf16[512,896]{1,0:T(8,128)(2,1)S(1)}, u32[]{:S(2)}, u32[]{:S(2)}) collective-permute-start(bf16[512,896]{1,0:T(8,128)(2,1)S(1)} %bitcast.12), channel_id=1, source_target_pairs={{0,2},{1,3},{2,4},{3,5},{4,6},{5,7},{6,0},{7,1},{8,10},{9,11},{10,... | collective-permute-start | bytes 2752520 | tf_op jit(solution)/shard_map/ppermute | solution.py:36
  70.0 25.7 %collective-permute-start.13 = (bf16[512,896]{1,0:T(8,128)(2,1)S(1)}, bf16[512,896]{1,0:T(8,128)(2,1)S(1)}, u32[]{:S(2)}, u32[]{:S(2)}) collective-permute-start(bf16[512,896]{1,0:T(8,128)(2,1)S(1)} %bitcast.13), channel_id=1, source_target_pairs={{0,6},{1,7},{2,0},{3,1},{4,2},{5,3},{6,4},{7,5},{8,14},{9,15},{10,... | collective-permute-start | bytes 2752520 | tf_op jit(solution)/shard_map/ppermute | solution.py:36
  72.7 2.6 %copy-start.1 = (bf16[7168,3,128]{2,0,1:T(8,128)(2,1)S(1)}, bf16[7168,3,128]{2,0,1:T(8,128)(2,1)}, u32[]{:S(2)}) copy-start(bf16[7168,3,128]{2,0,1:T(8,128)(2,1)} %param.9) | copy-start | bytes 16515076
  80.3 14.2 %collective-permute-start.10 = (bf16[16,7296]{1,0:T(8,128)(2,1)S(1)}, bf16[16,7296]{1,0:T(8,128)(2,1)S(1)}, u32[]{:S(2)}, u32[]{:S(2)}) collective-permute-start(bf16[16,7296]{1,0:T(8,128)(2,1)S(1)} %get-tuple-element.44), channel_id=1, source_target_pairs={{0,6},{1,7},{2,0},{3,1},{4,2},{5,3},{6,4},{7,5},{8,14},{9,15},{10,... | collective-permute-start | bytes 700424 | tf_op jit(solution)/shard_map/ppermute | solution.py:36
  81.6 14.0 %collective-permute-start.11 = (bf16[16,7296]{1,0:T(8,128)(2,1)S(1)}, bf16[16,7296]{1,0:T(8,128)(2,1)S(1)}, u32[]{:S(2)}, u32[]{:S(2)}) collective-permute-start(bf16[16,7296]{1,0:T(8,128)(2,1)S(1)} %get-tuple-element.45), channel_id=1, source_target_pairs={{0,2},{1,3},{2,4},{3,5},{4,6},{5,7},{6,0},{7,1},{8,10},{9,11},{10,... | collective-permute-start | bytes 700424 | tf_op jit(solution)/shard_map/ppermute | solution.py:36
  95.8 9.0 %collective-permute-start.14 = (bf16[32,7296]{1,0:T(8,128)(2,1)S(1)}, bf16[32,7296]{1,0:T(8,128)(2,1)S(1)}, u32[]{:S(2)}, u32[]{:S(2)}) collective-permute-start(bf16[32,7296]{1,0:T(8,128)(2,1)S(1)} %get-tuple-element.48), channel_id=1, source_target_pairs={{0,6},{1,7},{2,0},{3,1},{4,2},{5,3},{6,4},{7,5},{8,14},{9,15},{10,... | collective-permute-start | bytes 1400840 | tf_op jit(solution)/shard_map/ppermute | solution.py:36
  98.3 9.5 %collective-permute-start.15 = (bf16[32,7296]{1,0:T(8,128)(2,1)S(1)}, bf16[32,7296]{1,0:T(8,128)(2,1)S(1)}, u32[]{:S(2)}, u32[]{:S(2)}) collective-permute-start(bf16[32,7296]{1,0:T(8,128)(2,1)S(1)} %get-tuple-element.49), channel_id=1, source_target_pairs={{0,2},{1,3},{2,4},{3,5},{4,6},{5,7},{6,0},{7,1},{8,10},{9,11},{10,... | collective-permute-start | bytes 1400840 | tf_op jit(solution)/shard_map/ppermute | solution.py:36
  109.0 12.9 %collective-permute-start.19 = (bf16[256,896]{1,0:T(8,128)(2,1)}, bf16[256,896]{1,0:T(8,128)(2,1)S(1)}, u32[]{:S(2)}, u32[]{:S(2)}) collective-permute-start(bf16[256,896]{1,0:T(8,128)(2,1)} %get-tuple-element.58), channel_id=1, source_target_pairs={{0,2},{1,3},{2,4},{3,5},{4,6},{5,7},{6,0},{7,1},{8,10},{9,11},{10,... | collective-permute-start | bytes 1376264 | tf_op jit(solution)/shard_map/ppermute | solution.py:36
  109.0 12.9 %collective-permute-start.20 = (bf16[256,896]{1,0:T(8,128)(2,1)}, bf16[256,896]{1,0:T(8,128)(2,1)}, u32[]{:S(2)}, u32[]{:S(2)}) collective-permute-start(bf16[256,896]{1,0:T(8,128)(2,1)} %get-tuple-element.59), channel_id=1, source_target_pairs={{0,6},{1,7},{2,0},{3,1},{4,2},{5,3},{6,4},{7,5},{8,14},{9,15},{10,... | collective-permute-start | bytes 1376264 | tf_op jit(solution)/shard_map/ppermute | solution.py:36
  111.7 6.2 %collective-permute-start.16 = (bf16[8,7296]{1,0:T(8,128)(2,1)S(1)}, bf16[8,7296]{1,0:T(8,128)(2,1)S(1)}, u32[]{:S(2)}, u32[]{:S(2)}) collective-permute-start(bf16[8,7296]{1,0:T(8,128)(2,1)S(1)} %get-tuple-element.51), channel_id=1, source_target_pairs={{0,24},{1,25},{2,26},{3,27},{4,28},{5,29},{6,30},{7,31},{8,0},{9,1... | collective-permute-start | bytes 350216 | tf_op jit(solution)/shard_map/ppermute | solution.py:36
  114.8 5.3 %collective-permute-start.17 = (bf16[8,7296]{1,0:T(8,128)(2,1)S(1)}, bf16[8,7296]{1,0:T(8,128)(2,1)S(1)}, u32[]{:S(2)}, u32[]{:S(2)}) collective-permute-start(bf16[8,7296]{1,0:T(8,128)(2,1)S(1)} %get-tuple-element.52), channel_id=1, source_target_pairs={{0,16},{1,17},{2,18},{3,19},{4,20},{5,21},{6,22},{7,23},{8,24},{9,... | collective-permute-start | bytes 350216 | tf_op jit(solution)/shard_map/ppermute | solution.py:36
  114.8 6.4 %collective-permute-start.18 = (bf16[8,7296]{1,0:T(8,128)(2,1)S(1)}, bf16[8,7296]{1,0:T(8,128)(2,1)S(1)}, u32[]{:S(2)}, u32[]{:S(2)}) collective-permute-start(bf16[8,7296]{1,0:T(8,128)(2,1)S(1)} %get-tuple-element.53), channel_id=1, source_target_pairs={{0,8},{1,9},{2,10},{3,11},{4,12},{5,13},{6,14},{7,15},{8,16},{9,17... | collective-permute-start | bytes 350216 | tf_op jit(solution)/shard_map/ppermute | solution.py:36
  121.9 1.4 copy-start.4
  123.3 9.0 %copy-start.6 = (bf16[8,7296]{1,0:T(8,128)(2,1)S(1)}, bf16[8,7296]{1,0:T(8,128)(2,1)}, u32[]{:S(2)}) copy-start(bf16[8,7296]{1,0:T(8,128)(2,1)} %copy-done.5) | copy-start | bytes 350212
  123.3 9.0 %copy-start.8 = (bf16[8,7296]{1,0:T(8,128)(2,1)S(1)}, bf16[8,7296]{1,0:T(8,128)(2,1)}, u32[]{:S(2)}) copy-start(bf16[8,7296]{1,0:T(8,128)(2,1)} %copy-done.7) | copy-start | bytes 350212
  123.3 9.0 %copy-start.10 = (s32[128,8]{0,1:T(8,128)S(1)}, s32[128,8]{0,1:T(8,128)}, u32[]{:S(2)}) copy-start(s32[128,8]{0,1:T(8,128)} %param.7) | copy-start | bytes 12292
  126.0 8.3 %collective-permute-start.21 = (bf16[3,896,128]{2,1,0:T(8,128)(2,1)S(1)}, bf16[3,896,128]{2,1,0:T(8,128)(2,1)S(1)}, u32[]{:S(2)}, u32[]{:S(2)}) collective-permute-start(bf16[3,896,128]{2,1,0:T(8,128)(2,1)S(1)} %get-tuple-element.62), channel_id=1, source_target_pairs={{0,1},{1,0},{2,3},{3,2},{4,5},{5,4},{6,7},{7,6},{8,9},{9,8},{10,11... | collective-permute-start | bytes 2064392 | tf_op jit(solution)/shard_map/ppermute | solution.py:36
  (4 other events, 2.7 us)
Sparse Core Ops, SparseCore 0:
  70.1 38.6 all-gather.2

commit v4 on v3

--- a/solution.py
+++ b/solution.py
@@ -281,7 +281,7 @@
         functools.partial(experts, len(blocks)),
         [((total, 3 * NC * hidden), BF16), ((total, LANES), BF16)],
         [*blocks, *w_all],
-        flops=3 * work,
+        flops=6 * work,
     )
     keep, to_left, to_right, far_up, far_down = call(
         shard_grads,

time: 143 us -> 149 us (1.042)
  waiting for transfers between devices: 55.2 us -> 58.5 us
  starting transfers between devices: 41.7 us -> 44.4 us
    all_to_all x1, waiting for transfers between devices: 0.01 us -> 6.28 us  [local(): cut = lax.all_to_all(cut, 'dp', split_axis=0, concat_axis=0, tiled=True)]
    ppermute x22, waiting for transfers between devices: 55.2 us -> 52.2 us  [send(): return lax.ppermute(array, 'expert', shifted(dy, dx, dc))]
    ppermute x22, starting transfers between devices: 34.2 us -> 36.7 us  [send(): return lax.ppermute(array, 'expert', shifted(dy, dx, dc))]
  transfers between devices with their start and end apart: 24 -> 24, of which waited for: 12 -> 13; matrix products, arithmetic and copies ran while one was open for 0% -> 0% of each run, Pallas kernels for 11% -> 11%
where the time goes in v4:
time: 149 us
  waiting for transfers between devices  58.5 us (39%)
  starting transfers between devices  44.4 us (30%)
  Pallas kernels  19.3 us (13%)
  between operations  14.2 us (10%)
  local copies, waits for them, and re-layouts  12.2 us (8%)
    ppermute x22, waiting for transfers between devices, send(): return lax.ppermute(array, 'expert', shifted(dy, dx, dc))  52.2 us
    ppermute x22, starting transfers between devices, send(): return lax.ppermute(array, 'expert', shifted(dy, dx, dc))  36.7 us
    pallas_call x11, Pallas kernels, call(): pl.pallas_call(body, out_shape=[jax.ShapeDtypeStruct(s, d) for s, d in ou...  19.3 us
    unnamed x24, local copies, waits for them, and re-layouts  12.2 us
    all_to_all x1, starting transfers between devices, local(): cut = lax.all_to_all(cut, 'dp', split_axis=0, concat_axis=0, tiled=True)  7.74 us
    all_to_all x1, waiting for transfers between devices, local(): cut = lax.all_to_all(cut, 'dp', split_axis=0, concat_axis=0, tiled=True)  6.28 us
  transfers between devices with their start and end apart: 24, of which 13 were waited for; matrix products, arithmetic and copies ran while one was open for 0% of the time, Pallas kernels for 11%

profile of v4, /device:TPU:1, one launch (start us, length us, event | category | flops | bytes accessed | tf_op | source)
XLA Modules:
  0.0 148.6 jit_solution(809015986791967637)
XLA Ops:
  7.2 3.3 %collective-permute-start = (bf16[3,7168,128]{2,1,0:T(8,128)(2,1)}, bf16[3,7168,128]{2,1,0:T(8,128)(2,1)}, u32[]{:S(2)}, u32[]{:S(2)}) collective-permute-start(bf16[3,7168,128]{2,1,0:T(8,128)(2,1)} %bitcast.9), channel_id=1, source_target_pairs={{0,1},{1,0},{2,3},{3,2},{4,5},{5,4},{6,7},{7,6},{8,9},{9,8},{10,11... | collective-permute-start | bytes 16515080 | tf_op jit(solution)/shard_map/ppermute | solution.py:36
  10.5 1.5 %copy-done.2 = bf16[128,7168]{1,0:T(8,128)(2,1)S(1)} copy-done((bf16[128,7168]{1,0:T(8,128)(2,1)S(1)}, bf16[128,7168]{1,0:T(8,128)(2,1)}, u32[]{:S(2)}) %copy-start.2) | copy-done | bytes 1835032
  12.0 1.5 %copy-done.3 = bf16[128,7168]{1,0:T(8,128)(2,1)S(1)} copy-done((bf16[128,7168]{1,0:T(8,128)(2,1)S(1)}, bf16[128,7168]{1,0:T(8,128)(2,1)}, u32[]{:S(2)}) %copy-start.3) | copy-done | bytes 1835032
  15.7 2.2 %collective-permute-start.2 = (bf16[8,14464]{1,0:T(8,128)(2,1)S(1)}, bf16[8,14464]{1,0:T(8,128)(2,1)S(1)}, u32[]{:S(2)}, u32[]{:S(2)}) collective-permute-start(bf16[8,14464]{1,0:T(8,128)(2,1)S(1)} %get-tuple-element.35), channel_id=1, source_target_pairs={{0,16},{1,17},{2,18},{3,19},{4,20},{5,21},{6,22},{7,23},{8,24},{9,... | collective-permute-start | bytes 694280 | tf_op jit(solution)/shard_map/ppermute | solution.py:36
  17.9 1.1 collective-permute-start.3
  18.9 5.6 %collective-permute-done.1.refs_1_ = bf16[8,14464]{1,0:T(8,128)(2,1)S(1)} collective-permute-done((bf16[8,14464]{1,0:T(8,128)(2,1)S(1)}, bf16[8,14464]{1,0:T(8,128)(2,1)S(1)}, u32[]{:S(2)}, u32[]{:S(2)}) %collective-permute-start.1) | collective-permute-done | bytes 231456 | tf_op jit(solution)/shard_map/ppermute | solution.py:36
  24.6 4.1 %collective-permute-done.2.refs_2_ = bf16[8,14464]{1,0:T(8,128)(2,1)S(1)} collective-permute-done((bf16[8,14464]{1,0:T(8,128)(2,1)S(1)}, bf16[8,14464]{1,0:T(8,128)(2,1)S(1)}, u32[]{:S(2)}, u32[]{:S(2)}) %collective-permute-start.2) | collective-permute-done | bytes 231456 | tf_op jit(solution)/shard_map/ppermute | solution.py:36
  30.0 2.3 %collective-permute-start.7 = (bf16[16,14464]{1,0:T(8,128)(2,1)S(1)}, bf16[16,14464]{1,0:T(8,128)(2,1)S(1)}, u32[]{:S(2)}, u32[]{:S(2)}) collective-permute-start(bf16[16,14464]{1,0:T(8,128)(2,1)S(1)} %get-tuple-element.38.refs_1_.bottom_ref), channel_id=1, source_target_pairs={{0,6},{1,7},{2,0},{3,1},{4,2},{5,3},{6,4},{7,5},{8,14},{9,15},{10,... | collective-permute-start | bytes 1388552 | tf_op jit(solution)/shard_map/ppermute | solution.py:36
  32.2 2.7 %collective-permute-start.6 = (bf16[16,14464]{1,0:T(8,128)(2,1)S(1)}, bf16[16,14464]{1,0:T(8,128)(2,1)}, u32[]{:S(2)}, u32[]{:S(2)}) collective-permute-start(bf16[16,14464]{1,0:T(8,128)(2,1)S(1)} %get-tuple-element.37.refs_0_.top_ref), channel_id=1, source_target_pairs={{0,6},{1,7},{2,0},{3,1},{4,2},{5,3},{6,4},{7,5},{8,14},{9,15},{10,... | collective-permute-start | bytes 1388552 | tf_op jit(solution)/shard_map/ppermute | solution.py:36
  34.9 6.8 %collective-permute-done.4.refs_2_ = bf16[16,14464]{1,0:T(8,128)(2,1)S(1)} collective-permute-done((bf16[16,14464]{1,0:T(8,128)(2,1)S(1)}, bf16[16,14464]{1,0:T(8,128)(2,1)S(1)}, u32[]{:S(2)}, u32[]{:S(2)}) %collective-permute-start.4) | collective-permute-done | bytes 462880 | tf_op jit(solution)/shard_map/ppermute | solution.py:36
  41.7 2.7 %collective-permute-start.9 = (bf16[16,14464]{1,0:T(8,128)(2,1)S(1)}, bf16[16,14464]{1,0:T(8,128)(2,1)}, u32[]{:S(2)}, u32[]{:S(2)}) collective-permute-start(bf16[16,14464]{1,0:T(8,128)(2,1)S(1)} %collective-permute-done.7.refs_5_), channel_id=1, source_target_pairs={{0,6},{1,7},{2,0},{3,1},{4,2},{5,3},{6,4},{7,5},{8,14},{9,15},{10,... | collective-permute-start | bytes 1388552 | tf_op jit(solution)/shard_map/ppermute | solution.py:36
  45.4 7.7 %all-to-all-start = ((bf16[8,64,896]{2,1,0:T(8,128)(2,1)}), bf16[8,64,896]{2,1,0:T(8,128)(2,1)S(1)}, u32[]{:S(2)}, u32[]{:S(2)}) async-start(bf16[8,64,896]{2,1,0:T(8,128)(2,1)} %bitcast.4), calls=%async_computation | async-start | bytes 1835008 | tf_op jit(solution)/shard_map/all_to_all | solution.py:275
  53.2 8.5 %collective-permute-done.8.refs_6_ = bf16[16,14464]{1,0:T(8,128)(2,1)} collective-permute-done((bf16[16,14464]{1,0:T(8,128)(2,1)S(1)}, bf16[16,14464]{1,0:T(8,128)(2,1)}, u32[]{:S(2)}, u32[]{:S(2)}) %collective-permute-start.8) | collective-permute-done | bytes 462880 | tf_op jit(solution)/shard_map/ppermute | solution.py:36
  61.7 2.6 %copy-done = bf16[7168,3,128]{2,0,1:T(8,128)(2,1)S(1)} copy-done((bf16[7168,3,128]{2,0,1:T(8,128)(2,1)S(1)}, bf16[7168,3,128]{2,0,1:T(8,128)(2,1)}, u32[]{:S(2)}) %copy-start) | copy-done | bytes 5505048
  64.2 5.4 %shard_map.78 = (bf16[128,768]{1,0:T(8,128)(2,1)}, bf16[128,128]{1,0:T(8,128)(2,1)S(1)}) custom-call(bf16[16,14464]{1,0:T(8,128)(2,1)S(1)} %get-tuple-element.37.refs_0_.top_ref, bf16[16,14464]{1,0:T(8,128)(2,1)S(1)} %get-tuple-element.38.refs_1_.bottom_ref, bf16[16,14464]{1,0:T(8,128)(2,1)S(1)} %collective-permute-done.4.refs_2_, ...), custom_call_target="tpu_custom_call" | custom-call | flops 2818572288 | bytes 14942208 | tf_op jit(solution)/shard_map/pallas_call | solution.py:48
  69.7 6.3 %all-to-all-done = bf16[8,64,896]{2,1,0:T(8,128)(2,1)S(1)} async-done(((bf16[8,64,896]{2,1,0:T(8,128)(2,1)}), bf16[8,64,896]{2,1,0:T(8,128)(2,1)S(1)}, u32[]{:S(2)}, u32[]{:S(2)}) %all-to-all-start) | async-done | bytes 917536 | tf_op jit(solution)/shard_map/all_to_all | solution.py:275
  76.0 2.7 %collective-permute-start.13 = (bf16[512,896]{1,0:T(8,128)(2,1)S(1)}, bf16[512,896]{1,0:T(8,128)(2,1)S(1)}, u32[]{:S(2)}, u32[]{:S(2)}) collective-permute-start(bf16[512,896]{1,0:T(8,128)(2,1)S(1)} %bitcast.13), channel_id=1, source_target_pairs={{0,6},{1,7},{2,0},{3,1},{4,2},{5,3},{6,4},{7,5},{8,14},{9,15},{10,... | collective-permute-start | bytes 2752520 | tf_op jit(solution)/shard_map/ppermute | solution.py:36
  78.6 2.6 %copy-done.1 = bf16[7168,3,128]{2,0,1:T(8,128)(2,1)S(1)} copy-done((bf16[7168,3,128]{2,0,1:T(8,128)(2,1)S(1)}, bf16[7168,3,128]{2,0,1:T(8,128)(2,1)}, u32[]{:S(2)}) %copy-start.1) | copy-done | bytes 5505048
  81.2 5.0 %shard_map.79 = (bf16[32,7296]{1,0:T(8,128)(2,1)S(1)}, bf16[32,7296]{1,0:T(8,128)(2,1)S(1)}, bf16[32,7296]{1,0:T(8,128)(2,1)S(1)}, bf16[16,7296]{1,0:T(8,128)(2,1)S(1)}, bf16[16,7296]{1,0:T(8,128)(2,1)S(1)}) custom-call(bf16[3,7168,128]{2,1,0:T(8,128)(2,1)S(1)} %bitcast.11, bf16[3,7168,128]{2,1,0:T(8,128)(2,1)} %collective-permute-done.refs_9_.refs_1_, ...), custom_call_target="tpu_custom_call" | custom-call | flops 939524096 | bytes 13107200 | tf_op jit(solution)/shard_map/pallas_call | solution.py:48
  86.3 1.5 collective-permute-start.11
  87.8 11.1 %collective-permute-done.10.top_ref = bf16[16,7296]{1,0:T(8,128)(2,1)S(1)} collective-permute-done((bf16[16,7296]{1,0:T(8,128)(2,1)S(1)}, bf16[16,7296]{1,0:T(8,128)(2,1)S(1)}, u32[]{:S(2)}, u32[]{:S(2)}) %collective-permute-start.10) | collective-permute-done | bytes 233504 | tf_op jit(solution)/shard_map/ppermute | solution.py:36
  100.1 2.5 %collective-permute-start.14 = (bf16[32,7296]{1,0:T(8,128)(2,1)S(1)}, bf16[32,7296]{1,0:T(8,128)(2,1)S(1)}, u32[]{:S(2)}, u32[]{:S(2)}) collective-permute-start(bf16[32,7296]{1,0:T(8,128)(2,1)S(1)} %get-tuple-element.48), channel_id=1, source_target_pairs={{0,6},{1,7},{2,0},{3,1},{4,2},{5,3},{6,4},{7,5},{8,14},{9,15},{10,... | collective-permute-start | bytes 1400840 | tf_op jit(solution)/shard_map/ppermute | solution.py:36
  102.6 6.2 %collective-permute-done.14.b_ref = bf16[32,7296]{1,0:T(8,128)(2,1)S(1)} collective-permute-done((bf16[32,7296]{1,0:T(8,128)(2,1)S(1)}, bf16[32,7296]{1,0:T(8,128)(2,1)S(1)}, u32[]{:S(2)}, u32[]{:S(2)}) %collective-permute-start.14) | collective-permute-done | bytes 466976 | tf_op jit(solution)/shard_map/ppermute | solution.py:36
  108.8 2.8 %collective-permute-done.15.c_ref = bf16[32,7296]{1,0:T(8,128)(2,1)S(1)} collective-permute-done((bf16[32,7296]{1,0:T(8,128)(2,1)S(1)}, bf16[32,7296]{1,0:T(8,128)(2,1)S(1)}, u32[]{:S(2)}, u32[]{:S(2)}) %collective-permute-start.15) | collective-permute-done | bytes 466976 | tf_op jit(solution)/shard_map/ppermute | solution.py:36
  112.8 2.7 %collective-permute-start.20 = (bf16[256,896]{1,0:T(8,128)(2,1)}, bf16[256,896]{1,0:T(8,128)(2,1)}, u32[]{:S(2)}, u32[]{:S(2)}) collective-permute-start(bf16[256,896]{1,0:T(8,128)(2,1)} %get-tuple-element.59), channel_id=1, source_target_pairs={{0,6},{1,7},{2,0},{3,1},{4,2},{5,3},{6,4},{7,5},{8,14},{9,15},{10,... | collective-permute-start | bytes 1376264 | tf_op jit(solution)/shard_map/ppermute | solution.py:36
  115.5 3.6 %collective-permute-start.16 = (bf16[8,7296]{1,0:T(8,128)(2,1)S(1)}, bf16[8,7296]{1,0:T(8,128)(2,1)S(1)}, u32[]{:S(2)}, u32[]{:S(2)}) collective-permute-start(bf16[8,7296]{1,0:T(8,128)(2,1)S(1)} %get-tuple-element.51), channel_id=1, source_target_pairs={{0,24},{1,25},{2,26},{3,27},{4,28},{5,29},{6,30},{7,31},{8,0},{9,1... | collective-permute-start | bytes 350216 | tf_op jit(solution)/shard_map/ppermute | solution.py:36
  119.7 2.4 %collective-permute-done.16.b1 = bf16[8,7296]{1,0:T(8,128)(2,1)S(1)} collective-permute-done((bf16[8,7296]{1,0:T(8,128)(2,1)S(1)}, bf16[8,7296]{1,0:T(8,128)(2,1)S(1)}, u32[]{:S(2)}, u32[]{:S(2)}) %collective-permute-start.16) | collective-permute-done | bytes 116768 | tf_op jit(solution)/shard_map/ppermute | solution.py:36
  122.1 2.3 %collective-permute-done.17.b2 = bf16[8,7296]{1,0:T(8,128)(2,1)S(1)} collective-permute-done((bf16[8,7296]{1,0:T(8,128)(2,1)S(1)}, bf16[8,7296]{1,0:T(8,128)(2,1)S(1)}, u32[]{:S(2)}, u32[]{:S(2)}) %collective-permute-start.17) | collective-permute-done | bytes 116768 | tf_op jit(solution)/shard_map/ppermute | solution.py:36
  126.2 1.4 copy-done.4
  127.6 2.7 %shard_map.85 = (f32[3,896,128]{2,1,0:T(8,128)S(1)}, bf16[3,896,128]{2,1,0:T(8,128)(2,1)S(1)}) custom-call(bf16[512,896]{1,0:T(8,128)(2,1)S(1)} %bitcast.14, bf16[512,896]{1,0:T(8,128)(2,1)S(1)} %collective-permute-done.12.left_ref.refs_1_, bf16[512,896]{1,0:T(8,128)(2,1)S(1)} %collective-permute-done.13.right_ref.refs_2_, ...), custom_call_target="tpu_custom_call" | custom-call | flops 1409286144 | bytes 7307264 | tf_op jit(solution)/shard_map/pallas_call | solution.py:48
  130.3 8.4 %collective-permute-start.21 = (bf16[3,896,128]{2,1,0:T(8,128)(2,1)S(1)}, bf16[3,896,128]{2,1,0:T(8,128)(2,1)S(1)}, u32[]{:S(2)}, u32[]{:S(2)}) collective-permute-start(bf16[3,896,128]{2,1,0:T(8,128)(2,1)S(1)} %get-tuple-element.62), channel_id=1, source_target_pairs={{0,1},{1,0},{2,3},{3,2},{4,5},{5,4},{6,7},{7,6},{8,9},{9,8},{10,11... | collective-permute-start | bytes 2064392 | tf_op jit(solution)/shard_map/ppermute | solution.py:36
  138.7 2.1 %shard_map.83 = (bf16[128,7168]{1,0:T(8,128)(2,1)}, f32[8,128]{1,0:T(8,128)}) custom-call(s32[1]{0:T(128)} %bitcast.y_ref, s32[8,128]{1,0:T(8,128)S(1)} %bitcast.17, bf16[8,7296]{1,0:T(8,128)(2,1)S(1)} %get-tuple-element.50.b0._, bf16[8,7296]{1,0:T(8,128)(2,1)S(1)} %collective-permute-done.16.b1, bf16[8,7296]{1,0:T(8,128)(2,1)S(1)} %copy-done.6, ...), custom_call_target="tpu_custom_call" | custom-call | bytes 2310148 | tf_op jit(solution)/shard_map/pallas_call | solution.py:48
  (52 shorter events, 10.4 us)
Async XLA Ops:
  7.2 54.5 %collective-permute-start = (bf16[3,7168,128]{2,1,0:T(8,128)(2,1)}, bf16[3,7168,128]{2,1,0:T(8,128)(2,1)}, u32[]{:S(2)}, u32[]{:S(2)}) collective-permute-start(bf16[3,7168,128]{2,1,0:T(8,128)(2,1)} %bitcast.9), channel_id=1, source_target_pairs={{0,1},{1,0},{2,3},{3,2},{4,5},{5,4},{6,7},{7,6},{8,9},{9,8},{10,11... | collective-permute-start | bytes 16515080 | tf_op jit(solution)/shard_map/ppermute | solution.py:36
  10.5 1.5 %copy-start.2 = (bf16[128,7168]{1,0:T(8,128)(2,1)S(1)}, bf16[128,7168]{1,0:T(8,128)(2,1)}, u32[]{:S(2)}) copy-start(bf16[128,7168]{1,0:T(8,128)(2,1)} %tok_ref.1) | copy-start | bytes 5505028
  12.0 1.5 %copy-start.3 = (bf16[128,7168]{1,0:T(8,128)(2,1)S(1)}, bf16[128,7168]{1,0:T(8,128)(2,1)}, u32[]{:S(2)}) copy-start(bf16[128,7168]{1,0:T(8,128)(2,1)} %cot_ref.1) | copy-start | bytes 5505028
  15.6 9.0 %collective-permute-start.1 = (bf16[8,14464]{1,0:T(8,128)(2,1)S(1)}, bf16[8,14464]{1,0:T(8,128)(2,1)S(1)}, u32[]{:S(2)}, u32[]{:S(2)}) collective-permute-start(bf16[8,14464]{1,0:T(8,128)(2,1)S(1)} %get-tuple-element.34), channel_id=1, source_target_pairs={{0,8},{1,9},{2,10},{3,11},{4,12},{5,13},{6,14},{7,15},{8,16},{9,17... | collective-permute-start | bytes 694280 | tf_op jit(solution)/shard_map/ppermute | solution.py:36
  15.7 13.0 %collective-permute-start.2 = (bf16[8,14464]{1,0:T(8,128)(2,1)S(1)}, bf16[8,14464]{1,0:T(8,128)(2,1)S(1)}, u32[]{:S(2)}, u32[]{:S(2)}) collective-permute-start(bf16[8,14464]{1,0:T(8,128)(2,1)S(1)} %get-tuple-element.35), channel_id=1, source_target_pairs={{0,16},{1,17},{2,18},{3,19},{4,20},{5,21},{6,22},{7,23},{8,24},{9,... | collective-permute-start | bytes 694280 | tf_op jit(solution)/shard_map/ppermute | solution.py:36
  17.9 11.5 %collective-permute-start.3 = (bf16[8,14464]{1,0:T(8,128)(2,1)S(1)}, bf16[8,14464]{1,0:T(8,128)(2,1)S(1)}, u32[]{:S(2)}, u32[]{:S(2)}) collective-permute-start(bf16[8,14464]{1,0:T(8,128)(2,1)S(1)} %get-tuple-element.36), channel_id=1, source_target_pairs={{0,24},{1,25},{2,26},{3,27},{4,28},{5,29},{6,30},{7,31},{8,0},{9,1... | collective-permute-start | bytes 694280 | tf_op jit(solution)/shard_map/ppermute | solution.py:36
  29.5 12.3 %collective-permute-start.4 = (bf16[16,14464]{1,0:T(8,128)(2,1)S(1)}, bf16[16,14464]{1,0:T(8,128)(2,1)S(1)}, u32[]{:S(2)}, u32[]{:S(2)}) collective-permute-start(bf16[16,14464]{1,0:T(8,128)(2,1)S(1)} %get-tuple-element.37.refs_0_.top_ref), channel_id=1, source_target_pairs={{0,2},{1,3},{2,4},{3,5},{4,6},{5,7},{6,0},{7,1},{8,10},{9,11},{10,... | collective-permute-start | bytes 1388552 | tf_op jit(solution)/shard_map/ppermute | solution.py:36
  30.0 11.8 %collective-permute-start.7 = (bf16[16,14464]{1,0:T(8,128)(2,1)S(1)}, bf16[16,14464]{1,0:T(8,128)(2,1)S(1)}, u32[]{:S(2)}, u32[]{:S(2)}) collective-permute-start(bf16[16,14464]{1,0:T(8,128)(2,1)S(1)} %get-tuple-element.38.refs_1_.bottom_ref), channel_id=1, source_target_pairs={{0,6},{1,7},{2,0},{3,1},{4,2},{5,3},{6,4},{7,5},{8,14},{9,15},{10,... | collective-permute-start | bytes 1388552 | tf_op jit(solution)/shard_map/ppermute | solution.py:36
  32.2 21.0 %collective-permute-start.5 = (bf16[16,14464]{1,0:T(8,128)(2,1)S(1)}, bf16[16,14464]{1,0:T(8,128)(2,1)S(1)}, u32[]{:S(2)}, u32[]{:S(2)}) collective-permute-start(bf16[16,14464]{1,0:T(8,128)(2,1)S(1)} %get-tuple-element.38.refs_1_.bottom_ref), channel_id=1, source_target_pairs={{0,2},{1,3},{2,4},{3,5},{4,6},{5,7},{6,0},{7,1},{8,10},{9,11},{10,... | collective-permute-start | bytes 1388552 | tf_op jit(solution)/shard_map/ppermute | solution.py:36
  32.2 21.0 %collective-permute-start.6 = (bf16[16,14464]{1,0:T(8,128)(2,1)S(1)}, bf16[16,14464]{1,0:T(8,128)(2,1)}, u32[]{:S(2)}, u32[]{:S(2)}) collective-permute-start(bf16[16,14464]{1,0:T(8,128)(2,1)S(1)} %get-tuple-element.37.refs_0_.top_ref), channel_id=1, source_target_pairs={{0,6},{1,7},{2,0},{3,1},{4,2},{5,3},{6,4},{7,5},{8,14},{9,15},{10,... | collective-permute-start | bytes 1388552 | tf_op jit(solution)/shard_map/ppermute | solution.py:36
  41.7 19.9 %collective-permute-start.8 = (bf16[16,14464]{1,0:T(8,128)(2,1)S(1)}, bf16[16,14464]{1,0:T(8,128)(2,1)}, u32[]{:S(2)}, u32[]{:S(2)}) collective-permute-start(bf16[16,14464]{1,0:T(8,128)(2,1)S(1)} %collective-permute-done.4.refs_2_), channel_id=1, source_target_pairs={{0,2},{1,3},{2,4},{3,5},{4,6},{5,7},{6,0},{7,1},{8,10},{9,11},{10,... | collective-permute-start | bytes 1388552 | tf_op jit(solution)/shard_map/ppermute | solution.py:36
  41.7 19.9 %collective-permute-start.9 = (bf16[16,14464]{1,0:T(8,128)(2,1)S(1)}, bf16[16,14464]{1,0:T(8,128)(2,1)}, u32[]{:S(2)}, u32[]{:S(2)}) collective-permute-start(bf16[16,14464]{1,0:T(8,128)(2,1)S(1)} %collective-permute-done.7.refs_5_), channel_id=1, source_target_pairs={{0,6},{1,7},{2,0},{3,1},{4,2},{5,3},{6,4},{7,5},{8,14},{9,15},{10,... | collective-permute-start | bytes 1388552 | tf_op jit(solution)/shard_map/ppermute | solution.py:36
  45.4 30.6 %all-to-all-start = ((bf16[8,64,896]{2,1,0:T(8,128)(2,1)}), bf16[8,64,896]{2,1,0:T(8,128)(2,1)S(1)}, u32[]{:S(2)}, u32[]{:S(2)}) async-start(bf16[8,64,896]{2,1,0:T(8,128)(2,1)} %bitcast.4), calls=%async_computation | async-start | bytes 1835008 | tf_op jit(solution)/shard_map/all_to_all | solution.py:275
  53.1 73.0 %all-gather.3.cloned.1.call-start = ((), (), s32[]{:S(2)}) async-start(), calls=%async_computation.1 | async-start | bytes 1769472 | tf_op jit(solution)/shard_map/all_gather | solution.py:301
  61.7 2.6 %copy-start = (bf16[7168,3,128]{2,0,1:T(8,128)(2,1)S(1)}, bf16[7168,3,128]{2,0,1:T(8,128)(2,1)}, u32[]{:S(2)}) copy-start(bf16[7168,3,128]{2,0,1:T(8,128)(2,1)} %param.9) | copy-start | bytes 16515076
  76.0 24.2 %collective-permute-start.12 = (bf16[512,896]{1,0:T(8,128)(2,1)S(1)}, bf16[512,896]{1,0:T(8,128)(2,1)S(1)}, u32[]{:S(2)}, u32[]{:S(2)}) collective-permute-start(bf16[512,896]{1,0:T(8,128)(2,1)S(1)} %bitcast.12), channel_id=1, source_target_pairs={{0,2},{1,3},{2,4},{3,5},{4,6},{5,7},{6,0},{7,1},{8,10},{9,11},{10,... | collective-permute-start | bytes 2752520 | tf_op jit(solution)/shard_map/ppermute | solution.py:36
  76.0 24.2 %collective-permute-start.13 = (bf16[512,896]{1,0:T(8,128)(2,1)S(1)}, bf16[512,896]{1,0:T(8,128)(2,1)S(1)}, u32[]{:S(2)}, u32[]{:S(2)}) collective-permute-start(bf16[512,896]{1,0:T(8,128)(2,1)S(1)} %bitcast.13), channel_id=1, source_target_pairs={{0,6},{1,7},{2,0},{3,1},{4,2},{5,3},{6,4},{7,5},{8,14},{9,15},{10,... | collective-permute-start | bytes 2752520 | tf_op jit(solution)/shard_map/ppermute | solution.py:36
  78.6 2.6 %copy-start.1 = (bf16[7168,3,128]{2,0,1:T(8,128)(2,1)S(1)}, bf16[7168,3,128]{2,0,1:T(8,128)(2,1)}, u32[]{:S(2)}) copy-start(bf16[7168,3,128]{2,0,1:T(8,128)(2,1)} %param.9) | copy-start | bytes 16515076
  86.3 12.6 %collective-permute-start.10 = (bf16[16,7296]{1,0:T(8,128)(2,1)S(1)}, bf16[16,7296]{1,0:T(8,128)(2,1)S(1)}, u32[]{:S(2)}, u32[]{:S(2)}) collective-permute-start(bf16[16,7296]{1,0:T(8,128)(2,1)S(1)} %get-tuple-element.44), channel_id=1, source_target_pairs={{0,6},{1,7},{2,0},{3,1},{4,2},{5,3},{6,4},{7,5},{8,14},{9,15},{10,... | collective-permute-start | bytes 700424 | tf_op jit(solution)/shard_map/ppermute | solution.py:36
  86.3 13.6 %collective-permute-start.11 = (bf16[16,7296]{1,0:T(8,128)(2,1)S(1)}, bf16[16,7296]{1,0:T(8,128)(2,1)S(1)}, u32[]{:S(2)}, u32[]{:S(2)}) collective-permute-start(bf16[16,7296]{1,0:T(8,128)(2,1)S(1)} %get-tuple-element.45), channel_id=1, source_target_pairs={{0,2},{1,3},{2,4},{3,5},{4,6},{5,7},{6,0},{7,1},{8,10},{9,11},{10,... | collective-permute-start | bytes 700424 | tf_op jit(solution)/shard_map/ppermute | solution.py:36
  100.1 8.7 %collective-permute-start.14 = (bf16[32,7296]{1,0:T(8,128)(2,1)S(1)}, bf16[32,7296]{1,0:T(8,128)(2,1)S(1)}, u32[]{:S(2)}, u32[]{:S(2)}) collective-permute-start(bf16[32,7296]{1,0:T(8,128)(2,1)S(1)} %get-tuple-element.48), channel_id=1, source_target_pairs={{0,6},{1,7},{2,0},{3,1},{4,2},{5,3},{6,4},{7,5},{8,14},{9,15},{10,... | collective-permute-start | bytes 1400840 | tf_op jit(solution)/shard_map/ppermute | solution.py:36
  102.6 9.0 %collective-permute-start.15 = (bf16[32,7296]{1,0:T(8,128)(2,1)S(1)}, bf16[32,7296]{1,0:T(8,128)(2,1)S(1)}, u32[]{:S(2)}, u32[]{:S(2)}) collective-permute-start(bf16[32,7296]{1,0:T(8,128)(2,1)S(1)} %get-tuple-element.49), channel_id=1, source_target_pairs={{0,2},{1,3},{2,4},{3,5},{4,6},{5,7},{6,0},{7,1},{8,10},{9,11},{10,... | collective-permute-start | bytes 1400840 | tf_op jit(solution)/shard_map/ppermute | solution.py:36
  112.8 13.3 %collective-permute-start.19 = (bf16[256,896]{1,0:T(8,128)(2,1)}, bf16[256,896]{1,0:T(8,128)(2,1)S(1)}, u32[]{:S(2)}, u32[]{:S(2)}) collective-permute-start(bf16[256,896]{1,0:T(8,128)(2,1)} %get-tuple-element.58), channel_id=1, source_target_pairs={{0,2},{1,3},{2,4},{3,5},{4,6},{5,7},{6,0},{7,1},{8,10},{9,11},{10,... | collective-permute-start | bytes 1376264 | tf_op jit(solution)/shard_map/ppermute | solution.py:36
  112.8 13.3 %collective-permute-start.20 = (bf16[256,896]{1,0:T(8,128)(2,1)}, bf16[256,896]{1,0:T(8,128)(2,1)}, u32[]{:S(2)}, u32[]{:S(2)}) collective-permute-start(bf16[256,896]{1,0:T(8,128)(2,1)} %get-tuple-element.59), channel_id=1, source_target_pairs={{0,6},{1,7},{2,0},{3,1},{4,2},{5,3},{6,4},{7,5},{8,14},{9,15},{10,... | collective-permute-start | bytes 1376264 | tf_op jit(solution)/shard_map/ppermute | solution.py:36
  115.5 6.6 %collective-permute-start.16 = (bf16[8,7296]{1,0:T(8,128)(2,1)S(1)}, bf16[8,7296]{1,0:T(8,128)(2,1)S(1)}, u32[]{:S(2)}, u32[]{:S(2)}) collective-permute-start(bf16[8,7296]{1,0:T(8,128)(2,1)S(1)} %get-tuple-element.51), channel_id=1, source_target_pairs={{0,24},{1,25},{2,26},{3,27},{4,28},{5,29},{6,30},{7,31},{8,0},{9,1... | collective-permute-start | bytes 350216 | tf_op jit(solution)/shard_map/ppermute | solution.py:36
  119.1 5.3 %collective-permute-start.17 = (bf16[8,7296]{1,0:T(8,128)(2,1)S(1)}, bf16[8,7296]{1,0:T(8,128)(2,1)S(1)}, u32[]{:S(2)}, u32[]{:S(2)}) collective-permute-start(bf16[8,7296]{1,0:T(8,128)(2,1)S(1)} %get-tuple-element.52), channel_id=1, source_target_pairs={{0,16},{1,17},{2,18},{3,19},{4,20},{5,21},{6,22},{7,23},{8,24},{9,... | collective-permute-start | bytes 350216 | tf_op jit(solution)/shard_map/ppermute | solution.py:36
  119.1 6.4 %collective-permute-start.18 = (bf16[8,7296]{1,0:T(8,128)(2,1)S(1)}, bf16[8,7296]{1,0:T(8,128)(2,1)S(1)}, u32[]{:S(2)}, u32[]{:S(2)}) collective-permute-start(bf16[8,7296]{1,0:T(8,128)(2,1)S(1)} %get-tuple-element.53), channel_id=1, source_target_pairs={{0,8},{1,9},{2,10},{3,11},{4,12},{5,13},{6,14},{7,15},{8,16},{9,17... | collective-permute-start | bytes 350216 | tf_op jit(solution)/shard_map/ppermute | solution.py:36
  126.2 1.4 copy-start.4
  127.6 11.1 %copy-start.6 = (bf16[8,7296]{1,0:T(8,128)(2,1)S(1)}, bf16[8,7296]{1,0:T(8,128)(2,1)}, u32[]{:S(2)}) copy-start(bf16[8,7296]{1,0:T(8,128)(2,1)} %copy-done.5) | copy-start | bytes 350212
  127.6 11.1 %copy-start.8 = (bf16[8,7296]{1,0:T(8,128)(2,1)S(1)}, bf16[8,7296]{1,0:T(8,128)(2,1)}, u32[]{:S(2)}) copy-start(bf16[8,7296]{1,0:T(8,128)(2,1)} %copy-done.7) | copy-start | bytes 350212
  127.6 11.1 %copy-start.10 = (s32[128,8]{0,1:T(8,128)S(1)}, s32[128,8]{0,1:T(8,128)}, u32[]{:S(2)}) copy-start(s32[128,8]{0,1:T(8,128)} %param.7) | copy-start | bytes 12292
  130.3 10.5 %collective-permute-start.21 = (bf16[3,896,128]{2,1,0:T(8,128)(2,1)S(1)}, bf16[3,896,128]{2,1,0:T(8,128)(2,1)S(1)}, u32[]{:S(2)}, u32[]{:S(2)}) collective-permute-start(bf16[3,896,128]{2,1,0:T(8,128)(2,1)S(1)} %get-tuple-element.62), channel_id=1, source_target_pairs={{0,1},{1,0},{2,3},{3,2},{4,5},{5,4},{6,7},{7,6},{8,9},{9,8},{10,11... | collective-permute-start | bytes 2064392 | tf_op jit(solution)/shard_map/ppermute | solution.py:36
  (4 other events, 2.7 us)
Sparse Core Ops, SparseCore 0:
  69.8 38.9 all-gather.2

commit v5 on v3

--- a/solution.py
+++ b/solution.py
@@ -40,16 +40,18 @@
     return lax.optimization_barrier((array, *others))[0]
 
 
-def call(body, outs, operands, scalars=0, flops=0, limit=12):
+def call(body, outs, operands, scalars=0, flops=0, limit=12, far=0, scratch=()):
     moved = sum(o.size * o.dtype.itemsize for o in operands)
     moved += sum(math.prod(s) * jnp.dtype(d).itemsize for s, d in outs)
     specs = [pl.BlockSpec(memory_space=SMEM)] * scalars
-    specs += [pl.BlockSpec(memory_space=VMEM)] * (len(operands) - scalars)
+    specs += [pl.BlockSpec(memory_space=VMEM)] * (len(operands) - scalars - far)
+    specs += [pl.BlockSpec(memory_space=pltpu.MemorySpace.HBM)] * far
     return pl.pallas_call(
         body,
         out_shape=[jax.ShapeDtypeStruct(s, d) for s, d in outs],
         in_specs=specs,
         out_specs=[pl.BlockSpec(memory_space=VMEM)] * len(outs),
+        scratch_shapes=list(scratch),
         cost_estimate=pl.CostEstimate(flops=flops, bytes_accessed=moved, transcendentals=0),
         compiler_params=pltpu.CompilerParams(vmem_limit_bytes=limit * 1024 * 1024),
     )(*operands)
@@ -119,12 +121,29 @@
 
 
 def experts(n_blocks, *refs):
-    blocks, w_refs = refs[:n_blocks], refs[n_blocks : n_blocks + NC]
-    g_ref, sw_ref = refs[n_blocks + NC :]
-    width, hidden = w_refs[0].shape[1:]
+    blocks, w_far = refs[:n_blocks], refs[n_blocks : n_blocks + NC]
+    g_ref, sw_ref, w_ref, sems = refs[n_blocks + NC :]
+    width, hidden = w_far[0].shape[1:]
+    copies = [
+        [
+            pltpu.make_async_copy(
+                w_far[c].at[:, pl.ds(at, CHUNK), :],
+                w_ref.at[c, :, pl.ds(at, CHUNK), :],
+                sems.at[c, at // CHUNK],
+            )
+            for c in range(NC)
+        ]
+        for at in range(0, width, CHUNK)
+    ]
+    for two in copies:
+        for copy in two:
+            copy.start()
+    w_refs = [w_ref.at[c] for c in range(NC)]
     both, back = None, None
     for at in range(0, width, CHUNK):
         cols = slice(at, at + CHUNK)
+        for copy in copies[at // CHUNK]:
+            copy.wait()
         part = jnp.dot(
             rows_of(blocks, cols), side_by_side(w_refs, (0, 1), cols), preferred_element_type=F32
         )
@@ -282,6 +301,12 @@
         [((total, 3 * NC * hidden), BF16), ((total, LANES), BF16)],
         [*blocks, *w_all],
         flops=3 * work,
+        limit=50,
+        far=NC,
+        scratch=[
+            pltpu.VMEM((NC, 3, width, hidden), BF16),
+            pltpu.SemaphoreType.DMA((NC, width // CHUNK)),
+        ],
     )
     keep, to_left, to_right, far_up, far_down = call(
         shard_grads,

time: 143 us -> 140 us (0.979)
  local copies, waits for them, and re-layouts: 12.2 us -> 9.64 us
    unnamed x24 -> x22, local copies, waits for them, and re-layouts: 12.2 us -> 9.64 us
where the time goes in v5:
time: 140 us
  waiting for transfers between devices  55.2 us (39%)
  starting transfers between devices  41.7 us (30%)
  Pallas kernels  19.3 us (14%)
  between operations  14.2 us (10%)
  local copies, waits for them, and re-layouts  9.64 us (7%)
    ppermute x22, waiting for transfers between devices, send(): return lax.ppermute(array, 'expert', shifted(dy, dx, dc))  55.2 us
    ppermute x22, starting transfers between devices, send(): return lax.ppermute(array, 'expert', shifted(dy, dx, dc))  34.3 us
    pallas_call x11, Pallas kernels, call(): pl.pallas_call(body, out_shape=[jax.ShapeDtypeStruct(s, d) for s, d in ou...  19.3 us
    unnamed x22, local copies, waits for them, and re-layouts  9.64 us
    all_to_all x1, starting transfers between devices, local(): cut = lax.all_to_all(cut, 'dp', split_axis=0, concat_axis=0, tiled=True)  7.39 us
  transfers between devices with their start and end apart: 24, of which 12 were waited for; matrix products, arithmetic and copies ran while one was open for 0% of the time, Pallas kernels for 11%

profile of v5, /device:TPU:1, one launch (start us, length us, event | category | flops | bytes accessed | tf_op | source)
XLA Modules:
  0.0 140.0 jit_solution(10673286420950429054)
XLA Ops:
  7.2 3.3 %collective-permute-start = (bf16[3,7168,128]{2,1,0:T(8,128)(2,1)}, bf16[3,7168,128]{2,1,0:T(8,128)(2,1)}, u32[]{:S(2)}, u32[]{:S(2)}) collective-permute-start(bf16[3,7168,128]{2,1,0:T(8,128)(2,1)} %bitcast.9), channel_id=1, source_target_pairs={{0,1},{1,0},{2,3},{3,2},{4,5},{5,4},{6,7},{7,6},{8,9},{9,8},{10,11... | collective-permute-start | bytes 16515080 | tf_op jit(solution)/shard_map/ppermute | solution.py:36
  10.5 1.5 %copy-done.1 = bf16[128,7168]{1,0:T(8,128)(2,1)S(1)} copy-done((bf16[128,7168]{1,0:T(8,128)(2,1)S(1)}, bf16[128,7168]{1,0:T(8,128)(2,1)}, u32[]{:S(2)}) %copy-start.1) | copy-done | bytes 1835032
  12.0 1.5 %copy-done.2 = bf16[128,7168]{1,0:T(8,128)(2,1)S(1)} copy-done((bf16[128,7168]{1,0:T(8,128)(2,1)S(1)}, bf16[128,7168]{1,0:T(8,128)(2,1)}, u32[]{:S(2)}) %copy-start.2) | copy-done | bytes 1835032
  15.7 2.2 %collective-permute-start.2 = (bf16[8,14464]{1,0:T(8,128)(2,1)S(1)}, bf16[8,14464]{1,0:T(8,128)(2,1)S(1)}, u32[]{:S(2)}, u32[]{:S(2)}) collective-permute-start(bf16[8,14464]{1,0:T(8,128)(2,1)S(1)} %get-tuple-element.35), channel_id=1, source_target_pairs={{0,16},{1,17},{2,18},{3,19},{4,20},{5,21},{6,22},{7,23},{8,24},{9,... | collective-permute-start | bytes 694280 | tf_op jit(solution)/shard_map/ppermute | solution.py:36
  17.9 1.1 collective-permute-start.3
  18.9 5.6 %collective-permute-done.1.refs_1_ = bf16[8,14464]{1,0:T(8,128)(2,1)S(1)} collective-permute-done((bf16[8,14464]{1,0:T(8,128)(2,1)S(1)}, bf16[8,14464]{1,0:T(8,128)(2,1)S(1)}, u32[]{:S(2)}, u32[]{:S(2)}) %collective-permute-start.1) | collective-permute-done | bytes 231456 | tf_op jit(solution)/shard_map/ppermute | solution.py:36
  24.6 4.1 %collective-permute-done.2.refs_2_ = bf16[8,14464]{1,0:T(8,128)(2,1)S(1)} collective-permute-done((bf16[8,14464]{1,0:T(8,128)(2,1)S(1)}, bf16[8,14464]{1,0:T(8,128)(2,1)S(1)}, u32[]{:S(2)}, u32[]{:S(2)}) %collective-permute-start.2) | collective-permute-done | bytes 231456 | tf_op jit(solution)/shard_map/ppermute | solution.py:36
  30.0 2.3 %collective-permute-start.7 = (bf16[16,14464]{1,0:T(8,128)(2,1)S(1)}, bf16[16,14464]{1,0:T(8,128)(2,1)S(1)}, u32[]{:S(2)}, u32[]{:S(2)}) collective-permute-start(bf16[16,14464]{1,0:T(8,128)(2,1)S(1)} %get-tuple-element.38.refs_1_.bottom_ref), channel_id=1, source_target_pairs={{0,6},{1,7},{2,0},{3,1},{4,2},{5,3},{6,4},{7,5},{8,14},{9,15},{10,... | collective-permute-start | bytes 1388552 | tf_op jit(solution)/shard_map/ppermute | solution.py:36
  32.2 1.0 shard_map.81
  33.2 7.4 %all-to-all-start = ((bf16[8,64,896]{2,1,0:T(8,128)(2,1)}), bf16[8,64,896]{2,1,0:T(8,128)(2,1)S(1)}, u32[]{:S(2)}, u32[]{:S(2)}) async-start(bf16[8,64,896]{2,1,0:T(8,128)(2,1)} %bitcast.4), calls=%async_computation | async-start | bytes 1835008 | tf_op jit(solution)/shard_map/all_to_all | solution.py:294
  40.8 2.7 %collective-permute-start.6 = (bf16[16,14464]{1,0:T(8,128)(2,1)S(1)}, bf16[16,14464]{1,0:T(8,128)(2,1)S(1)}, u32[]{:S(2)}, u32[]{:S(2)}) collective-permute-start(bf16[16,14464]{1,0:T(8,128)(2,1)S(1)} %get-tuple-element.37.refs_0_.top_ref), channel_id=1, source_target_pairs={{0,6},{1,7},{2,0},{3,1},{4,2},{5,3},{6,4},{7,5},{8,14},{9,15},{10,... | collective-permute-start | bytes 1388552 | tf_op jit(solution)/shard_map/ppermute | solution.py:36
  43.4 2.7 %collective-permute-start.9 = (bf16[16,14464]{1,0:T(8,128)(2,1)S(1)}, bf16[16,14464]{1,0:T(8,128)(2,1)S(1)}, u32[]{:S(2)}, u32[]{:S(2)}) collective-permute-start(bf16[16,14464]{1,0:T(8,128)(2,1)S(1)} %collective-permute-done.7.refs_5_), channel_id=1, source_target_pairs={{0,6},{1,7},{2,0},{3,1},{4,2},{5,3},{6,4},{7,5},{8,14},{9,15},{10,... | collective-permute-start | bytes 1388552 | tf_op jit(solution)/shard_map/ppermute | solution.py:36
  46.1 6.3 %collective-permute-done.5.refs_3_ = bf16[16,14464]{1,0:T(8,128)(2,1)S(1)} collective-permute-done((bf16[16,14464]{1,0:T(8,128)(2,1)S(1)}, bf16[16,14464]{1,0:T(8,128)(2,1)S(1)}, u32[]{:S(2)}, u32[]{:S(2)}) %collective-permute-start.5) | collective-permute-done | bytes 462880 | tf_op jit(solution)/shard_map/ppermute | solution.py:36
  52.4 9.9 %collective-permute-done.8.refs_6_ = bf16[16,14464]{1,0:T(8,128)(2,1)S(1)} collective-permute-done((bf16[16,14464]{1,0:T(8,128)(2,1)S(1)}, bf16[16,14464]{1,0:T(8,128)(2,1)S(1)}, u32[]{:S(2)}, u32[]{:S(2)}) %collective-permute-start.8) | collective-permute-done | bytes 462880 | tf_op jit(solution)/shard_map/ppermute | solution.py:36
  62.3 5.4 %shard_map.78 = (bf16[128,768]{1,0:T(8,128)(2,1)}, bf16[128,128]{1,0:T(8,128)(2,1)S(1)}) custom-call(bf16[16,14464]{1,0:T(8,128)(2,1)S(1)} %get-tuple-element.37.refs_0_.top_ref, bf16[16,14464]{1,0:T(8,128)(2,1)S(1)} %get-tuple-element.38.refs_1_.bottom_ref, bf16[16,14464]{1,0:T(8,128)(2,1)S(1)} %collective-permute-done.4.refs_2_, ...), custom_call_target="tpu_custom_call" | custom-call | flops 1409286144 | bytes 14942208 | tf_op jit(solution)/shard_map/pallas_call | solution.py:49
  67.9 2.7 %collective-permute-start.13 = (bf16[512,896]{1,0:T(8,128)(2,1)S(1)}, bf16[512,896]{1,0:T(8,128)(2,1)S(1)}, u32[]{:S(2)}, u32[]{:S(2)}) collective-permute-start(bf16[512,896]{1,0:T(8,128)(2,1)S(1)} %bitcast.13), channel_id=1, source_target_pairs={{0,6},{1,7},{2,0},{3,1},{4,2},{5,3},{6,4},{7,5},{8,14},{9,15},{10,... | collective-permute-start | bytes 2752520 | tf_op jit(solution)/shard_map/ppermute | solution.py:36
  70.5 2.6 %copy-done = bf16[7168,3,128]{2,0,1:T(8,128)(2,1)S(1)} copy-done((bf16[7168,3,128]{2,0,1:T(8,128)(2,1)S(1)}, bf16[7168,3,128]{2,0,1:T(8,128)(2,1)}, u32[]{:S(2)}) %copy-start) | copy-done | bytes 5505048
  73.1 5.0 %shard_map.79 = (bf16[32,7296]{1,0:T(8,128)(2,1)S(1)}, bf16[32,7296]{1,0:T(8,128)(2,1)S(1)}, bf16[32,7296]{1,0:T(8,128)(2,1)S(1)}, bf16[16,7296]{1,0:T(8,128)(2,1)S(1)}, bf16[16,7296]{1,0:T(8,128)(2,1)S(1)}) custom-call(bf16[3,7168,128]{2,1,0:T(8,128)(2,1)S(1)} %bitcast.11, bf16[3,7168,128]{2,1,0:T(8,128)(2,1)} %collective-permute-done.refs_9_.refs_1_, ...), custom_call_target="tpu_custom_call" | custom-call | flops 939524096 | bytes 13107200 | tf_op jit(solution)/shard_map/pallas_call | solution.py:49
  78.1 1.3 collective-permute-start.10
  79.7 12.7 %collective-permute-done.10.top_ref = bf16[16,7296]{1,0:T(8,128)(2,1)S(1)} collective-permute-done((bf16[16,7296]{1,0:T(8,128)(2,1)S(1)}, bf16[16,7296]{1,0:T(8,128)(2,1)S(1)}, u32[]{:S(2)}, u32[]{:S(2)}) %collective-permute-start.10) | collective-permute-done | bytes 233504 | tf_op jit(solution)/shard_map/ppermute | solution.py:36
  92.4 1.0 collective-permute-done.11.bottom_ref
  93.6 2.5 %collective-permute-start.14 = (bf16[32,7296]{1,0:T(8,128)(2,1)S(1)}, bf16[32,7296]{1,0:T(8,128)(2,1)S(1)}, u32[]{:S(2)}, u32[]{:S(2)}) collective-permute-start(bf16[32,7296]{1,0:T(8,128)(2,1)S(1)} %get-tuple-element.48), channel_id=1, source_target_pairs={{0,6},{1,7},{2,0},{3,1},{4,2},{5,3},{6,4},{7,5},{8,14},{9,15},{10,... | collective-permute-start | bytes 1400840 | tf_op jit(solution)/shard_map/ppermute | solution.py:36
  96.1 6.5 %collective-permute-done.14.b_ref = bf16[32,7296]{1,0:T(8,128)(2,1)S(1)} collective-permute-done((bf16[32,7296]{1,0:T(8,128)(2,1)S(1)}, bf16[32,7296]{1,0:T(8,128)(2,1)S(1)}, u32[]{:S(2)}, u32[]{:S(2)}) %collective-permute-start.14) | collective-permute-done | bytes 466976 | tf_op jit(solution)/shard_map/ppermute | solution.py:36
  102.6 3.1 %collective-permute-done.15.c_ref = bf16[32,7296]{1,0:T(8,128)(2,1)S(1)} collective-permute-done((bf16[32,7296]{1,0:T(8,128)(2,1)S(1)}, bf16[32,7296]{1,0:T(8,128)(2,1)S(1)}, u32[]{:S(2)}, u32[]{:S(2)}) %collective-permute-start.15) | collective-permute-done | bytes 466976 | tf_op jit(solution)/shard_map/ppermute | solution.py:36
  106.8 2.7 %collective-permute-start.20 = (bf16[256,896]{1,0:T(8,128)(2,1)}, bf16[256,896]{1,0:T(8,128)(2,1)}, u32[]{:S(2)}, u32[]{:S(2)}) collective-permute-start(bf16[256,896]{1,0:T(8,128)(2,1)} %get-tuple-element.59), channel_id=1, source_target_pairs={{0,6},{1,7},{2,0},{3,1},{4,2},{5,3},{6,4},{7,5},{8,14},{9,15},{10,... | collective-permute-start | bytes 1376264 | tf_op jit(solution)/shard_map/ppermute | solution.py:36
  109.5 3.2 %collective-permute-start.16 = (bf16[8,7296]{1,0:T(8,128)(2,1)S(1)}, bf16[8,7296]{1,0:T(8,128)(2,1)S(1)}, u32[]{:S(2)}, u32[]{:S(2)}) collective-permute-start(bf16[8,7296]{1,0:T(8,128)(2,1)S(1)} %get-tuple-element.51), channel_id=1, source_target_pairs={{0,24},{1,25},{2,26},{3,27},{4,28},{5,29},{6,30},{7,31},{8,0},{9,1... | collective-permute-start | bytes 350216 | tf_op jit(solution)/shard_map/ppermute | solution.py:36
  113.2 2.4 %collective-permute-done.16.b1 = bf16[8,7296]{1,0:T(8,128)(2,1)S(1)} collective-permute-done((bf16[8,7296]{1,0:T(8,128)(2,1)S(1)}, bf16[8,7296]{1,0:T(8,128)(2,1)S(1)}, u32[]{:S(2)}, u32[]{:S(2)}) %collective-permute-start.16) | collective-permute-done | bytes 116768 | tf_op jit(solution)/shard_map/ppermute | solution.py:36
  115.7 2.3 %collective-permute-done.17.b2 = bf16[8,7296]{1,0:T(8,128)(2,1)S(1)} collective-permute-done((bf16[8,7296]{1,0:T(8,128)(2,1)S(1)}, bf16[8,7296]{1,0:T(8,128)(2,1)S(1)}, u32[]{:S(2)}, u32[]{:S(2)}) %collective-permute-start.17) | collective-permute-done | bytes 116768 | tf_op jit(solution)/shard_map/ppermute | solution.py:36
  119.7 1.4 copy-done.3
  121.2 2.7 %shard_map.85 = (f32[3,896,128]{2,1,0:T(8,128)S(1)}, bf16[3,896,128]{2,1,0:T(8,128)(2,1)S(1)}) custom-call(bf16[512,896]{1,0:T(8,128)(2,1)S(1)} %bitcast.14, bf16[512,896]{1,0:T(8,128)(2,1)S(1)} %collective-permute-done.12.left_ref.refs_1_, bf16[512,896]{1,0:T(8,128)(2,1)S(1)} %collective-permute-done.13.right_ref.refs_2_, ...), custom_call_target="tpu_custom_call" | custom-call | flops 1409286144 | bytes 7307264 | tf_op jit(solution)/shard_map/pallas_call | solution.py:49
  123.9 6.2 %collective-permute-start.21 = (bf16[3,896,128]{2,1,0:T(8,128)(2,1)S(1)}, bf16[3,896,128]{2,1,0:T(8,128)(2,1)S(1)}, u32[]{:S(2)}, u32[]{:S(2)}) collective-permute-start(bf16[3,896,128]{2,1,0:T(8,128)(2,1)S(1)} %get-tuple-element.62), channel_id=1, source_target_pairs={{0,1},{1,0},{2,3},{3,2},{4,5},{5,4},{6,7},{7,6},{8,9},{9,8},{10,11... | collective-permute-start | bytes 2064392 | tf_op jit(solution)/shard_map/ppermute | solution.py:36
  130.1 2.1 %shard_map.83 = (bf16[128,7168]{1,0:T(8,128)(2,1)}, f32[8,128]{1,0:T(8,128)}) custom-call(s32[1]{0:T(128)} %bitcast.y_ref, s32[8,128]{1,0:T(8,128)S(1)} %bitcast.17, bf16[8,7296]{1,0:T(8,128)(2,1)S(1)} %get-tuple-element.50.b0._, bf16[8,7296]{1,0:T(8,128)(2,1)S(1)} %collective-permute-done.16.b1, bf16[8,7296]{1,0:T(8,128)(2,1)S(1)} %copy-done.5, ...), custom_call_target="tpu_custom_call" | custom-call | bytes 2310148 | tf_op jit(solution)/shard_map/pallas_call | solution.py:49
  (50 shorter events, 8.7 us)
Async XLA Ops:
  7.2 55.2 %collective-permute-start = (bf16[3,7168,128]{2,1,0:T(8,128)(2,1)}, bf16[3,7168,128]{2,1,0:T(8,128)(2,1)}, u32[]{:S(2)}, u32[]{:S(2)}) collective-permute-start(bf16[3,7168,128]{2,1,0:T(8,128)(2,1)} %bitcast.9), channel_id=1, source_target_pairs={{0,1},{1,0},{2,3},{3,2},{4,5},{5,4},{6,7},{7,6},{8,9},{9,8},{10,11... | collective-permute-start | bytes 16515080 | tf_op jit(solution)/shard_map/ppermute | solution.py:36
  10.5 1.5 %copy-start.1 = (bf16[128,7168]{1,0:T(8,128)(2,1)S(1)}, bf16[128,7168]{1,0:T(8,128)(2,1)}, u32[]{:S(2)}) copy-start(bf16[128,7168]{1,0:T(8,128)(2,1)} %tok_ref.1) | copy-start | bytes 5505028
  12.0 1.5 %copy-start.2 = (bf16[128,7168]{1,0:T(8,128)(2,1)S(1)}, bf16[128,7168]{1,0:T(8,128)(2,1)}, u32[]{:S(2)}) copy-start(bf16[128,7168]{1,0:T(8,128)(2,1)} %cot_ref.1) | copy-start | bytes 5505028
  13.5 0.7 copy-start.8
  15.6 9.0 %collective-permute-start.1 = (bf16[8,14464]{1,0:T(8,128)(2,1)S(1)}, bf16[8,14464]{1,0:T(8,128)(2,1)S(1)}, u32[]{:S(2)}, u32[]{:S(2)}) collective-permute-start(bf16[8,14464]{1,0:T(8,128)(2,1)S(1)} %get-tuple-element.34), channel_id=1, source_target_pairs={{0,8},{1,9},{2,10},{3,11},{4,12},{5,13},{6,14},{7,15},{8,16},{9,17... | collective-permute-start | bytes 694280 | tf_op jit(solution)/shard_map/ppermute | solution.py:36
  15.7 13.0 %collective-permute-start.2 = (bf16[8,14464]{1,0:T(8,128)(2,1)S(1)}, bf16[8,14464]{1,0:T(8,128)(2,1)S(1)}, u32[]{:S(2)}, u32[]{:S(2)}) collective-permute-start(bf16[8,14464]{1,0:T(8,128)(2,1)S(1)} %get-tuple-element.35), channel_id=1, source_target_pairs={{0,16},{1,17},{2,18},{3,19},{4,20},{5,21},{6,22},{7,23},{8,24},{9,... | collective-permute-start | bytes 694280 | tf_op jit(solution)/shard_map/ppermute | solution.py:36
  17.9 11.5 %collective-permute-start.3 = (bf16[8,14464]{1,0:T(8,128)(2,1)S(1)}, bf16[8,14464]{1,0:T(8,128)(2,1)S(1)}, u32[]{:S(2)}, u32[]{:S(2)}) collective-permute-start(bf16[8,14464]{1,0:T(8,128)(2,1)S(1)} %get-tuple-element.36), channel_id=1, source_target_pairs={{0,24},{1,25},{2,26},{3,27},{4,28},{5,29},{6,30},{7,31},{8,0},{9,1... | collective-permute-start | bytes 694280 | tf_op jit(solution)/shard_map/ppermute | solution.py:36
  29.5 13.9 %collective-permute-start.4 = (bf16[16,14464]{1,0:T(8,128)(2,1)S(1)}, bf16[16,14464]{1,0:T(8,128)(2,1)S(1)}, u32[]{:S(2)}, u32[]{:S(2)}) collective-permute-start(bf16[16,14464]{1,0:T(8,128)(2,1)S(1)} %get-tuple-element.37.refs_0_.top_ref), channel_id=1, source_target_pairs={{0,2},{1,3},{2,4},{3,5},{4,6},{5,7},{6,0},{7,1},{8,10},{9,11},{10,... | collective-permute-start | bytes 1388552 | tf_op jit(solution)/shard_map/ppermute | solution.py:36
  30.0 13.5 %collective-permute-start.7 = (bf16[16,14464]{1,0:T(8,128)(2,1)S(1)}, bf16[16,14464]{1,0:T(8,128)(2,1)S(1)}, u32[]{:S(2)}, u32[]{:S(2)}) collective-permute-start(bf16[16,14464]{1,0:T(8,128)(2,1)S(1)} %get-tuple-element.38.refs_1_.bottom_ref), channel_id=1, source_target_pairs={{0,6},{1,7},{2,0},{3,1},{4,2},{5,3},{6,4},{7,5},{8,14},{9,15},{10,... | collective-permute-start | bytes 1388552 | tf_op jit(solution)/shard_map/ppermute | solution.py:36
  33.2 34.5 %all-to-all-start = ((bf16[8,64,896]{2,1,0:T(8,128)(2,1)}), bf16[8,64,896]{2,1,0:T(8,128)(2,1)S(1)}, u32[]{:S(2)}, u32[]{:S(2)}) async-start(bf16[8,64,896]{2,1,0:T(8,128)(2,1)} %bitcast.4), calls=%async_computation | async-start | bytes 1835008 | tf_op jit(solution)/shard_map/all_to_all | solution.py:294
  40.6 79.1 %all-gather.3.cloned.1.call-start = ((), (), s32[]{:S(2)}) async-start(), calls=%async_computation.1 | async-start | bytes 1769472 | tf_op jit(solution)/shard_map/all_gather | solution.py:326
  40.7 11.7 %collective-permute-start.5 = (bf16[16,14464]{1,0:T(8,128)(2,1)S(1)}, bf16[16,14464]{1,0:T(8,128)(2,1)S(1)}, u32[]{:S(2)}, u32[]{:S(2)}) collective-permute-start(bf16[16,14464]{1,0:T(8,128)(2,1)S(1)} %get-tuple-element.38.refs_1_.bottom_ref), channel_id=1, source_target_pairs={{0,2},{1,3},{2,4},{3,5},{4,6},{5,7},{6,0},{7,1},{8,10},{9,11},{10,... | collective-permute-start | bytes 1388552 | tf_op jit(solution)/shard_map/ppermute | solution.py:36
  40.8 11.6 %collective-permute-start.6 = (bf16[16,14464]{1,0:T(8,128)(2,1)S(1)}, bf16[16,14464]{1,0:T(8,128)(2,1)S(1)}, u32[]{:S(2)}, u32[]{:S(2)}) collective-permute-start(bf16[16,14464]{1,0:T(8,128)(2,1)S(1)} %get-tuple-element.37.refs_0_.top_ref), channel_id=1, source_target_pairs={{0,6},{1,7},{2,0},{3,1},{4,2},{5,3},{6,4},{7,5},{8,14},{9,15},{10,... | collective-permute-start | bytes 1388552 | tf_op jit(solution)/shard_map/ppermute | solution.py:36
  43.4 18.9 %collective-permute-start.8 = (bf16[16,14464]{1,0:T(8,128)(2,1)S(1)}, bf16[16,14464]{1,0:T(8,128)(2,1)S(1)}, u32[]{:S(2)}, u32[]{:S(2)}) collective-permute-start(bf16[16,14464]{1,0:T(8,128)(2,1)S(1)} %collective-permute-done.4.refs_2_), channel_id=1, source_target_pairs={{0,2},{1,3},{2,4},{3,5},{4,6},{5,7},{6,0},{7,1},{8,10},{9,11},{10,... | collective-permute-start | bytes 1388552 | tf_op jit(solution)/shard_map/ppermute | solution.py:36
  43.4 18.9 %collective-permute-start.9 = (bf16[16,14464]{1,0:T(8,128)(2,1)S(1)}, bf16[16,14464]{1,0:T(8,128)(2,1)S(1)}, u32[]{:S(2)}, u32[]{:S(2)}) collective-permute-start(bf16[16,14464]{1,0:T(8,128)(2,1)S(1)} %collective-permute-done.7.refs_5_), channel_id=1, source_target_pairs={{0,6},{1,7},{2,0},{3,1},{4,2},{5,3},{6,4},{7,5},{8,14},{9,15},{10,... | collective-permute-start | bytes 1388552 | tf_op jit(solution)/shard_map/ppermute | solution.py:36
  67.8 25.8 %collective-permute-start.12 = (bf16[512,896]{1,0:T(8,128)(2,1)S(1)}, bf16[512,896]{1,0:T(8,128)(2,1)S(1)}, u32[]{:S(2)}, u32[]{:S(2)}) collective-permute-start(bf16[512,896]{1,0:T(8,128)(2,1)S(1)} %bitcast.12), channel_id=1, source_target_pairs={{0,2},{1,3},{2,4},{3,5},{4,6},{5,7},{6,0},{7,1},{8,10},{9,11},{10,... | collective-permute-start | bytes 2752520 | tf_op jit(solution)/shard_map/ppermute | solution.py:36
  67.9 25.7 %collective-permute-start.13 = (bf16[512,896]{1,0:T(8,128)(2,1)S(1)}, bf16[512,896]{1,0:T(8,128)(2,1)S(1)}, u32[]{:S(2)}, u32[]{:S(2)}) collective-permute-start(bf16[512,896]{1,0:T(8,128)(2,1)S(1)} %bitcast.13), channel_id=1, source_target_pairs={{0,6},{1,7},{2,0},{3,1},{4,2},{5,3},{6,4},{7,5},{8,14},{9,15},{10,... | collective-permute-start | bytes 2752520 | tf_op jit(solution)/shard_map/ppermute | solution.py:36
  70.5 2.6 %copy-start = (bf16[7168,3,128]{2,0,1:T(8,128)(2,1)S(1)}, bf16[7168,3,128]{2,0,1:T(8,128)(2,1)}, u32[]{:S(2)}) copy-start(bf16[7168,3,128]{2,0,1:T(8,128)(2,1)} %param.9) | copy-start | bytes 16515076
  78.1 14.3 %collective-permute-start.10 = (bf16[16,7296]{1,0:T(8,128)(2,1)S(1)}, bf16[16,7296]{1,0:T(8,128)(2,1)S(1)}, u32[]{:S(2)}, u32[]{:S(2)}) collective-permute-start(bf16[16,7296]{1,0:T(8,128)(2,1)S(1)} %get-tuple-element.44), channel_id=1, source_target_pairs={{0,6},{1,7},{2,0},{3,1},{4,2},{5,3},{6,4},{7,5},{8,14},{9,15},{10,... | collective-permute-start | bytes 700424 | tf_op jit(solution)/shard_map/ppermute | solution.py:36
  79.4 14.0 %collective-permute-start.11 = (bf16[16,7296]{1,0:T(8,128)(2,1)S(1)}, bf16[16,7296]{1,0:T(8,128)(2,1)S(1)}, u32[]{:S(2)}, u32[]{:S(2)}) collective-permute-start(bf16[16,7296]{1,0:T(8,128)(2,1)S(1)} %get-tuple-element.45), channel_id=1, source_target_pairs={{0,2},{1,3},{2,4},{3,5},{4,6},{5,7},{6,0},{7,1},{8,10},{9,11},{10,... | collective-permute-start | bytes 700424 | tf_op jit(solution)/shard_map/ppermute | solution.py:36
  93.6 9.0 %collective-permute-start.14 = (bf16[32,7296]{1,0:T(8,128)(2,1)S(1)}, bf16[32,7296]{1,0:T(8,128)(2,1)S(1)}, u32[]{:S(2)}, u32[]{:S(2)}) collective-permute-start(bf16[32,7296]{1,0:T(8,128)(2,1)S(1)} %get-tuple-element.48), channel_id=1, source_target_pairs={{0,6},{1,7},{2,0},{3,1},{4,2},{5,3},{6,4},{7,5},{8,14},{9,15},{10,... | collective-permute-start | bytes 1400840 | tf_op jit(solution)/shard_map/ppermute | solution.py:36
  96.1 9.5 %collective-permute-start.15 = (bf16[32,7296]{1,0:T(8,128)(2,1)S(1)}, bf16[32,7296]{1,0:T(8,128)(2,1)S(1)}, u32[]{:S(2)}, u32[]{:S(2)}) collective-permute-start(bf16[32,7296]{1,0:T(8,128)(2,1)S(1)} %get-tuple-element.49), channel_id=1, source_target_pairs={{0,2},{1,3},{2,4},{3,5},{4,6},{5,7},{6,0},{7,1},{8,10},{9,11},{10,... | collective-permute-start | bytes 1400840 | tf_op jit(solution)/shard_map/ppermute | solution.py:36
  106.8 12.9 %collective-permute-start.19 = (bf16[256,896]{1,0:T(8,128)(2,1)}, bf16[256,896]{1,0:T(8,128)(2,1)S(1)}, u32[]{:S(2)}, u32[]{:S(2)}) collective-permute-start(bf16[256,896]{1,0:T(8,128)(2,1)} %get-tuple-element.58), channel_id=1, source_target_pairs={{0,2},{1,3},{2,4},{3,5},{4,6},{5,7},{6,0},{7,1},{8,10},{9,11},{10,... | collective-permute-start | bytes 1376264 | tf_op jit(solution)/shard_map/ppermute | solution.py:36
  106.8 12.9 %collective-permute-start.20 = (bf16[256,896]{1,0:T(8,128)(2,1)}, bf16[256,896]{1,0:T(8,128)(2,1)}, u32[]{:S(2)}, u32[]{:S(2)}) collective-permute-start(bf16[256,896]{1,0:T(8,128)(2,1)} %get-tuple-element.59), channel_id=1, source_target_pairs={{0,6},{1,7},{2,0},{3,1},{4,2},{5,3},{6,4},{7,5},{8,14},{9,15},{10,... | collective-permute-start | bytes 1376264 | tf_op jit(solution)/shard_map/ppermute | solution.py:36
  109.5 6.2 %collective-permute-start.16 = (bf16[8,7296]{1,0:T(8,128)(2,1)S(1)}, bf16[8,7296]{1,0:T(8,128)(2,1)S(1)}, u32[]{:S(2)}, u32[]{:S(2)}) collective-permute-start(bf16[8,7296]{1,0:T(8,128)(2,1)S(1)} %get-tuple-element.51), channel_id=1, source_target_pairs={{0,24},{1,25},{2,26},{3,27},{4,28},{5,29},{6,30},{7,31},{8,0},{9,1... | collective-permute-start | bytes 350216 | tf_op jit(solution)/shard_map/ppermute | solution.py:36
  112.7 5.3 %collective-permute-start.17 = (bf16[8,7296]{1,0:T(8,128)(2,1)S(1)}, bf16[8,7296]{1,0:T(8,128)(2,1)S(1)}, u32[]{:S(2)}, u32[]{:S(2)}) collective-permute-start(bf16[8,7296]{1,0:T(8,128)(2,1)S(1)} %get-tuple-element.52), channel_id=1, source_target_pairs={{0,16},{1,17},{2,18},{3,19},{4,20},{5,21},{6,22},{7,23},{8,24},{9,... | collective-permute-start | bytes 350216 | tf_op jit(solution)/shard_map/ppermute | solution.py:36
  112.7 6.4 %collective-permute-start.18 = (bf16[8,7296]{1,0:T(8,128)(2,1)S(1)}, bf16[8,7296]{1,0:T(8,128)(2,1)S(1)}, u32[]{:S(2)}, u32[]{:S(2)}) collective-permute-start(bf16[8,7296]{1,0:T(8,128)(2,1)S(1)} %get-tuple-element.53), channel_id=1, source_target_pairs={{0,8},{1,9},{2,10},{3,11},{4,12},{5,13},{6,14},{7,15},{8,16},{9,17... | collective-permute-start | bytes 350216 | tf_op jit(solution)/shard_map/ppermute | solution.py:36
  119.7 1.4 %copy-start.3 = (bf16[1024,768]{1,0:T(8,128)(2,1)S(1)}, bf16[1024,768]{1,0:T(8,128)(2,1)}, u32[]{:S(2)}) copy-start(bf16[1024,768]{1,0:T(8,128)(2,1)} %all-gather.3.cloned.1.call-done) | copy-start | bytes 4718596
  121.1 9.0 %copy-start.5 = (bf16[8,7296]{1,0:T(8,128)(2,1)S(1)}, bf16[8,7296]{1,0:T(8,128)(2,1)}, u32[]{:S(2)}) copy-start(bf16[8,7296]{1,0:T(8,128)(2,1)} %copy-done.4) | copy-start | bytes 350212
  121.1 9.0 %copy-start.7 = (bf16[8,7296]{1,0:T(8,128)(2,1)S(1)}, bf16[8,7296]{1,0:T(8,128)(2,1)}, u32[]{:S(2)}) copy-start(bf16[8,7296]{1,0:T(8,128)(2,1)} %copy-done.6) | copy-start | bytes 350212
  121.1 9.0 %copy-start.9 = (s32[128,8]{0,1:T(8,128)S(1)}, s32[128,8]{0,1:T(8,128)}, u32[]{:S(2)}) copy-start(s32[128,8]{0,1:T(8,128)} %param.7) | copy-start | bytes 12292
  123.9 8.3 %collective-permute-start.21 = (bf16[3,896,128]{2,1,0:T(8,128)(2,1)S(1)}, bf16[3,896,128]{2,1,0:T(8,128)(2,1)S(1)}, u32[]{:S(2)}, u32[]{:S(2)}) collective-permute-start(bf16[3,896,128]{2,1,0:T(8,128)(2,1)S(1)} %get-tuple-element.62), channel_id=1, source_target_pairs={{0,1},{1,0},{2,3},{3,2},{4,5},{5,4},{6,7},{7,6},{8,9},{9,8},{10,11... | collective-permute-start | bytes 2064392 | tf_op jit(solution)/shard_map/ppermute | solution.py:36
  (3 other events, 2.0 us)
Sparse Core Ops, SparseCore 0:
  67.9 38.6 all-gather.2

commit v6 on v5

--- a/solution.py
+++ b/solution.py
@@ -348,6 +348,7 @@
         [((3, piece, hidden), F32), ((3, piece, hidden), BF16)],
         [*cuts, g_all],
         flops=3 * work,
+        limit=52,
     )
     d_weights = call(add_cores, [((3, piece, hidden), BF16)], [d_mine, send(d_other, dc=1)])[0]
     return d_tokens, d_rw.T, jnp.transpose(d_weights, (1, 0, 2))

time: 140 us -> 142 us (1.014)
  Pallas kernels: 19.3 us -> 21.6 us
    pallas_call x11, Pallas kernels: 19.3 us -> 21.6 us  [call(): pl.pallas_call(body, out_shape=[jax.ShapeDtypeStruct(s, d) for s, d in ou...]
    unnamed x22 -> x20, local copies, waits for them, and re-layouts: 9.64 us -> 8.28 us
where the time goes in v6:
time: 142 us; the launch traced here: 141 us
  waiting for transfers between devices  55.9 us (39%)
  starting transfers between devices  41.6 us (29%)
  Pallas kernels  21.6 us (15%)
  between operations  14.2 us (10%)
  local copies, waits for them, and re-layouts  8.28 us (6%)
    ppermute x22, waiting for transfers between devices, send(): return lax.ppermute(array, 'expert', shifted(dy, dx, dc))  55.8 us
    ppermute x22, starting transfers between devices, send(): return lax.ppermute(array, 'expert', shifted(dy, dx, dc))  34.2 us
    pallas_call x11, Pallas kernels, call(): pl.pallas_call(body, out_shape=[jax.ShapeDtypeStruct(s, d) for s, d in ou...  21.6 us
    unnamed x20, local copies, waits for them, and re-layouts  8.28 us
    all_to_all x1, starting transfers between devices, local(): cut = lax.all_to_all(cut, 'dp', split_axis=0, concat_axis=0, tiled=True)  7.39 us
  transfers between devices with their start and end apart: 24, of which 12 were waited for; matrix products, arithmetic and copies ran while one was open for 0% of the time, Pallas kernels for 11%

profile of v6, /device:TPU:1, one launch (start us, length us, event | category | flops | bytes accessed | tf_op | source)
XLA Modules:
  0.0 141.5 jit_solution(590994258243479917)
XLA Ops:
  7.2 3.3 %collective-permute-start = (bf16[3,7168,128]{2,1,0:T(8,128)(2,1)}, bf16[3,7168,128]{2,1,0:T(8,128)(2,1)}, u32[]{:S(2)}, u32[]{:S(2)}) collective-permute-start(bf16[3,7168,128]{2,1,0:T(8,128)(2,1)} %bitcast.9), channel_id=1, source_target_pairs={{0,1},{1,0},{2,3},{3,2},{4,5},{5,4},{6,7},{7,6},{8,9},{9,8},{10,11... | collective-permute-start | bytes 16515080 | tf_op jit(solution)/shard_map/ppermute | solution.py:36
  10.5 1.5 %copy-done.3 = bf16[128,7168]{1,0:T(8,128)(2,1)S(1)} copy-done((bf16[128,7168]{1,0:T(8,128)(2,1)S(1)}, bf16[128,7168]{1,0:T(8,128)(2,1)}, u32[]{:S(2)}) %copy-start.3) | copy-done | bytes 1835032
  12.0 1.5 %copy-done.4 = bf16[128,7168]{1,0:T(8,128)(2,1)S(1)} copy-done((bf16[128,7168]{1,0:T(8,128)(2,1)S(1)}, bf16[128,7168]{1,0:T(8,128)(2,1)}, u32[]{:S(2)}) %copy-start.4) | copy-done | bytes 1835032
  15.7 2.2 %collective-permute-start.2 = (bf16[8,14464]{1,0:T(8,128)(2,1)S(1)}, bf16[8,14464]{1,0:T(8,128)(2,1)S(1)}, u32[]{:S(2)}, u32[]{:S(2)}) collective-permute-start(bf16[8,14464]{1,0:T(8,128)(2,1)S(1)} %get-tuple-element.35), channel_id=1, source_target_pairs={{0,16},{1,17},{2,18},{3,19},{4,20},{5,21},{6,22},{7,23},{8,24},{9,... | collective-permute-start | bytes 694280 | tf_op jit(solution)/shard_map/ppermute | solution.py:36
  17.9 1.1 collective-permute-start.3
  18.9 5.6 %collective-permute-done.1.refs_1_ = bf16[8,14464]{1,0:T(8,128)(2,1)S(1)} collective-permute-done((bf16[8,14464]{1,0:T(8,128)(2,1)S(1)}, bf16[8,14464]{1,0:T(8,128)(2,1)S(1)}, u32[]{:S(2)}, u32[]{:S(2)}) %collective-permute-start.1) | collective-permute-done | bytes 231456 | tf_op jit(solution)/shard_map/ppermute | solution.py:36
  24.6 4.1 %collective-permute-done.2.refs_2_ = bf16[8,14464]{1,0:T(8,128)(2,1)S(1)} collective-permute-done((bf16[8,14464]{1,0:T(8,128)(2,1)S(1)}, bf16[8,14464]{1,0:T(8,128)(2,1)S(1)}, u32[]{:S(2)}, u32[]{:S(2)}) %collective-permute-start.2) | collective-permute-done | bytes 231456 | tf_op jit(solution)/shard_map/ppermute | solution.py:36
  30.0 2.3 %collective-permute-start.7 = (bf16[16,14464]{1,0:T(8,128)(2,1)S(1)}, bf16[16,14464]{1,0:T(8,128)(2,1)S(1)}, u32[]{:S(2)}, u32[]{:S(2)}) collective-permute-start(bf16[16,14464]{1,0:T(8,128)(2,1)S(1)} %get-tuple-element.38.refs_1_.bottom_ref), channel_id=1, source_target_pairs={{0,6},{1,7},{2,0},{3,1},{4,2},{5,3},{6,4},{7,5},{8,14},{9,15},{10,... | collective-permute-start | bytes 1388552 | tf_op jit(solution)/shard_map/ppermute | solution.py:36
  33.2 7.4 %all-to-all-start = ((bf16[8,64,896]{2,1,0:T(8,128)(2,1)}), bf16[8,64,896]{2,1,0:T(8,128)(2,1)S(1)}, u32[]{:S(2)}, u32[]{:S(2)}) async-start(bf16[8,64,896]{2,1,0:T(8,128)(2,1)} %bitcast.4), calls=%async_computation | async-start | bytes 1835008 | tf_op jit(solution)/shard_map/all_to_all | solution.py:294
  40.8 2.7 %collective-permute-start.6 = (bf16[16,14464]{1,0:T(8,128)(2,1)S(1)}, bf16[16,14464]{1,0:T(8,128)(2,1)S(1)}, u32[]{:S(2)}, u32[]{:S(2)}) collective-permute-start(bf16[16,14464]{1,0:T(8,128)(2,1)S(1)} %get-tuple-element.37.refs_0_.top_ref), channel_id=1, source_target_pairs={{0,6},{1,7},{2,0},{3,1},{4,2},{5,3},{6,4},{7,5},{8,14},{9,15},{10,... | collective-permute-start | bytes 1388552 | tf_op jit(solution)/shard_map/ppermute | solution.py:36
  43.4 2.7 %collective-permute-start.9 = (bf16[16,14464]{1,0:T(8,128)(2,1)S(1)}, bf16[16,14464]{1,0:T(8,128)(2,1)S(1)}, u32[]{:S(2)}, u32[]{:S(2)}) collective-permute-start(bf16[16,14464]{1,0:T(8,128)(2,1)S(1)} %collective-permute-done.7.refs_5_), channel_id=1, source_target_pairs={{0,6},{1,7},{2,0},{3,1},{4,2},{5,3},{6,4},{7,5},{8,14},{9,15},{10,... | collective-permute-start | bytes 1388552 | tf_op jit(solution)/shard_map/ppermute | solution.py:36
  46.1 6.3 %collective-permute-done.5.refs_3_ = bf16[16,14464]{1,0:T(8,128)(2,1)S(1)} collective-permute-done((bf16[16,14464]{1,0:T(8,128)(2,1)S(1)}, bf16[16,14464]{1,0:T(8,128)(2,1)S(1)}, u32[]{:S(2)}, u32[]{:S(2)}) %collective-permute-start.5) | collective-permute-done | bytes 462880 | tf_op jit(solution)/shard_map/ppermute | solution.py:36
  52.4 9.9 %collective-permute-done.8.refs_6_ = bf16[16,14464]{1,0:T(8,128)(2,1)S(1)} collective-permute-done((bf16[16,14464]{1,0:T(8,128)(2,1)S(1)}, bf16[16,14464]{1,0:T(8,128)(2,1)S(1)}, u32[]{:S(2)}, u32[]{:S(2)}) %collective-permute-start.8) | collective-permute-done | bytes 462880 | tf_op jit(solution)/shard_map/ppermute | solution.py:36
  62.3 5.4 %shard_map.78 = (bf16[128,768]{1,0:T(8,128)(2,1)}, bf16[128,128]{1,0:T(8,128)(2,1)S(1)}) custom-call(bf16[16,14464]{1,0:T(8,128)(2,1)S(1)} %get-tuple-element.37.refs_0_.top_ref, bf16[16,14464]{1,0:T(8,128)(2,1)S(1)} %get-tuple-element.38.refs_1_.bottom_ref, bf16[16,14464]{1,0:T(8,128)(2,1)S(1)} %collective-permute-done.4.refs_2_, ...), custom_call_target="tpu_custom_call" | custom-call | flops 1409286144 | bytes 14942208 | tf_op jit(solution)/shard_map/pallas_call | solution.py:49
  67.9 2.7 %collective-permute-start.13 = (bf16[512,896]{1,0:T(8,128)(2,1)S(1)}, bf16[512,896]{1,0:T(8,128)(2,1)S(1)}, u32[]{:S(2)}, u32[]{:S(2)}) collective-permute-start(bf16[512,896]{1,0:T(8,128)(2,1)S(1)} %bitcast.16), channel_id=1, source_target_pairs={{0,6},{1,7},{2,0},{3,1},{4,2},{5,3},{6,4},{7,5},{8,14},{9,15},{10,... | collective-permute-start | bytes 2752520 | tf_op jit(solution)/shard_map/ppermute | solution.py:36
  70.5 2.6 %copy-done = bf16[7168,3,128]{2,0,1:T(8,128)(2,1)S(1)} copy-done((bf16[7168,3,128]{2,0,1:T(8,128)(2,1)S(1)}, bf16[7168,3,128]{2,0,1:T(8,128)(2,1)}, u32[]{:S(2)}) %copy-start) | copy-done | bytes 5505048
  73.1 5.0 %shard_map.79 = (bf16[32,7296]{1,0:T(8,128)(2,1)S(1)}, bf16[32,7296]{1,0:T(8,128)(2,1)S(1)}, bf16[32,7296]{1,0:T(8,128)(2,1)S(1)}, bf16[16,7296]{1,0:T(8,128)(2,1)S(1)}, bf16[16,7296]{1,0:T(8,128)(2,1)S(1)}) custom-call(bf16[3,7168,128]{2,1,0:T(8,128)(2,1)S(1)} %bitcast.11, bf16[3,7168,128]{2,1,0:T(8,128)(2,1)} %collective-permute-done.refs_9_.refs_1_, ...), custom_call_target="tpu_custom_call" | custom-call | flops 939524096 | bytes 13107200 | tf_op jit(solution)/shard_map/pallas_call | solution.py:49
  78.1 1.3 collective-permute-start.10
  79.7 12.7 %collective-permute-done.10.top_ref = bf16[16,7296]{1,0:T(8,128)(2,1)S(1)} collective-permute-done((bf16[16,7296]{1,0:T(8,128)(2,1)S(1)}, bf16[16,7296]{1,0:T(8,128)(2,1)S(1)}, u32[]{:S(2)}, u32[]{:S(2)}) %collective-permute-start.10) | collective-permute-done | bytes 233504 | tf_op jit(solution)/shard_map/ppermute | solution.py:36
  92.4 1.0 collective-permute-done.11.bottom_ref
  93.6 2.5 %collective-permute-start.14 = (bf16[32,7296]{1,0:T(8,128)(2,1)S(1)}, bf16[32,7296]{1,0:T(8,128)(2,1)S(1)}, u32[]{:S(2)}, u32[]{:S(2)}) collective-permute-start(bf16[32,7296]{1,0:T(8,128)(2,1)S(1)} %get-tuple-element.48), channel_id=1, source_target_pairs={{0,6},{1,7},{2,0},{3,1},{4,2},{5,3},{6,4},{7,5},{8,14},{9,15},{10,... | collective-permute-start | bytes 1400840 | tf_op jit(solution)/shard_map/ppermute | solution.py:36
  96.1 6.5 %collective-permute-done.14.b_ref = bf16[32,7296]{1,0:T(8,128)(2,1)S(1)} collective-permute-done((bf16[32,7296]{1,0:T(8,128)(2,1)S(1)}, bf16[32,7296]{1,0:T(8,128)(2,1)S(1)}, u32[]{:S(2)}, u32[]{:S(2)}) %collective-permute-start.14) | collective-permute-done | bytes 466976 | tf_op jit(solution)/shard_map/ppermute | solution.py:36
  102.6 3.1 %collective-permute-done.15.c_ref = bf16[32,7296]{1,0:T(8,128)(2,1)S(1)} collective-permute-done((bf16[32,7296]{1,0:T(8,128)(2,1)S(1)}, bf16[32,7296]{1,0:T(8,128)(2,1)S(1)}, u32[]{:S(2)}, u32[]{:S(2)}) %collective-permute-start.15) | collective-permute-done | bytes 466976 | tf_op jit(solution)/shard_map/ppermute | solution.py:36
  106.8 2.7 %collective-permute-start.20 = (bf16[256,896]{1,0:T(8,128)(2,1)}, bf16[256,896]{1,0:T(8,128)(2,1)S(1)}, u32[]{:S(2)}, u32[]{:S(2)}) collective-permute-start(bf16[256,896]{1,0:T(8,128)(2,1)} %get-tuple-element.59), channel_id=1, source_target_pairs={{0,6},{1,7},{2,0},{3,1},{4,2},{5,3},{6,4},{7,5},{8,14},{9,15},{10,... | collective-permute-start | bytes 1376264 | tf_op jit(solution)/shard_map/ppermute | solution.py:36
  109.5 3.2 %collective-permute-start.16 = (bf16[8,7296]{1,0:T(8,128)(2,1)S(1)}, bf16[8,7296]{1,0:T(8,128)(2,1)S(1)}, u32[]{:S(2)}, u32[]{:S(2)}) collective-permute-start(bf16[8,7296]{1,0:T(8,128)(2,1)S(1)} %get-tuple-element.51), channel_id=1, source_target_pairs={{0,24},{1,25},{2,26},{3,27},{4,28},{5,29},{6,30},{7,31},{8,0},{9,1... | collective-permute-start | bytes 350216 | tf_op jit(solution)/shard_map/ppermute | solution.py:36
  113.2 2.4 %collective-permute-done.16.b1 = bf16[8,7296]{1,0:T(8,128)(2,1)S(1)} collective-permute-done((bf16[8,7296]{1,0:T(8,128)(2,1)S(1)}, bf16[8,7296]{1,0:T(8,128)(2,1)S(1)}, u32[]{:S(2)}, u32[]{:S(2)}) %collective-permute-start.16) | collective-permute-done | bytes 116768 | tf_op jit(solution)/shard_map/ppermute | solution.py:36
  115.7 2.3 %collective-permute-done.17.b2 = bf16[8,7296]{1,0:T(8,128)(2,1)S(1)} collective-permute-done((bf16[8,7296]{1,0:T(8,128)(2,1)S(1)}, bf16[8,7296]{1,0:T(8,128)(2,1)S(1)}, u32[]{:S(2)}, u32[]{:S(2)}) %collective-permute-start.17) | collective-permute-done | bytes 116768 | tf_op jit(solution)/shard_map/ppermute | solution.py:36
  117.9 1.1 collective-permute-done.18.b3
  119.1 5.0 %shard_map.85 = (f32[3,896,128]{2,1,0:T(8,128)}, bf16[3,896,128]{2,1,0:T(8,128)(2,1)S(1)}) custom-call(bf16[512,896]{1,0:T(8,128)(2,1)} %bitcast.17, bf16[512,896]{1,0:T(8,128)(2,1)} %copy-done.1, bf16[512,896]{1,0:T(8,128)(2,1)} %copy-done.2, bf16[256,896]{1,0:T(8,128)(2,1)S(1)} %collective-permute-done.19.refs_3_, ...), custom_call_target="tpu_custom_call" | custom-call | flops 1409286144 | bytes 7307264 | tf_op jit(solution)/shard_map/pallas_call | solution.py:49
  124.1 6.1 %collective-permute-start.21 = (bf16[3,896,128]{2,1,0:T(8,128)(2,1)S(1)}, bf16[3,896,128]{2,1,0:T(8,128)(2,1)S(1)}, u32[]{:S(2)}, u32[]{:S(2)}) collective-permute-start(bf16[3,896,128]{2,1,0:T(8,128)(2,1)S(1)} %get-tuple-element.62), channel_id=1, source_target_pairs={{0,1},{1,0},{2,3},{3,2},{4,5},{5,4},{6,7},{7,6},{8,9},{9,8},{10,11... | collective-permute-start | bytes 2064392 | tf_op jit(solution)/shard_map/ppermute | solution.py:36
  130.3 2.0 %shard_map.83 = (bf16[128,7168]{1,0:T(8,128)(2,1)}, f32[8,128]{1,0:T(8,128)}) custom-call(s32[1]{0:T(128)} %bitcast.y_ref, s32[8,128]{1,0:T(8,128)S(1)} %bitcast.13, bf16[8,7296]{1,0:T(8,128)(2,1)S(1)} %get-tuple-element.50.b0._, bf16[8,7296]{1,0:T(8,128)(2,1)S(1)} %collective-permute-done.16.b1, bf16[8,7296]{1,0:T(8,128)(2,1)S(1)} %collective-permute-done.17.b2, ...), custom_call_target="tpu_custom_call" | custom-call | bytes 2310148 | tf_op jit(solution)/shard_map/pallas_call | solution.py:49
  132.4 1.3 copy-done.5
  (48 shorter events, 7.9 us)
Async XLA Ops:
  7.2 55.2 %collective-permute-start = (bf16[3,7168,128]{2,1,0:T(8,128)(2,1)}, bf16[3,7168,128]{2,1,0:T(8,128)(2,1)}, u32[]{:S(2)}, u32[]{:S(2)}) collective-permute-start(bf16[3,7168,128]{2,1,0:T(8,128)(2,1)} %bitcast.9), channel_id=1, source_target_pairs={{0,1},{1,0},{2,3},{3,2},{4,5},{5,4},{6,7},{7,6},{8,9},{9,8},{10,11... | collective-permute-start | bytes 16515080 | tf_op jit(solution)/shard_map/ppermute | solution.py:36
  10.5 1.5 %copy-start.3 = (bf16[128,7168]{1,0:T(8,128)(2,1)S(1)}, bf16[128,7168]{1,0:T(8,128)(2,1)}, u32[]{:S(2)}) copy-start(bf16[128,7168]{1,0:T(8,128)(2,1)} %tok_ref.1) | copy-start | bytes 5505028
  12.0 1.5 %copy-start.4 = (bf16[128,7168]{1,0:T(8,128)(2,1)S(1)}, bf16[128,7168]{1,0:T(8,128)(2,1)}, u32[]{:S(2)}) copy-start(bf16[128,7168]{1,0:T(8,128)(2,1)} %cot_ref.1) | copy-start | bytes 5505028
  15.6 9.0 %collective-permute-start.1 = (bf16[8,14464]{1,0:T(8,128)(2,1)S(1)}, bf16[8,14464]{1,0:T(8,128)(2,1)S(1)}, u32[]{:S(2)}, u32[]{:S(2)}) collective-permute-start(bf16[8,14464]{1,0:T(8,128)(2,1)S(1)} %get-tuple-element.34), channel_id=1, source_target_pairs={{0,8},{1,9},{2,10},{3,11},{4,12},{5,13},{6,14},{7,15},{8,16},{9,17... | collective-permute-start | bytes 694280 | tf_op jit(solution)/shard_map/ppermute | solution.py:36
  15.7 13.0 %collective-permute-start.2 = (bf16[8,14464]{1,0:T(8,128)(2,1)S(1)}, bf16[8,14464]{1,0:T(8,128)(2,1)S(1)}, u32[]{:S(2)}, u32[]{:S(2)}) collective-permute-start(bf16[8,14464]{1,0:T(8,128)(2,1)S(1)} %get-tuple-element.35), channel_id=1, source_target_pairs={{0,16},{1,17},{2,18},{3,19},{4,20},{5,21},{6,22},{7,23},{8,24},{9,... | collective-permute-start | bytes 694280 | tf_op jit(solution)/shard_map/ppermute | solution.py:36
  17.9 11.5 %collective-permute-start.3 = (bf16[8,14464]{1,0:T(8,128)(2,1)S(1)}, bf16[8,14464]{1,0:T(8,128)(2,1)S(1)}, u32[]{:S(2)}, u32[]{:S(2)}) collective-permute-start(bf16[8,14464]{1,0:T(8,128)(2,1)S(1)} %get-tuple-element.36), channel_id=1, source_target_pairs={{0,24},{1,25},{2,26},{3,27},{4,28},{5,29},{6,30},{7,31},{8,0},{9,1... | collective-permute-start | bytes 694280 | tf_op jit(solution)/shard_map/ppermute | solution.py:36
  29.5 13.9 %collective-permute-start.4 = (bf16[16,14464]{1,0:T(8,128)(2,1)S(1)}, bf16[16,14464]{1,0:T(8,128)(2,1)S(1)}, u32[]{:S(2)}, u32[]{:S(2)}) collective-permute-start(bf16[16,14464]{1,0:T(8,128)(2,1)S(1)} %get-tuple-element.37.refs_0_.top_ref), channel_id=1, source_target_pairs={{0,2},{1,3},{2,4},{3,5},{4,6},{5,7},{6,0},{7,1},{8,10},{9,11},{10,... | collective-permute-start | bytes 1388552 | tf_op jit(solution)/shard_map/ppermute | solution.py:36
  30.0 13.5 %collective-permute-start.7 = (bf16[16,14464]{1,0:T(8,128)(2,1)S(1)}, bf16[16,14464]{1,0:T(8,128)(2,1)S(1)}, u32[]{:S(2)}, u32[]{:S(2)}) collective-permute-start(bf16[16,14464]{1,0:T(8,128)(2,1)S(1)} %get-tuple-element.38.refs_1_.bottom_ref), channel_id=1, source_target_pairs={{0,6},{1,7},{2,0},{3,1},{4,2},{5,3},{6,4},{7,5},{8,14},{9,15},{10,... | collective-permute-start | bytes 1388552 | tf_op jit(solution)/shard_map/ppermute | solution.py:36
  33.2 34.5 %all-to-all-start = ((bf16[8,64,896]{2,1,0:T(8,128)(2,1)}), bf16[8,64,896]{2,1,0:T(8,128)(2,1)S(1)}, u32[]{:S(2)}, u32[]{:S(2)}) async-start(bf16[8,64,896]{2,1,0:T(8,128)(2,1)} %bitcast.4), calls=%async_computation | async-start | bytes 1835008 | tf_op jit(solution)/shard_map/all_to_all | solution.py:294
  40.6 78.5 %all-gather.3.cloned.1.call-start = ((), (), s32[]{:S(2)}) async-start(), calls=%async_computation.1 | async-start | bytes 1769472 | tf_op jit(solution)/shard_map/all_gather | solution.py:326
  40.7 11.7 %collective-permute-start.5 = (bf16[16,14464]{1,0:T(8,128)(2,1)S(1)}, bf16[16,14464]{1,0:T(8,128)(2,1)S(1)}, u32[]{:S(2)}, u32[]{:S(2)}) collective-permute-start(bf16[16,14464]{1,0:T(8,128)(2,1)S(1)} %get-tuple-element.38.refs_1_.bottom_ref), channel_id=1, source_target_pairs={{0,2},{1,3},{2,4},{3,5},{4,6},{5,7},{6,0},{7,1},{8,10},{9,11},{10,... | collective-permute-start | bytes 1388552 | tf_op jit(solution)/shard_map/ppermute | solution.py:36
  40.8 11.6 %collective-permute-start.6 = (bf16[16,14464]{1,0:T(8,128)(2,1)S(1)}, bf16[16,14464]{1,0:T(8,128)(2,1)S(1)}, u32[]{:S(2)}, u32[]{:S(2)}) collective-permute-start(bf16[16,14464]{1,0:T(8,128)(2,1)S(1)} %get-tuple-element.37.refs_0_.top_ref), channel_id=1, source_target_pairs={{0,6},{1,7},{2,0},{3,1},{4,2},{5,3},{6,4},{7,5},{8,14},{9,15},{10,... | collective-permute-start | bytes 1388552 | tf_op jit(solution)/shard_map/ppermute | solution.py:36
  43.4 18.9 %collective-permute-start.8 = (bf16[16,14464]{1,0:T(8,128)(2,1)S(1)}, bf16[16,14464]{1,0:T(8,128)(2,1)S(1)}, u32[]{:S(2)}, u32[]{:S(2)}) collective-permute-start(bf16[16,14464]{1,0:T(8,128)(2,1)S(1)} %collective-permute-done.4.refs_2_), channel_id=1, source_target_pairs={{0,2},{1,3},{2,4},{3,5},{4,6},{5,7},{6,0},{7,1},{8,10},{9,11},{10,... | collective-permute-start | bytes 1388552 | tf_op jit(solution)/shard_map/ppermute | solution.py:36
  43.4 18.9 %collective-permute-start.9 = (bf16[16,14464]{1,0:T(8,128)(2,1)S(1)}, bf16[16,14464]{1,0:T(8,128)(2,1)S(1)}, u32[]{:S(2)}, u32[]{:S(2)}) collective-permute-start(bf16[16,14464]{1,0:T(8,128)(2,1)S(1)} %collective-permute-done.7.refs_5_), channel_id=1, source_target_pairs={{0,6},{1,7},{2,0},{3,1},{4,2},{5,3},{6,4},{7,5},{8,14},{9,15},{10,... | collective-permute-start | bytes 1388552 | tf_op jit(solution)/shard_map/ppermute | solution.py:36
  67.8 10.4 %copy-start.9 = (bf16[8,64,896]{2,1,0:T(8,128)(2,1)}, bf16[8,64,896]{2,1,0:T(8,128)(2,1)S(1)}, u32[]{:S(2)}) copy-start(bf16[8,64,896]{2,1,0:T(8,128)(2,1)S(1)} %all-to-all-done) | copy-start | bytes 2752516
  67.8 25.8 %collective-permute-start.12 = (bf16[512,896]{1,0:T(8,128)(2,1)S(1)}, bf16[512,896]{1,0:T(8,128)(2,1)S(1)}, u32[]{:S(2)}, u32[]{:S(2)}) collective-permute-start(bf16[512,896]{1,0:T(8,128)(2,1)S(1)} %bitcast.15), channel_id=1, source_target_pairs={{0,2},{1,3},{2,4},{3,5},{4,6},{5,7},{6,0},{7,1},{8,10},{9,11},{10,... | collective-permute-start | bytes 2752520 | tf_op jit(solution)/shard_map/ppermute | solution.py:36
  67.9 25.8 %collective-permute-start.13 = (bf16[512,896]{1,0:T(8,128)(2,1)S(1)}, bf16[512,896]{1,0:T(8,128)(2,1)S(1)}, u32[]{:S(2)}, u32[]{:S(2)}) collective-permute-start(bf16[512,896]{1,0:T(8,128)(2,1)S(1)} %bitcast.16), channel_id=1, source_target_pairs={{0,6},{1,7},{2,0},{3,1},{4,2},{5,3},{6,4},{7,5},{8,14},{9,15},{10,... | collective-permute-start | bytes 2752520 | tf_op jit(solution)/shard_map/ppermute | solution.py:36
  70.5 2.6 %copy-start = (bf16[7168,3,128]{2,0,1:T(8,128)(2,1)S(1)}, bf16[7168,3,128]{2,0,1:T(8,128)(2,1)}, u32[]{:S(2)}) copy-start(bf16[7168,3,128]{2,0,1:T(8,128)(2,1)} %param.9) | copy-start | bytes 16515076
  78.1 14.2 %collective-permute-start.10 = (bf16[16,7296]{1,0:T(8,128)(2,1)S(1)}, bf16[16,7296]{1,0:T(8,128)(2,1)S(1)}, u32[]{:S(2)}, u32[]{:S(2)}) collective-permute-start(bf16[16,7296]{1,0:T(8,128)(2,1)S(1)} %get-tuple-element.44), channel_id=1, source_target_pairs={{0,6},{1,7},{2,0},{3,1},{4,2},{5,3},{6,4},{7,5},{8,14},{9,15},{10,... | collective-permute-start | bytes 700424 | tf_op jit(solution)/shard_map/ppermute | solution.py:36
  79.4 14.0 %collective-permute-start.11 = (bf16[16,7296]{1,0:T(8,128)(2,1)S(1)}, bf16[16,7296]{1,0:T(8,128)(2,1)S(1)}, u32[]{:S(2)}, u32[]{:S(2)}) collective-permute-start(bf16[16,7296]{1,0:T(8,128)(2,1)S(1)} %get-tuple-element.45), channel_id=1, source_target_pairs={{0,2},{1,3},{2,4},{3,5},{4,6},{5,7},{6,0},{7,1},{8,10},{9,11},{10,... | collective-permute-start | bytes 700424 | tf_op jit(solution)/shard_map/ppermute | solution.py:36
  93.6 25.5 %copy-start.1 = (bf16[512,896]{1,0:T(8,128)(2,1)}, bf16[512,896]{1,0:T(8,128)(2,1)S(1)}, u32[]{:S(2)}) copy-start(bf16[512,896]{1,0:T(8,128)(2,1)S(1)} %collective-permute-done.12.left_ref.refs_1_) | copy-start | bytes 2752516
  93.6 25.5 %copy-start.2 = (bf16[512,896]{1,0:T(8,128)(2,1)}, bf16[512,896]{1,0:T(8,128)(2,1)S(1)}, u32[]{:S(2)}) copy-start(bf16[512,896]{1,0:T(8,128)(2,1)S(1)} %collective-permute-done.13.right_ref.refs_2_) | copy-start | bytes 2752516
  93.6 9.0 %collective-permute-start.14 = (bf16[32,7296]{1,0:T(8,128)(2,1)S(1)}, bf16[32,7296]{1,0:T(8,128)(2,1)S(1)}, u32[]{:S(2)}, u32[]{:S(2)}) collective-permute-start(bf16[32,7296]{1,0:T(8,128)(2,1)S(1)} %get-tuple-element.48), channel_id=1, source_target_pairs={{0,6},{1,7},{2,0},{3,1},{4,2},{5,3},{6,4},{7,5},{8,14},{9,15},{10,... | collective-permute-start | bytes 1400840 | tf_op jit(solution)/shard_map/ppermute | solution.py:36
  96.1 9.5 %collective-permute-start.15 = (bf16[32,7296]{1,0:T(8,128)(2,1)S(1)}, bf16[32,7296]{1,0:T(8,128)(2,1)S(1)}, u32[]{:S(2)}, u32[]{:S(2)}) collective-permute-start(bf16[32,7296]{1,0:T(8,128)(2,1)S(1)} %get-tuple-element.49), channel_id=1, source_target_pairs={{0,2},{1,3},{2,4},{3,5},{4,6},{5,7},{6,0},{7,1},{8,10},{9,11},{10,... | collective-permute-start | bytes 1400840 | tf_op jit(solution)/shard_map/ppermute | solution.py:36
  106.8 12.3 %collective-permute-start.19 = (bf16[256,896]{1,0:T(8,128)(2,1)}, bf16[256,896]{1,0:T(8,128)(2,1)S(1)}, u32[]{:S(2)}, u32[]{:S(2)}) collective-permute-start(bf16[256,896]{1,0:T(8,128)(2,1)} %get-tuple-element.58), channel_id=1, source_target_pairs={{0,2},{1,3},{2,4},{3,5},{4,6},{5,7},{6,0},{7,1},{8,10},{9,11},{10,... | collective-permute-start | bytes 1376264 | tf_op jit(solution)/shard_map/ppermute | solution.py:36
  106.8 12.3 %collective-permute-start.20 = (bf16[256,896]{1,0:T(8,128)(2,1)}, bf16[256,896]{1,0:T(8,128)(2,1)S(1)}, u32[]{:S(2)}, u32[]{:S(2)}) collective-permute-start(bf16[256,896]{1,0:T(8,128)(2,1)} %get-tuple-element.59), channel_id=1, source_target_pairs={{0,6},{1,7},{2,0},{3,1},{4,2},{5,3},{6,4},{7,5},{8,14},{9,15},{10,... | collective-permute-start | bytes 1376264 | tf_op jit(solution)/shard_map/ppermute | solution.py:36
  109.5 6.2 %collective-permute-start.16 = (bf16[8,7296]{1,0:T(8,128)(2,1)S(1)}, bf16[8,7296]{1,0:T(8,128)(2,1)S(1)}, u32[]{:S(2)}, u32[]{:S(2)}) collective-permute-start(bf16[8,7296]{1,0:T(8,128)(2,1)S(1)} %get-tuple-element.51), channel_id=1, source_target_pairs={{0,24},{1,25},{2,26},{3,27},{4,28},{5,29},{6,30},{7,31},{8,0},{9,1... | collective-permute-start | bytes 350216 | tf_op jit(solution)/shard_map/ppermute | solution.py:36
  112.7 5.3 %collective-permute-start.17 = (bf16[8,7296]{1,0:T(8,128)(2,1)S(1)}, bf16[8,7296]{1,0:T(8,128)(2,1)S(1)}, u32[]{:S(2)}, u32[]{:S(2)}) collective-permute-start(bf16[8,7296]{1,0:T(8,128)(2,1)S(1)} %get-tuple-element.52), channel_id=1, source_target_pairs={{0,16},{1,17},{2,18},{3,19},{4,20},{5,21},{6,22},{7,23},{8,24},{9,... | collective-permute-start | bytes 350216 | tf_op jit(solution)/shard_map/ppermute | solution.py:36
  112.7 6.4 %collective-permute-start.18 = (bf16[8,7296]{1,0:T(8,128)(2,1)S(1)}, bf16[8,7296]{1,0:T(8,128)(2,1)S(1)}, u32[]{:S(2)}, u32[]{:S(2)}) collective-permute-start(bf16[8,7296]{1,0:T(8,128)(2,1)S(1)} %get-tuple-element.53), channel_id=1, source_target_pairs={{0,8},{1,9},{2,10},{3,11},{4,12},{5,13},{6,14},{7,15},{8,16},{9,17... | collective-permute-start | bytes 350216 | tf_op jit(solution)/shard_map/ppermute | solution.py:36
  119.1 11.2 %copy-start.7 = (s32[128,8]{0,1:T(8,128)S(1)}, s32[128,8]{0,1:T(8,128)}, u32[]{:S(2)}) copy-start(s32[128,8]{0,1:T(8,128)} %param.7) | copy-start | bytes 12292
  124.1 8.2 %collective-permute-start.21 = (bf16[3,896,128]{2,1,0:T(8,128)(2,1)S(1)}, bf16[3,896,128]{2,1,0:T(8,128)(2,1)S(1)}, u32[]{:S(2)}, u32[]{:S(2)}) collective-permute-start(bf16[3,896,128]{2,1,0:T(8,128)(2,1)S(1)} %get-tuple-element.62), channel_id=1, source_target_pairs={{0,1},{1,0},{2,3},{3,2},{4,5},{5,4},{6,7},{7,6},{8,9},{9,8},{10,11... | collective-permute-start | bytes 2064392 | tf_op jit(solution)/shard_map/ppermute | solution.py:36
  132.3 1.3 copy-start.5
  (2 other events, 1.4 us)
Sparse Core Ops, SparseCore 0:
  67.9 38.6 all-gather.2
